TPU v7x, 32 devices: a whole 2x2x4 slice. The times are simulated.
32 devices in a mesh: batch: 8 (over z, x), height: 4 (over y, core).
Axes of the slice: x: 2, y: 2, z: 4, core: 2. Of those that a mesh axis runs over, the one named last changes fastest.
Arguments:
- image_small: bfloat16 [96, 16, 10, 1024], P('batch', 'height'), may hold values from -6 to 6
- image_medium: bfloat16 [96, 24, 14, 1024], P('batch', 'height'), may hold values from -6 to 6
- image_large: bfloat16 [96, 32, 18, 1024], P('batch', 'height'), may hold values from -6 to 6
- row_counts: int32 [3, 4], replicated, may hold values from 1 to 4, as said below
- reduce_a: bfloat16 [1024, 512], replicated, may hold values from -0.1875 to 0.1875
- first_spatial_weight: bfloat16 [3, 3, 512, 512], replicated, may hold values from -0.09375 to 0.09375
- expand_a: bfloat16 [512, 2048], replicated, may hold values from -0.25 to 0.25
- shortcut_a: bfloat16 [1024, 2048], replicated, may hold values from -0.1875 to 0.1875
- reduce_b: bfloat16 [2048, 512], replicated, may hold values from -0.125 to 0.125
- second_spatial_weight: bfloat16 [3, 3, 512, 512], replicated, may hold values from -0.09375 to 0.09375
- expand_b: bfloat16 [512, 2048], replicated, may hold values from -0.25 to 0.25
- gain_mid: float32 [4, 512], replicated, may hold values from 0.25 to 1.75
- shift_mid: float32 [4, 512], replicated, may hold values from -3 to 3
- gain_out: float32 [3, 2048], replicated, may hold values from 0.25 to 1.75
- shift_out: float32 [3, 2048], replicated, may hold values from -3 to 3
- upstream_small: bfloat16 [96, 2048], P('batch'), may hold values from -6 to 6
- upstream_medium: bfloat16 [96, 2048], P('batch'), may hold values from -6 to 6
- upstream_large: bfloat16 [96, 2048], P('batch'), may hold values from -6 to 6
Outputs:
- pooled_small: float32 [96, 2048], P('batch')
- pooled_medium: float32 [96, 2048], P('batch')
- pooled_large: float32 [96, 2048], P('batch')
- back_small: bfloat16 [96, 16, 10, 1024], P('batch', 'height')
- back_medium: bfloat16 [96, 24, 14, 1024], P('batch', 'height')
- back_large: bfloat16 [96, 32, 18, 1024], P('batch', 'height')
- reduce_a_grad: float32 [1024, 512], P('batch')
- spatial_a_grad: float32 [3, 3, 512, 512], P(None, None, 'batch')
- expand_a_grad: float32 [512, 2048], P('batch')
- shortcut_a_grad: float32 [1024, 2048], P('batch')
- reduce_b_grad: float32 [2048, 512], P('batch')
- spatial_b_grad: float32 [3, 3, 512, 512], P(None, None, 'batch')
- expand_b_grad: float32 [512, 2048], P('batch')
- gain_mid_grad: float32 [4, 512], replicated
- shift_mid_grad: float32 [4, 512], replicated
- gain_out_grad: float32 [3, 2048], replicated
- shift_out_grad: float32 [3, 2048], replicated
Inputs may be any that keep to these rules, and one draw needn't show every extreme that they name: Row g of row_counts gives the output rows of each band of height for group g (small, medium, large); row sums are 5, 7, 9; the largest entry of row g is exactly 2, 3, 4.
All inputs are finite; a program needn't handle non-finite values.
Results may differ from a plain program's by a relative error of at most 0.019.
Values may be sent and summed in bfloat16 or wider, within the bound.
A program may use at most 320 MiB of HBM per device.

v0:
```python
import jax
import jax.numpy as jnp
from jax import lax
from jax.sharding import PartitionSpec as P

epsilon = 1e-05


def passed_along(value, axis, steps):
    count = lax.axis_size(axis)
    first, last = (max(0, -steps), min(count, count - steps))
    return lax.ppermute(value, axis, [(source, source + steps) for source in range(first, last)])


def extended(value, sides, width):
    for axis, dim in sides:
        peers, length = (lax.axis_size(axis), value.shape[dim])
        up = [(i, (i + 1) % peers) for i in range(peers - 1)]
        down = [(j, i) for i, j in up]
        last = lax.slice_in_dim(value, length - width, length, axis=dim)
        first = lax.slice_in_dim(value, 0, width, axis=dim)
        before = lax.ppermute(last, axis, up)
        after = lax.ppermute(first, axis, down)
        value = jnp.concatenate([before, value, after], axis=dim)
    return value


def sigmoid_slope(values):
    logistic = jax.nn.sigmoid(values)
    return logistic * (1.0 + values * (1.0 - logistic))


def project(values, weight):
    return jnp.einsum("ihwc,cd->ihwd", values, weight, preferred_element_type=jnp.float32)


def project_back(grad_in, weight):
    return jnp.einsum("ihwd,cd->ihwc", grad_in, weight, preferred_element_type=jnp.float32)


def weight_term(values, grad_in):
    return jnp.einsum("ihwc,ihwd->cd", values, grad_in, preferred_element_type=jnp.float32)


def tap_window(padded, stride, out_rows, out_cols, row_tap, col_tap):
    return padded[
        :,
        row_tap : row_tap + stride * (out_rows - 1) + 1 : stride,
        col_tap : col_tap + stride * (out_cols - 1) + 1 : stride,
    ]


def spatial_kernel(padded, weight, stride, out_rows, out_cols):
    summed = None
    for row_tap in range(3):
        for col_tap in range(3):
            product = project(
                tap_window(padded, stride, out_rows, out_cols, row_tap, col_tap),
                weight[row_tap, col_tap],
            )
            summed = product if summed is None else summed + product
    return summed


def spatial_back(padded, weight, grad_in, stride, out_rows, out_cols):
    padded_grad = jnp.zeros(padded.shape, jnp.float32)
    tap_grads = []
    for row_tap in range(3):
        row_list = []
        for col_tap in range(3):
            window = tap_window(padded, stride, out_rows, out_cols, row_tap, col_tap)
            row_list.append(weight_term(window, grad_in))
            padded_grad = padded_grad.at[
                :,
                row_tap : row_tap + stride * (out_rows - 1) + 1 : stride,
                col_tap : col_tap + stride * (out_cols - 1) + 1 : stride,
            ].add(project_back(grad_in, weight[row_tap, col_tap]))
        tap_grads.append(jnp.stack(row_list))
    return (jnp.stack(tap_grads), padded_grad)


def gather_stats(levels, numbers):
    local_sums = []
    for tensors in levels:
        local_sums.append(sum((jnp.sum(member, axis=(0, 1, 2)) for member in tensors)))
        local_sums.append(sum((jnp.sum(member * member, axis=(0, 1, 2)) for member in tensors)))
    summed = lax.psum(jnp.stack(local_sums), ("batch", "height"))
    result = []
    for position in range(len(levels)):
        centre = summed[2 * position] / numbers[position]
        square = summed[2 * position + 1] / numbers[position]
        result.append((centre, lax.rsqrt(square - centre * centre + epsilon)))
    return result


def grad_stats(triples):
    local_sums = []
    for grad_list, value_list, stat in triples:
        centre, inv_root = stat
        local_sums.append(
            sum(
                (
                    jnp.sum(grad_list[picture_batches], axis=(0, 1, 2))
                    for picture_batches in range(3)
                )
            )
        )
        local_sums.append(
            sum(
                (
                    jnp.sum(
                        grad_list[picture_batches]
                        * (value_list[picture_batches] - centre)
                        * inv_root,
                        axis=(0, 1, 2),
                    )
                    for picture_batches in range(3)
                )
            )
        )
    summed = lax.psum(jnp.stack(local_sums), ("batch", "height"))
    return [(summed[2 * position], summed[2 * position + 1]) for position in range(len(triples))]


def apply_norm(values, stat, gain, shift):
    centre, inv_root = stat
    return (values - centre) * (inv_root * gain) + shift


def norm_back(grad_in, values, stat, gain, grad_sums, number):
    centre, inv_root = stat
    normed = (values - centre) * inv_root
    return gain * inv_root * (grad_in - grad_sums[0] / number - normed * (grad_sums[1] / number))


def per_device(
    image_small,
    image_medium,
    image_large,
    row_counts,
    reduce_a,
    first_spatial_weight,
    expand_a,
    shortcut_a,
    reduce_b,
    second_spatial_weight,
    expand_b,
    gain_mid,
    shift_mid,
    gain_out,
    shift_out,
    upstream_small,
    upstream_medium,
    upstream_large,
):
    raw_images = (image_small, image_medium, image_large)
    upstreams = (upstream_small, upstream_medium, upstream_large)
    band_index = lax.axis_index("height")
    batch_devices = lax.axis_size("batch")
    entering_photos, entering_filters, line_filters, genuine_lines, edge_extents, bucket_limits = (
        [],
        [],
        [],
        [],
        [],
        [],
    )
    total_in = 0
    total_out = 0
    for picture_batches in range(3):
        slab_rows = raw_images[picture_batches].shape[1]
        bucket_limit = slab_rows // 2
        out_side = raw_images[picture_batches].shape[2] // 2
        live = row_counts[picture_batches, band_index]
        mask_low = (jnp.arange(slab_rows, dtype=jnp.int32) < 2 * live).astype(jnp.bfloat16)[
            None, :, None, None
        ]
        entering_photos.append(raw_images[picture_batches] * mask_low)
        entering_filters.append(mask_low.astype(jnp.float32))
        line_filters.append(
            (jnp.arange(bucket_limit, dtype=jnp.int32) < live).astype(jnp.float32)[
                None, :, None, None
            ]
        )
        genuine_lines.append(live)
        edge_extents.append(out_side)
        bucket_limits.append(bucket_limit)
        total_in += batch_devices * raw_images[picture_batches].shape[0] * 4 * out_side * out_side
        total_out += batch_devices * raw_images[picture_batches].shape[0] * out_side * out_side
    width_cuts = [edge_extents[0], edge_extents[0] + edge_extents[1]]
    input_cuts = [2 * edge_extents[0], 2 * edge_extents[0] + 2 * edge_extents[1]]
    first_out = [
        project(entering_photos[picture_batches], reduce_a) for picture_batches in range(3)
    ]
    (stat_one,) = gather_stats([first_out], [total_in])
    pre_one = [
        apply_norm(first_out[picture_batches], stat_one, gain_mid[0], shift_mid[0])
        for picture_batches in range(3)
    ]
    act_one = [
        (jax.nn.silu(pre_one[picture_batches]) * entering_filters[picture_batches]).astype(
            jnp.bfloat16
        )
        for picture_batches in range(3)
    ]
    tail_rows = [
        lax.dynamic_index_in_dim(
            act_one[picture_batches], 2 * genuine_lines[picture_batches] - 1, 1, keepdims=False
        )
        for picture_batches in range(3)
    ]
    rim_rows = passed_along(jnp.concatenate(tail_rows, axis=1), "height", 1)
    rim_parts = jnp.split(rim_rows, input_cuts, axis=1)
    first_padded = []
    for picture_batches in range(3):
        joined = jnp.concatenate(
            [rim_parts[picture_batches][:, None], act_one[picture_batches]], axis=1
        )
        first_padded.append(jnp.pad(joined, ((0, 0), (0, 0), (1, 0), (0, 0))))
    second_out = [
        spatial_kernel(
            first_padded[picture_batches],
            first_spatial_weight,
            2,
            bucket_limits[picture_batches],
            edge_extents[picture_batches],
        )
        * line_filters[picture_batches]
        for picture_batches in range(3)
    ]
    (stat_two,) = gather_stats([second_out], [total_out])
    pre_two = [
        apply_norm(second_out[picture_batches], stat_two, gain_mid[1], shift_mid[1])
        for picture_batches in range(3)
    ]
    act_two = [
        (jax.nn.silu(pre_two[picture_batches]) * line_filters[picture_batches]).astype(jnp.bfloat16)
        for picture_batches in range(3)
    ]
    third_out = [project(act_two[picture_batches], expand_a) for picture_batches in range(3)]
    side_inputs = [entering_photos[picture_batches][:, ::2, ::2] for picture_batches in range(3)]
    side_out = [project(side_inputs[picture_batches], shortcut_a) for picture_batches in range(3)]
    stat_three, stat_side = gather_stats([third_out, side_out], [total_out, total_out])
    joint_one = [
        apply_norm(third_out[picture_batches], stat_three, gain_out[0], shift_out[0])
        + apply_norm(side_out[picture_batches], stat_side, gain_out[1], shift_out[1])
        for picture_batches in range(3)
    ]
    middle = [
        jax.nn.silu(joint_one[picture_batches]) * line_filters[picture_batches]
        for picture_batches in range(3)
    ]
    middle_low = [middle[picture_batches].astype(jnp.bfloat16) for picture_batches in range(3)]
    fourth_out = [project(middle_low[picture_batches], reduce_b) for picture_batches in range(3)]
    (stat_four,) = gather_stats([fourth_out], [total_out])
    pre_four = [
        apply_norm(fourth_out[picture_batches], stat_four, gain_mid[2], shift_mid[2])
        for picture_batches in range(3)
    ]
    act_four = [
        (jax.nn.silu(pre_four[picture_batches]) * line_filters[picture_batches]).astype(
            jnp.bfloat16
        )
        for picture_batches in range(3)
    ]
    edge_pairs = [
        jnp.stack(
            [
                act_four[picture_batches][:, 0],
                lax.dynamic_index_in_dim(
                    act_four[picture_batches], genuine_lines[picture_batches] - 1, 1, keepdims=False
                ),
            ],
            axis=1,
        )
        for picture_batches in range(3)
    ]
    rim_pairs = extended(jnp.concatenate(edge_pairs, axis=2), (("height", 1),), 1)
    pair_parts = jnp.split(rim_pairs, width_cuts, axis=2)
    fourth_padded = []
    for picture_batches in range(3):
        rim_pair = pair_parts[picture_batches]
        joined = jnp.concatenate(
            [rim_pair[:, 0:1], act_four[picture_batches], jnp.zeros_like(rim_pair[:, 0:1])], axis=1
        )
        joined = lax.dynamic_update_slice_in_dim(
            joined, rim_pair[:, 3:4], genuine_lines[picture_batches] + 1, 1
        )
        fourth_padded.append(jnp.pad(joined, ((0, 0), (0, 0), (1, 1), (0, 0))))
    fifth_out = [
        spatial_kernel(
            fourth_padded[picture_batches],
            second_spatial_weight,
            1,
            bucket_limits[picture_batches],
            edge_extents[picture_batches],
        )
        * line_filters[picture_batches]
        for picture_batches in range(3)
    ]
    (stat_five,) = gather_stats([fifth_out], [total_out])
    pre_five = [
        apply_norm(fifth_out[picture_batches], stat_five, gain_mid[3], shift_mid[3])
        for picture_batches in range(3)
    ]
    act_five = [
        (jax.nn.silu(pre_five[picture_batches]) * line_filters[picture_batches]).astype(
            jnp.bfloat16
        )
        for picture_batches in range(3)
    ]
    sixth_out = [project(act_five[picture_batches], expand_b) for picture_batches in range(3)]
    (stat_six,) = gather_stats([sixth_out], [total_out])
    joint_two = [
        apply_norm(sixth_out[picture_batches], stat_six, gain_out[2], shift_out[2])
        + middle[picture_batches]
        for picture_batches in range(3)
    ]
    final = [
        jax.nn.silu(joint_two[picture_batches]) * line_filters[picture_batches]
        for picture_batches in range(3)
    ]
    pooled_sums = lax.psum(
        jnp.stack(
            [jnp.sum(final[picture_batches], axis=(1, 2)) for picture_batches in range(3)]
        ).astype(jnp.bfloat16),
        "height",
    ).astype(jnp.float32)
    pooled = [
        pooled_sums[picture_batches]
        / (edge_extents[picture_batches] * edge_extents[picture_batches])
        for picture_batches in range(3)
    ]
    d_joint_two = [
        upstreams[picture_batches].astype(jnp.float32)[:, None, None, :]
        / (edge_extents[picture_batches] * edge_extents[picture_batches])
        * line_filters[picture_batches]
        * sigmoid_slope(joint_two[picture_batches])
        for picture_batches in range(3)
    ]
    (sums_six,) = grad_stats([(d_joint_two, sixth_out, stat_six)])
    grad_six = [
        (
            norm_back(
                d_joint_two[picture_batches],
                sixth_out[picture_batches],
                stat_six,
                gain_out[2],
                sums_six,
                total_out,
            )
            * line_filters[picture_batches]
        ).astype(jnp.bfloat16)
        for picture_batches in range(3)
    ]
    expand_b_local = sum(
        (
            weight_term(act_five[picture_batches], grad_six[picture_batches])
            for picture_batches in range(3)
        )
    )
    d_five = [
        project_back(grad_six[picture_batches], expand_b)
        * sigmoid_slope(pre_five[picture_batches])
        * line_filters[picture_batches]
        for picture_batches in range(3)
    ]
    (sums_five,) = grad_stats([(d_five, fifth_out, stat_five)])
    fifth_gradient = [
        (
            norm_back(
                d_five[picture_batches],
                fifth_out[picture_batches],
                stat_five,
                gain_mid[3],
                sums_five,
                total_out,
            )
            * line_filters[picture_batches]
        ).astype(jnp.bfloat16)
        for picture_batches in range(3)
    ]
    spatial_b_local = None
    d_swish_four = []
    edge_grads = []
    for picture_batches in range(3):
        tap_grad, padded_grad = spatial_back(
            fourth_padded[picture_batches],
            second_spatial_weight,
            fifth_gradient[picture_batches],
            1,
            bucket_limits[picture_batches],
            edge_extents[picture_batches],
        )
        spatial_b_local = tap_grad if spatial_b_local is None else spatial_b_local + tap_grad
        central_block = padded_grad[:, :, 1:-1]
        top_grad = central_block[:, 0]
        below_grad = lax.dynamic_index_in_dim(
            central_block, genuine_lines[picture_batches] + 1, 1, keepdims=False
        )
        d_swish_four.append(central_block[:, 1 : bucket_limits[picture_batches] + 1])
        edge_grads.append(jnp.stack([top_grad, below_grad], axis=1))
    returned = extended(
        jnp.concatenate(edge_grads, axis=2).astype(jnp.bfloat16), (("height", 1),), 1
    ).astype(jnp.float32)
    returned_parts = jnp.split(returned, width_cuts, axis=2)
    d_four = []
    for picture_batches in range(3):
        grad_rows = (
            d_swish_four[picture_batches].at[:, 0].add(returned_parts[picture_batches][:, 0])
        )
        last_row = (
            lax.dynamic_index_in_dim(
                grad_rows, genuine_lines[picture_batches] - 1, 1, keepdims=False
            )
            + returned_parts[picture_batches][:, 3]
        )
        grad_rows = lax.dynamic_update_index_in_dim(
            grad_rows, last_row, genuine_lines[picture_batches] - 1, 1
        )
        d_four.append(
            grad_rows * sigmoid_slope(pre_four[picture_batches]) * line_filters[picture_batches]
        )
    (sums_four,) = grad_stats([(d_four, fourth_out, stat_four)])
    grad_four = [
        (
            norm_back(
                d_four[picture_batches],
                fourth_out[picture_batches],
                stat_four,
                gain_mid[2],
                sums_four,
                total_out,
            )
            * line_filters[picture_batches]
        ).astype(jnp.bfloat16)
        for picture_batches in range(3)
    ]
    reduce_b_local = sum(
        (
            weight_term(middle_low[picture_batches], grad_four[picture_batches])
            for picture_batches in range(3)
        )
    )
    d_joint_one = [
        (project_back(grad_four[picture_batches], reduce_b) + d_joint_two[picture_batches])
        * sigmoid_slope(joint_one[picture_batches])
        * line_filters[picture_batches]
        for picture_batches in range(3)
    ]
    sums_three, sums_side = grad_stats(
        [(d_joint_one, third_out, stat_three), (d_joint_one, side_out, stat_side)]
    )
    grad_three = [
        (
            norm_back(
                d_joint_one[picture_batches],
                third_out[picture_batches],
                stat_three,
                gain_out[0],
                sums_three,
                total_out,
            )
            * line_filters[picture_batches]
        ).astype(jnp.bfloat16)
        for picture_batches in range(3)
    ]
    grad_side = [
        (
            norm_back(
                d_joint_one[picture_batches],
                side_out[picture_batches],
                stat_side,
                gain_out[1],
                sums_side,
                total_out,
            )
            * line_filters[picture_batches]
        ).astype(jnp.bfloat16)
        for picture_batches in range(3)
    ]
    expand_a_local = sum(
        (
            weight_term(act_two[picture_batches], grad_three[picture_batches])
            for picture_batches in range(3)
        )
    )
    shortcut_a_local = sum(
        (
            weight_term(side_inputs[picture_batches], grad_side[picture_batches])
            for picture_batches in range(3)
        )
    )
    d_two = [
        project_back(grad_three[picture_batches], expand_a)
        * sigmoid_slope(pre_two[picture_batches])
        * line_filters[picture_batches]
        for picture_batches in range(3)
    ]
    (sums_two,) = grad_stats([(d_two, second_out, stat_two)])
    second_gradient = [
        (
            norm_back(
                d_two[picture_batches],
                second_out[picture_batches],
                stat_two,
                gain_mid[1],
                sums_two,
                total_out,
            )
            * line_filters[picture_batches]
        ).astype(jnp.bfloat16)
        for picture_batches in range(3)
    ]
    spatial_a_local = None
    d_act_one = []
    rim_grads = []
    for picture_batches in range(3):
        tap_grad, padded_grad = spatial_back(
            first_padded[picture_batches],
            first_spatial_weight,
            second_gradient[picture_batches],
            2,
            bucket_limits[picture_batches],
            edge_extents[picture_batches],
        )
        spatial_a_local = tap_grad if spatial_a_local is None else spatial_a_local + tap_grad
        rim_grads.append(padded_grad[:, 0, 1:])
        d_act_one.append(padded_grad[:, 1:, 1:])
    rim_back = passed_along(
        jnp.concatenate(rim_grads, axis=1).astype(jnp.bfloat16), "height", -1
    ).astype(jnp.float32)
    rim_back_parts = jnp.split(rim_back, input_cuts, axis=1)
    d_one = []
    for picture_batches in range(3):
        row_place = 2 * genuine_lines[picture_batches] - 1
        last_row = (
            lax.dynamic_index_in_dim(d_act_one[picture_batches], row_place, 1, keepdims=False)
            + rim_back_parts[picture_batches]
        )
        grad_rows = lax.dynamic_update_index_in_dim(
            d_act_one[picture_batches], last_row, row_place, 1
        )
        d_one.append(
            grad_rows * sigmoid_slope(pre_one[picture_batches]) * entering_filters[picture_batches]
        )
    (sums_one,) = grad_stats([(d_one, first_out, stat_one)])
    grad_one = [
        (
            norm_back(
                d_one[picture_batches],
                first_out[picture_batches],
                stat_one,
                gain_mid[0],
                sums_one,
                total_in,
            )
            * entering_filters[picture_batches]
        ).astype(jnp.bfloat16)
        for picture_batches in range(3)
    ]
    reduce_a_local = sum(
        (
            weight_term(entering_photos[picture_batches], grad_one[picture_batches])
            for picture_batches in range(3)
        )
    )
    backs = []
    for picture_batches in range(3):
        image_grad = project_back(grad_one[picture_batches], reduce_a)
        image_grad = image_grad.at[:, ::2, ::2].add(
            project_back(grad_side[picture_batches], shortcut_a)
        )
        backs.append(image_grad.astype(jnp.bfloat16))
    shards = (
        lax.psum_scatter(reduce_a_local, "batch", scatter_dimension=0, tiled=True),
        lax.psum_scatter(spatial_a_local, "batch", scatter_dimension=2, tiled=True),
        lax.psum_scatter(expand_a_local, "batch", scatter_dimension=0, tiled=True),
        lax.psum_scatter(shortcut_a_local, "batch", scatter_dimension=0, tiled=True),
        lax.psum_scatter(reduce_b_local, "batch", scatter_dimension=0, tiled=True),
        lax.psum_scatter(spatial_b_local, "batch", scatter_dimension=2, tiled=True),
        lax.psum_scatter(expand_b_local, "batch", scatter_dimension=0, tiled=True),
    )
    shards = (
        lax.psum(shards[0].astype(jnp.bfloat16), "height").astype(jnp.float32),
        lax.psum(shards[1].astype(jnp.bfloat16), "height").astype(jnp.float32),
        lax.psum(shards[2].astype(jnp.bfloat16), "height").astype(jnp.float32),
        lax.psum(shards[3].astype(jnp.bfloat16), "height").astype(jnp.float32),
        lax.psum(shards[4].astype(jnp.bfloat16), "height").astype(jnp.float32),
        lax.psum(shards[5].astype(jnp.bfloat16), "height").astype(jnp.float32),
        lax.psum(shards[6].astype(jnp.bfloat16), "height").astype(jnp.float32),
    )
    gain_mid_grad = jnp.stack([sums_one[1], sums_two[1], sums_four[1], sums_five[1]])
    shift_mid_grad = jnp.stack([sums_one[0], sums_two[0], sums_four[0], sums_five[0]])
    gain_out_grad = jnp.stack([sums_three[1], sums_side[1], sums_six[1]])
    shift_out_grad = jnp.stack([sums_three[0], sums_side[0], sums_six[0]])
    return (
        pooled[0],
        pooled[1],
        pooled[2],
        backs[0],
        backs[1],
        backs[2],
        shards[0],
        shards[1],
        shards[2],
        shards[3],
        shards[4],
        shards[5],
        shards[6],
        gain_mid_grad,
        shift_mid_grad,
        gain_out_grad,
        shift_out_grad,
    )


def solution(mesh):
    placed = (
        P("batch", "height", None, None),
        P("batch", "height", None, None),
        P("batch", "height", None, None),
        P(),
        P(),
        P(),
        P(),
        P(),
        P(),
        P(),
        P(),
        P(),
        P(),
        P(),
        P(),
        P("batch", None),
        P("batch", None),
        P("batch", None),
    )
    return jax.shard_map(
        per_device,
        mesh=mesh,
        in_specs=placed,
        out_specs=(
            P("batch", None),
            P("batch", None),
            P("batch", None),
            P("batch", "height", None, None),
            P("batch", "height", None, None),
            P("batch", "height", None, None),
            P("batch", None),
            P(None, None, "batch", None),
            P("batch", None),
            P("batch", None),
            P("batch", None),
            P(None, None, "batch", None),
            P("batch", None),
            P(),
            P(),
            P(),
            P(),
        ),
        check_vma=False,
    )
```

profile of v0, /device:TPU:0, one launch (start us, length us, event | category | flops | bytes accessed | tf_op | source)
XLA Modules:
  0.0 2539.6 jit_solution(662237160074046232)
XLA Ops:
  29.7 52.7 %psum.140 = f32[2,512]{1,0:T(2,128)S(1)} all-reduce(f32[2,512]{1,0:T(2,128)S(1)} %pad_maximum_fusion.16), channel_id=1, replica_groups=mesh['batch'=8,'height'=4] {'batch','height'}, use_global_device_ids=true, to_apply=%region_6.0 | all-reduce | flops 1024 | bytes 8192 | tf_op jit(solution)/shard_map/psum | solution.py:87
  326.9 23.7 slice.1699
  350.5 23.5 slice.1698
  397.6 23.6 slice.1696
  421.2 23.5 slice.1695
  444.7 23.5 slice.1694
  468.2 23.9 slice.1702
  512.5 40.2 %psum.141 = f32[2,512]{1,0:T(2,128)S(1)} all-reduce(f32[2,512]{1,0:T(2,128)S(1)} %pad_maximum_fusion.17), channel_id=1, replica_groups=mesh['batch'=8,'height'=4] {'batch','height'}, use_global_device_ids=true, to_apply=%region_13.14 | all-reduce | flops 1024 | bytes 8192 | tf_op jit(solution)/shard_map/psum | solution.py:87
  565.2 40.3 %psum.142 = f32[4,2048]{1,0:T(4,128)S(1)} all-reduce(f32[4,2048]{1,0:T(4,128)S(1)} %pad_maximum_fusion.8), channel_id=1, replica_groups=mesh['batch'=8,'height'=4] {'batch','height'}, use_global_device_ids=true, to_apply=%region_26.27 | all-reduce | flops 8192 | bytes 65536 | tf_op jit(solution)/shard_map/psum | solution.py:87
  621.5 40.0 %psum.143 = f32[2,512]{1,0:T(2,128)S(1)} all-reduce(f32[2,512]{1,0:T(2,128)S(1)} %pad_maximum_fusion.18), channel_id=1, replica_groups=mesh['batch'=8,'height'=4] {'batch','height'}, use_global_device_ids=true, to_apply=%region_33.34 | all-reduce | flops 1024 | bytes 8192 | tf_op jit(solution)/shard_map/psum | solution.py:87
  702.2 43.5 %psum.144 = f32[2,512]{1,0:T(2,128)S(1)} all-reduce(f32[2,512]{1,0:T(2,128)S(1)} %pad_maximum_fusion.19), channel_id=1, replica_groups=mesh['batch'=8,'height'=4] {'batch','height'}, use_global_device_ids=true, to_apply=%region_40.41 | all-reduce | flops 1024 | bytes 8192 | tf_op jit(solution)/shard_map/psum | solution.py:87
  757.5 40.1 %psum.145 = f32[2,2048]{1,0:T(2,128)S(1)} all-reduce(f32[2,2048]{1,0:T(2,128)S(1)} %pad_maximum_fusion.12), channel_id=1, replica_groups=mesh['batch'=8,'height'=4] {'batch','height'}, use_global_device_ids=true, to_apply=%region_47.48 | all-reduce | flops 4096 | bytes 32768 | tf_op jit(solution)/shard_map/psum | solution.py:87
  813.7 40.4 %psum.147 = f32[2,2048]{1,0:T(2,128)S(1)} all-reduce(f32[2,2048]{1,0:T(2,128)S(1)} %pad_maximum_fusion.13), channel_id=1, replica_groups=mesh['batch'=8,'height'=4] {'batch','height'}, use_global_device_ids=true, to_apply=%region_58.59 | all-reduce | flops 4096 | bytes 32768 | tf_op jit(solution)/shard_map/psum | solution.py:121
  872.1 40.3 %psum.148 = f32[2,512]{1,0:T(2,128)S(1)} all-reduce(f32[2,512]{1,0:T(2,128)S(1)} %pad_maximum_fusion.20), channel_id=1, replica_groups=mesh['batch'=8,'height'=4] {'batch','height'}, use_global_device_ids=true, to_apply=%region_65.66 | all-reduce | flops 1024 | bytes 8192 | tf_op jit(solution)/shard_map/psum | solution.py:121
  1160.6 42.8 %psum.149 = f32[2,512]{1,0:T(2,128)} all-reduce(f32[2,512]{1,0:T(2,128)} %pad_maximum_fusion.21), channel_id=1, replica_groups=mesh['batch'=8,'height'=4] {'batch','height'}, use_global_device_ids=true, to_apply=%region_73.74 | all-reduce | flops 1024 | bytes 8192 | tf_op jit(solution)/shard_map/psum | solution.py:121
  1228.1 40.6 %psum.150 = f32[4,2048]{1,0:T(4,128)S(1)} all-reduce(f32[4,2048]{1,0:T(4,128)S(1)} %pad_maximum_fusion.9), channel_id=1, replica_groups=mesh['batch'=8,'height'=4] {'batch','height'}, use_global_device_ids=true, to_apply=%region_83.84 | all-reduce | flops 8192 | bytes 65536 | tf_op jit(solution)/shard_map/psum | solution.py:121
  1292.7 40.5 %psum.151 = f32[2,512]{1,0:T(2,128)S(1)} all-reduce(f32[2,512]{1,0:T(2,128)S(1)} %pad_maximum_fusion.22), channel_id=1, replica_groups=mesh['batch'=8,'height'=4] {'batch','height'}, use_global_device_ids=true, to_apply=%region_90.91 | all-reduce | flops 1024 | bytes 8192 | tf_op jit(solution)/shard_map/psum | solution.py:121
  1566.2 41.0 %psum.152 = f32[2,512]{1,0:T(2,128)S(1)} all-reduce(f32[2,512]{1,0:T(2,128)S(1)} %pad_maximum_fusion.23), channel_id=1, replica_groups=mesh['batch'=8,'height'=4] {'batch','height'}, use_global_device_ids=true, to_apply=%region_124.125 | all-reduce | flops 1024 | bytes 8192 | tf_op jit(solution)/shard_map/psum | solution.py:121
  1751.0 35.3 %reduce-scatter.20.cloned.1.call-done = f32[64,2048]{1,0:T(8,128)} async-done(((f32[512,2048]{1,0:T(8,128)}), f32[64,2048]{1,0:T(8,128)}) %reduce-scatter.20.cloned.1.call-update) | async-done | bytes 524304 | tf_op jit(solution)/shard_map/reduce_scatter | solution.py:582
  1788.1 90.2 %reduce-scatter.16.cloned.1.call-done = f32[256,512]{1,0:T(8,128)} async-done(((f32[2048,512]{1,0:T(8,128)}), f32[256,512]{1,0:T(8,128)}) %reduce-scatter.16.cloned.1.call-update) | async-done | bytes 524304 | tf_op jit(solution)/shard_map/reduce_scatter | solution.py:580
  1880.1 89.5 %reduce-scatter.12.cloned.1.call-done = f32[64,2048]{1,0:T(8,128)} async-done(((f32[512,2048]{1,0:T(8,128)}), f32[64,2048]{1,0:T(8,128)}) %reduce-scatter.12.cloned.1.call-update) | async-done | bytes 524304 | tf_op jit(solution)/shard_map/reduce_scatter | solution.py:578
  1971.4 150.9 %reduce-scatter.14.cloned.1.call-done = f32[128,2048]{1,0:T(8,128)} async-done(((f32[1024,2048]{1,0:T(8,128)}), f32[128,2048]{1,0:T(8,128)}) %reduce-scatter.14.cloned.1.call-update) | async-done | bytes 1048592 | tf_op jit(solution)/shard_map/reduce_scatter | solution.py:579
  2124.4 164.3 %reduce-scatter.18.cloned.1.call-done = f32[3,3,64,512]{3,2,1,0:T(8,128)} async-done(((f32[3,3,512,512]{3,2,1,0:T(8,128)}), f32[3,3,64,512]{3,2,1,0:T(8,128)}) %reduce-scatter.18.cloned.1.call-update) | async-done | bytes 1179664 | tf_op jit(solution)/shard_map/reduce_scatter | solution.py:581
  2290.8 164.4 %reduce-scatter.10.cloned.1.call-done = f32[3,3,64,512]{3,2,1,0:T(8,128)} async-done(((f32[3,3,512,512]{3,2,1,0:T(8,128)}), f32[3,3,64,512]{3,2,1,0:T(8,128)}) %reduce-scatter.10.cloned.1.call-update) | async-done | bytes 1179664 | tf_op jit(solution)/shard_map/reduce_scatter | solution.py:577
  (1415 shorter events, 1172.5 us)
Async XLA Ops:
  7.2 604.6 %copy-start = (bf16[2048,512]{1,0:T(8,128)(2,1)S(1)}, bf16[2048,512]{1,0:T(8,128)(2,1)}, u32[]{:S(2)}) copy-start(bf16[2048,512]{1,0:T(8,128)(2,1)} %param.86) | copy-start | bytes 6291460
  7.2 1742.2 %reduce-scatter.8.cloned.1.call-start = ((), (), s32[]{:S(2)}) async-start(), calls=%async_computation.7 | async-start | bytes 2359296 | tf_op jit(solution)/shard_map/reduce_scatter | solution.py:576
  83.6 476.0 %copy-start.291 = (f32[1,512]{1,0:T(1,128)}, f32[1,512]{1,0:T(1,128)S(1)}, u32[]{:S(2)}) copy-start(f32[1,512]{1,0:T(1,128)S(1)} %get-tuple-element.650) | copy-start | bytes 6148
  97.8 58.7 %collective-permute-start = (bf16[12,42,512]{2,1,0:T(8,128)(2,1)}, bf16[12,42,512]{2,1,0:T(8,128)(2,1)}, u32[]{:S(2)}, u32[]{:S(2)}) collective-permute-start(bf16[12,42,512]{2,1,0:T(8,128)(2,1)} %pad_maximum_fusion.1), channel_id=1, source_target_pairs={{0,1},{1,2},{2,3},{4,5},{5,6},{6,7},{8,9},{9,10},{10,11},{12,13},{... | collective-permute-start | bytes 1548296 | tf_op jit(solution)/shard_map/ppermute | solution.py:12
  143.8 472.7 %copy-start.254 = (f32[1,2048]{1,0:T(1,128)}, f32[1,2048]{1,0:T(1,128)S(1)}, u32[]{:S(2)}) copy-start(f32[1,2048]{1,0:T(1,128)S(1)} %get-tuple-element.627) | copy-start | bytes 24580
  143.8 472.7 %copy-start.256 = (f32[1,2048]{1,0:T(1,128)}, f32[1,2048]{1,0:T(1,128)S(1)}, u32[]{:S(2)}) copy-start(f32[1,2048]{1,0:T(1,128)S(1)} %get-tuple-element.628) | copy-start | bytes 24580
  326.9 168.8 %copy-start.83 = (bf16[12,4,9,512]{3,2,1,0:T(8,128)(2,1)}, bf16[12,4,9,512]{3,2,1,0:T(8,128)(2,1)S(1)}, u32[]{:S(2)}) copy-start(bf16[12,4,9,512]{3,2,1,0:T(8,128)(2,1)S(1)} %slice.1700) | copy-start | bytes 1327108
  661.5 491.3 %copy-start.241 = (f32[1,512]{1,0:T(1,128)}, f32[1,512]{1,0:T(1,128)S(1)}, u32[]{:S(2)}) copy-start(f32[1,512]{1,0:T(1,128)S(1)} %get-tuple-element.679) | copy-start | bytes 6148
  661.5 491.2 %copy-start.246 = (f32[512]{0:T(512)}, f32[512]{0:T(512)S(1)}, u32[]{:S(2)}) copy-start(f32[512]{0:T(512)S(1)} %get-tuple-element.674) | copy-start | bytes 6148
  661.5 491.2 %copy-start.276 = (f32[512]{0:T(512)}, f32[512]{0:T(512)S(1)}, u32[]{:S(2)}) copy-start(f32[512]{0:T(512)S(1)} %get-tuple-element.673) | copy-start | bytes 6148
  667.5 7.9 collective-permute-start.1
  670.0 6.5 collective-permute-start.2
  745.7 268.2 %copy-start.273 = (f32[1,512]{1,0:T(1,128)}, f32[1,512]{1,0:T(1,128)S(1)}, u32[]{:S(2)}) copy-start(f32[1,512]{1,0:T(1,128)S(1)} %get-tuple-element.677) | copy-start | bytes 6148
  745.8 268.2 %copy-start.282 = (f32[512]{0:T(512)}, f32[512]{0:T(512)S(1)}, u32[]{:S(2)}) copy-start(f32[512]{0:T(512)S(1)} %get-tuple-element.672) | copy-start | bytes 6148
  1123.3 23.5 collective-permute-start.3
  1125.3 21.5 collective-permute-start.4
  1546.7 9.4 collective-permute-start.5
  1626.8 159.5 %reduce-scatter.20.cloned.1.call-start = ((), (), s32[]{:S(2)}) async-start(), calls=%async_computation.13 | async-start | bytes 4718592 | tf_op jit(solution)/shard_map/reduce_scatter | solution.py:582
  1634.6 243.7 %reduce-scatter.16.cloned.1.call-start = ((), (), s32[]{:S(2)}) async-start(), calls=%async_computation.11 | async-start | bytes 4718592 | tf_op jit(solution)/shard_map/reduce_scatter | solution.py:580
  1642.9 326.7 %reduce-scatter.12.cloned.1.call-start = ((), (), s32[]{:S(2)}) async-start(), calls=%async_computation.9 | async-start | bytes 4718592 | tf_op jit(solution)/shard_map/reduce_scatter | solution.py:578
  1655.4 466.9 %reduce-scatter.14.cloned.1.call-start = ((), (), s32[]{:S(2)}) async-start(), calls=%async_computation.10 | async-start | bytes 9437184 | tf_op jit(solution)/shard_map/reduce_scatter | solution.py:579
  1668.0 620.7 %reduce-scatter.18.cloned.1.call-start = ((), (), s32[]{:S(2)}) async-start(), calls=%async_computation.12 | async-start | bytes 10616832 | tf_op jit(solution)/shard_map/reduce_scatter | solution.py:581
  1702.2 753.1 %reduce-scatter.10.cloned.1.call-start = ((), (), s32[]{:S(2)}) async-start(), calls=%async_computation.8 | async-start | bytes 10616832 | tf_op jit(solution)/shard_map/reduce_scatter | solution.py:577
  1735.3 787.4 %all-reduce.12.cloned.1.call-start = ((), (), s32[]{:S(2)}) async-start(), calls=%async_computation.14 | async-start | bytes 5636096 | tf_op jit(solution)/shard_map/psum | solution.py:323
  (372 other events, 3026.2 us)
Sparse Core Ops, SparseCore 0:
  1626.9 68.5 reduce-scatter.7
  1699.2 87.1 reduce-scatter.19
  1790.4 87.8 reduce-scatter.15
  1881.8 87.7 reduce-scatter.11
  1973.5 148.7 reduce-scatter.13
  2125.8 162.8 reduce-scatter.17
  2292.3 162.9 reduce-scatter.9
  2459.2 63.4 all-reduce.11
where the time goes:
time: 2580 us; the launch traced here: 2540 us
  waiting for transfers between devices  708 us (27%)
  local copies, waits for them, and re-layouts  563 us (22%)
  blocking collectives  502 us (19%)
  other arithmetic  378 us (15%)
  matrix products  349 us (14%)
  between operations  28.3 us (1%)
    slice x21, local copies, waits for them, and re-layouts, tap_window(): padded[:, row_tap:row_tap + stride * (out_rows - 1) + 1:stride, col_tap:c...  312 us
    psum x6, blocking collectives, gather_stats(): summed = lax.psum(jnp.stack(local_sums), ('batch', 'height'))  257 us
    psum x6, blocking collectives, grad_stats(): summed = lax.psum(jnp.stack(local_sums), ('batch', 'height'))  246 us
    dot_general x69, matrix products, project_back(): jnp.einsum('ihwd,cd->ihwc', grad_in, weight, preferred_element_type=jnp.f...  175 us
    reduce_scatter x1, waiting for transfers between devices, per_device(): lax.psum_scatter(spatial_a_local, 'batch', scatter_dimension=2, tiled=True)  164 us
    reduce_scatter x1, waiting for transfers between devices, per_device(): lax.psum_scatter(spatial_b_local, 'batch', scatter_dimension=2, tiled=True)  164 us
    reduce_scatter x1, waiting for transfers between devices, per_device(): lax.psum_scatter(shortcut_a_local, 'batch', scatter_dimension=0, tiled=True)  151 us
    scatter-add x27, other arithmetic, spatial_back(): padded_grad = padded_grad.at[:, row_tap:row_tap + stride * (out_rows - 1)...  139 us
  transfers between devices with their start and end apart: 14, of which 7 were waited for; matrix products, arithmetic and copies ran while one was open for 9% of the time, Pallas kernels for 0%

commit v1 on v0

--- a/solution.py
+++ b/solution.py
@@ -1,9 +1,75 @@
+import functools
+
 import jax
 import jax.numpy as jnp
 from jax import lax
+from jax.experimental import pallas as pl
+from jax.experimental.pallas import tpu as pltpu
 from jax.sharding import PartitionSpec as P
 
 epsilon = 1e-05
+
+MESH = pl.DeviceIdType.MESH
+
+
+def sum_kernel(n_batch, n_height, value_ref, out_ref, height_slots, batch_slots, send_sem, recv_sem):
+    b, h = lax.axis_index("batch"), lax.axis_index("height")
+    barrier = pltpu.get_barrier_semaphore()
+    for k in range(1, n_height):
+        pl.semaphore_signal(
+            barrier, inc=1, device_id=(b, lax.rem(h + k, n_height)), device_id_type=MESH
+        )
+
+    @pl.loop(1, n_batch)
+    def _(k):
+        pl.semaphore_signal(
+            barrier, inc=1, device_id=(lax.rem(b + k, n_batch), h), device_id_type=MESH
+        )
+
+    pl.semaphore_wait(barrier, n_height + n_batch - 2)
+    for slots, me, count, level, peer in (
+        (height_slots, h, n_height, 0, lambda p: (b, p)),
+        (batch_slots, b, n_batch, 1, lambda p: (p, h)),
+    ):
+        slots[me] = value_ref[...] if level == 0 else jnp.sum(height_slots[...], axis=0)
+
+        @pl.loop(1, count)
+        def _(k):
+            pltpu.make_async_remote_copy(
+                src_ref=slots.at[me],
+                dst_ref=slots.at[me],
+                send_sem=send_sem.at[level],
+                recv_sem=recv_sem.at[level],
+                device_id=peer(lax.rem(me + k, count)),
+                device_id_type=MESH,
+            ).start()
+
+        others = slots.at[0 : count - 1]
+        pltpu.make_async_copy(others, others, send_sem.at[level]).wait()
+        pltpu.make_async_copy(others, others, recv_sem.at[level]).wait()
+    out_ref[...] = jnp.sum(batch_slots[...], axis=0)
+
+
+def sum_over_all(stacked):
+    flat = (stacked.size // 128, 128)
+    n_batch, n_height = lax.axis_size("batch"), lax.axis_size("height")
+    summed = pl.pallas_call(
+        functools.partial(sum_kernel, n_batch, n_height),
+        out_shape=jax.ShapeDtypeStruct(flat, jnp.float32),
+        in_specs=[pl.BlockSpec(memory_space=pltpu.VMEM)],
+        out_specs=pl.BlockSpec(memory_space=pltpu.VMEM),
+        scratch_shapes=[
+            pltpu.VMEM((n_height,) + flat, jnp.float32),
+            pltpu.VMEM((n_batch,) + flat, jnp.float32),
+            pltpu.SemaphoreType.DMA((2,)),
+            pltpu.SemaphoreType.DMA((2,)),
+        ],
+        compiler_params=pltpu.CompilerParams(
+            collective_id=stacked.size.bit_length() - 10, has_side_effects=True
+        ),
+        name="sum_over_all",
+    )(stacked.reshape(flat))
+    return summed.reshape(stacked.shape)
 
 
 def passed_along(value, axis, steps):
@@ -31,20 +97,19 @@
 
 
 def project(values, weight):
-    return jnp.einsum("ihwc,cd->ihwd", values, weight, preferred_element_type=jnp.float32)
+    return jnp.einsum("hwic,cd->hwid", values, weight, preferred_element_type=jnp.float32)
 
 
 def project_back(grad_in, weight):
-    return jnp.einsum("ihwd,cd->ihwc", grad_in, weight, preferred_element_type=jnp.float32)
+    return jnp.einsum("hwid,cd->hwic", grad_in, weight, preferred_element_type=jnp.float32)
 
 
 def weight_term(values, grad_in):
-    return jnp.einsum("ihwc,ihwd->cd", values, grad_in, preferred_element_type=jnp.float32)
+    return jnp.einsum("hwic,hwid->cd", values, grad_in, preferred_element_type=jnp.float32)
 
 
 def tap_window(padded, stride, out_rows, out_cols, row_tap, col_tap):
     return padded[
-        :,
         row_tap : row_tap + stride * (out_rows - 1) + 1 : stride,
         col_tap : col_tap + stride * (out_cols - 1) + 1 : stride,
     ]
@@ -71,7 +136,6 @@
             window = tap_window(padded, stride, out_rows, out_cols, row_tap, col_tap)
             row_list.append(weight_term(window, grad_in))
             padded_grad = padded_grad.at[
-                :,
                 row_tap : row_tap + stride * (out_rows - 1) + 1 : stride,
                 col_tap : col_tap + stride * (out_cols - 1) + 1 : stride,
             ].add(project_back(grad_in, weight[row_tap, col_tap]))
@@ -84,7 +148,7 @@
     for tensors in levels:
         local_sums.append(sum((jnp.sum(member, axis=(0, 1, 2)) for member in tensors)))
         local_sums.append(sum((jnp.sum(member * member, axis=(0, 1, 2)) for member in tensors)))
-    summed = lax.psum(jnp.stack(local_sums), ("batch", "height"))
+    summed = sum_over_all(jnp.stack(local_sums))
     result = []
     for position in range(len(levels)):
         centre = summed[2 * position] / numbers[position]
@@ -118,7 +182,7 @@
                 )
             )
         )
-    summed = lax.psum(jnp.stack(local_sums), ("batch", "height"))
+    summed = sum_over_all(jnp.stack(local_sums))
     return [(summed[2 * position], summed[2 * position + 1]) for position in range(len(triples))]
 
 
@@ -153,7 +217,7 @@
     upstream_medium,
     upstream_large,
 ):
-    raw_images = (image_small, image_medium, image_large)
+    raw_images = tuple(jnp.transpose(v, (1, 2, 0, 3)) for v in (image_small, image_medium, image_large))
     upstreams = (upstream_small, upstream_medium, upstream_large)
     band_index = lax.axis_index("height")
     batch_devices = lax.axis_size("batch")
@@ -168,25 +232,26 @@
     total_in = 0
     total_out = 0
     for picture_batches in range(3):
-        slab_rows = raw_images[picture_batches].shape[1]
+        slab_rows = raw_images[picture_batches].shape[0]
         bucket_limit = slab_rows // 2
-        out_side = raw_images[picture_batches].shape[2] // 2
+        out_side = raw_images[picture_batches].shape[1] // 2
         live = row_counts[picture_batches, band_index]
         mask_low = (jnp.arange(slab_rows, dtype=jnp.int32) < 2 * live).astype(jnp.bfloat16)[
-            None, :, None, None
+
+            :, None, None, None
         ]
         entering_photos.append(raw_images[picture_batches] * mask_low)
         entering_filters.append(mask_low.astype(jnp.float32))
         line_filters.append(
             (jnp.arange(bucket_limit, dtype=jnp.int32) < live).astype(jnp.float32)[
-                None, :, None, None
+            :, None, None, None
             ]
         )
         genuine_lines.append(live)
         edge_extents.append(out_side)
         bucket_limits.append(bucket_limit)
-        total_in += batch_devices * raw_images[picture_batches].shape[0] * 4 * out_side * out_side
-        total_out += batch_devices * raw_images[picture_batches].shape[0] * out_side * out_side
+        total_in += batch_devices * raw_images[picture_batches].shape[2] * 4 * out_side * out_side
+        total_out += batch_devices * raw_images[picture_batches].shape[2] * out_side * out_side
     width_cuts = [edge_extents[0], edge_extents[0] + edge_extents[1]]
     input_cuts = [2 * edge_extents[0], 2 * edge_extents[0] + 2 * edge_extents[1]]
     first_out = [
@@ -205,18 +270,18 @@
     ]
     tail_rows = [
         lax.dynamic_index_in_dim(
-            act_one[picture_batches], 2 * genuine_lines[picture_batches] - 1, 1, keepdims=False
-        )
-        for picture_batches in range(3)
-    ]
-    rim_rows = passed_along(jnp.concatenate(tail_rows, axis=1), "height", 1)
-    rim_parts = jnp.split(rim_rows, input_cuts, axis=1)
+            act_one[picture_batches], 2 * genuine_lines[picture_batches] - 1, 0, keepdims=False
+        )
+        for picture_batches in range(3)
+    ]
+    rim_rows = passed_along(jnp.concatenate(tail_rows, axis=0), "height", 1)
+    rim_parts = jnp.split(rim_rows, input_cuts, axis=0)
     first_padded = []
     for picture_batches in range(3):
         joined = jnp.concatenate(
-            [rim_parts[picture_batches][:, None], act_one[picture_batches]], axis=1
-        )
-        first_padded.append(jnp.pad(joined, ((0, 0), (0, 0), (1, 0), (0, 0))))
+            [rim_parts[picture_batches][None], act_one[picture_batches]], axis=0
+        )
+        first_padded.append(jnp.pad(joined, ((0, 0), (1, 0), (0, 0), (0, 0))))
     second_out = [
         spatial_kernel(
             first_padded[picture_batches],
@@ -238,7 +303,7 @@
         for picture_batches in range(3)
     ]
     third_out = [project(act_two[picture_batches], expand_a) for picture_batches in range(3)]
-    side_inputs = [entering_photos[picture_batches][:, ::2, ::2] for picture_batches in range(3)]
+    side_inputs = [entering_photos[picture_batches][::2, ::2] for picture_batches in range(3)]
     side_out = [project(side_inputs[picture_batches], shortcut_a) for picture_batches in range(3)]
     stat_three, stat_side = gather_stats([third_out, side_out], [total_out, total_out])
     joint_one = [
@@ -266,27 +331,27 @@
     edge_pairs = [
         jnp.stack(
             [
-                act_four[picture_batches][:, 0],
+                act_four[picture_batches][0],
                 lax.dynamic_index_in_dim(
-                    act_four[picture_batches], genuine_lines[picture_batches] - 1, 1, keepdims=False
+                    act_four[picture_batches], genuine_lines[picture_batches] - 1, 0, keepdims=False
                 ),
             ],
-            axis=1,
-        )
-        for picture_batches in range(3)
-    ]
-    rim_pairs = extended(jnp.concatenate(edge_pairs, axis=2), (("height", 1),), 1)
-    pair_parts = jnp.split(rim_pairs, width_cuts, axis=2)
+            axis=0,
+        )
+        for picture_batches in range(3)
+    ]
+    rim_pairs = extended(jnp.concatenate(edge_pairs, axis=1), (("height", 0),), 1)
+    pair_parts = jnp.split(rim_pairs, width_cuts, axis=1)
     fourth_padded = []
     for picture_batches in range(3):
         rim_pair = pair_parts[picture_batches]
         joined = jnp.concatenate(
-            [rim_pair[:, 0:1], act_four[picture_batches], jnp.zeros_like(rim_pair[:, 0:1])], axis=1
+            [rim_pair[0:1], act_four[picture_batches], jnp.zeros_like(rim_pair[0:1])], axis=0
         )
         joined = lax.dynamic_update_slice_in_dim(
-            joined, rim_pair[:, 3:4], genuine_lines[picture_batches] + 1, 1
-        )
-        fourth_padded.append(jnp.pad(joined, ((0, 0), (0, 0), (1, 1), (0, 0))))
+            joined, rim_pair[3:4], genuine_lines[picture_batches] + 1, 0
+        )
+        fourth_padded.append(jnp.pad(joined, ((0, 0), (1, 1), (0, 0), (0, 0))))
     fifth_out = [
         spatial_kernel(
             fourth_padded[picture_batches],
@@ -322,7 +387,7 @@
     ]
     pooled_sums = lax.psum(
         jnp.stack(
-            [jnp.sum(final[picture_batches], axis=(1, 2)) for picture_batches in range(3)]
+            [jnp.sum(final[picture_batches], axis=(0, 1)) for picture_batches in range(3)]
         ).astype(jnp.bfloat16),
         "height",
     ).astype(jnp.float32)
@@ -332,7 +397,7 @@
         for picture_batches in range(3)
     ]
     d_joint_two = [
-        upstreams[picture_batches].astype(jnp.float32)[:, None, None, :]
+        upstreams[picture_batches].astype(jnp.float32)[None, None]
         / (edge_extents[picture_batches] * edge_extents[picture_batches])
         * line_filters[picture_batches]
         * sigmoid_slope(joint_two[picture_batches])
@@ -393,30 +458,30 @@
             edge_extents[picture_batches],
         )
         spatial_b_local = tap_grad if spatial_b_local is None else spatial_b_local + tap_grad
-        central_block = padded_grad[:, :, 1:-1]
-        top_grad = central_block[:, 0]
+        central_block = padded_grad[:, 1:-1]
+        top_grad = central_block[0]
         below_grad = lax.dynamic_index_in_dim(
-            central_block, genuine_lines[picture_batches] + 1, 1, keepdims=False
-        )
-        d_swish_four.append(central_block[:, 1 : bucket_limits[picture_batches] + 1])
-        edge_grads.append(jnp.stack([top_grad, below_grad], axis=1))
+            central_block, genuine_lines[picture_batches] + 1, 0, keepdims=False
+        )
+        d_swish_four.append(central_block[1 : bucket_limits[picture_batches] + 1])
+        edge_grads.append(jnp.stack([top_grad, below_grad], axis=0))
     returned = extended(
-        jnp.concatenate(edge_grads, axis=2).astype(jnp.bfloat16), (("height", 1),), 1
+        jnp.concatenate(edge_grads, axis=1).astype(jnp.bfloat16), (("height", 0),), 1
     ).astype(jnp.float32)
-    returned_parts = jnp.split(returned, width_cuts, axis=2)
+    returned_parts = jnp.split(returned, width_cuts, axis=1)
     d_four = []
     for picture_batches in range(3):
         grad_rows = (
-            d_swish_four[picture_batches].at[:, 0].add(returned_parts[picture_batches][:, 0])
+            d_swish_four[picture_batches].at[0].add(returned_parts[picture_batches][0])
         )
         last_row = (
             lax.dynamic_index_in_dim(
-                grad_rows, genuine_lines[picture_batches] - 1, 1, keepdims=False
-            )
-            + returned_parts[picture_batches][:, 3]
+                grad_rows, genuine_lines[picture_batches] - 1, 0, keepdims=False
+            )
+            + returned_parts[picture_batches][3]
         )
         grad_rows = lax.dynamic_update_index_in_dim(
-            grad_rows, last_row, genuine_lines[picture_batches] - 1, 1
+            grad_rows, last_row, genuine_lines[picture_batches] - 1, 0
         )
         d_four.append(
             grad_rows * sigmoid_slope(pre_four[picture_batches]) * line_filters[picture_batches]
@@ -525,21 +590,21 @@
             edge_extents[picture_batches],
         )
         spatial_a_local = tap_grad if spatial_a_local is None else spatial_a_local + tap_grad
-        rim_grads.append(padded_grad[:, 0, 1:])
-        d_act_one.append(padded_grad[:, 1:, 1:])
+        rim_grads.append(padded_grad[0, 1:])
+        d_act_one.append(padded_grad[1:, 1:])
     rim_back = passed_along(
-        jnp.concatenate(rim_grads, axis=1).astype(jnp.bfloat16), "height", -1
+        jnp.concatenate(rim_grads, axis=0).astype(jnp.bfloat16), "height", -1
     ).astype(jnp.float32)
-    rim_back_parts = jnp.split(rim_back, input_cuts, axis=1)
+    rim_back_parts = jnp.split(rim_back, input_cuts, axis=0)
     d_one = []
     for picture_batches in range(3):
         row_place = 2 * genuine_lines[picture_batches] - 1
         last_row = (
-            lax.dynamic_index_in_dim(d_act_one[picture_batches], row_place, 1, keepdims=False)
+            lax.dynamic_index_in_dim(d_act_one[picture_batches], row_place, 0, keepdims=False)
             + rim_back_parts[picture_batches]
         )
         grad_rows = lax.dynamic_update_index_in_dim(
-            d_act_one[picture_batches], last_row, row_place, 1
+            d_act_one[picture_batches], last_row, row_place, 0
         )
         d_one.append(
             grad_rows * sigmoid_slope(pre_one[picture_batches]) * entering_filters[picture_batches]
@@ -568,10 +633,10 @@
     backs = []
     for picture_batches in range(3):
         image_grad = project_back(grad_one[picture_batches], reduce_a)
-        image_grad = image_grad.at[:, ::2, ::2].add(
+        image_grad = image_grad.at[::2, ::2].add(
             project_back(grad_side[picture_batches], shortcut_a)
         )
-        backs.append(image_grad.astype(jnp.bfloat16))
+        backs.append(jnp.transpose(image_grad.astype(jnp.bfloat16), (2, 0, 1, 3)))
     shards = (
         lax.psum_scatter(reduce_a_local, "batch", scatter_dimension=0, tiled=True),
         lax.psum_scatter(spatial_a_local, "batch", scatter_dimension=2, tiled=True),

time: 2580 us -> 1820 us (0.71)
  blocking collectives: 502 us -> 0 us
  local copies, waits for them, and re-layouts: 563 us -> 275 us
  Pallas kernels: 0 us -> 147 us
  matrix products: 349 us -> 275 us
  other arithmetic: 378 us -> 343 us
    psum x12 -> x0, blocking collectives: 502 us -> none  [the longest x6 257 us: gather_stats(): summed = lax.psum(jnp.stack(local_sums), ('batch', 'height'))]
    slice x40 -> x39, local copies, waits for them, and re-layouts: 341 us -> 176 us  [the longest x18 84.6 us: tap_window(): padded[row_tap:row_tap + stride * (out_rows - 1) + 1:stride, col_tap:col_...]
    pallas_call x0 -> x12, Pallas kernels: none -> 147 us  [sum_over_all(): pl.pallas_call(functools.partial(sum_kernel, n_batch, n_height), out_shap...]
    scatter-add x27 -> x3, local copies, waits for them, and re-layouts: 115 us -> 0.56 us  [spatial_back(): padded_grad = padded_grad.at[row_tap:row_tap + stride * (out_rows - 1) +...]
    dot_general x207, matrix products: 349 us -> 275 us  [the longest x69 130 us: project_back(): jnp.einsum('hwid,cd->hwic', grad_in, weight, preferred_element_type=jnp.f...]
  transfers between devices with their start and end apart: 14 -> 14, of which waited for: 7 -> 7; matrix products, arithmetic and copies ran while one was open for 9% -> 16% of each run, Pallas kernels for 0% -> 0%
where the time goes in v1:
time: 1820 us; the launch traced here: 1800 us
  waiting for transfers between devices  719 us (40%)
  other arithmetic  343 us (19%)
  local copies, waits for them, and re-layouts  275 us (15%)
  matrix products  275 us (15%)
  Pallas kernels  147 us (8%)
  between operations  28.8 us (2%)
    reduce_scatter x1, waiting for transfers between devices, per_device(): lax.psum_scatter(spatial_a_local, 'batch', scatter_dimension=2, tiled=True)  164 us
    reduce_scatter x1, waiting for transfers between devices, per_device(): lax.psum_scatter(spatial_b_local, 'batch', scatter_dimension=2, tiled=True)  164 us
    reduce_scatter x1, waiting for transfers between devices, per_device(): lax.psum_scatter(shortcut_a_local, 'batch', scatter_dimension=0, tiled=True)  151 us
    pallas_call x12, Pallas kernels, sum_over_all(): pl.pallas_call(functools.partial(sum_kernel, n_batch, n_height), out_shap...  147 us
    scatter-add x27, other arithmetic, spatial_back(): padded_grad = padded_grad.at[row_tap:row_tap + stride * (out_rows - 1) +...  142 us
    dot_general x69, matrix products, project_back(): jnp.einsum('hwid,cd->hwic', grad_in, weight, preferred_element_type=jnp.f...  130 us
    reduce_scatter x1, waiting for transfers between devices, per_device(): lax.psum_scatter(reduce_b_local, 'batch', scatter_dimension=0, tiled=True)  90 us
    reduce_scatter x1, waiting for transfers between devices, per_device(): lax.psum_scatter(expand_a_local, 'batch', scatter_dimension=0, tiled=True)  89.4 us
  transfers between devices with their start and end apart: 14, of which 7 were waited for; matrix products, arithmetic and copies ran while one was open for 16% of the time, Pallas kernels for 0%

profile of v1, /device:TPU:0, one launch (start us, length us, event | category | flops | bytes accessed | tf_op | source)
XLA Modules:
  0.0 1798.9 jit_solution(17401650065120820566)
XLA Ops:
  27.2 12.7 sum_over_all.12
  58.9 42.5 %slice.1765 = bf16[4,9,12,1024]{3,0,1,2:T(4,128)(2,1)S(1)} slice(bf16[8,18,12,1024]{3,0,1,2:T(8,128)(2,1)} %copy-done.57), slice={[0:8:2], [0:18:2], [0:12:1], [0:1024:1]} | slice | bytes 1769472 | tf_op jit(solution)/shard_map/slice | solution.py:306
  101.4 18.5 %slice.1764 = bf16[3,7,12,1024]{3,1,0,2:T(8,128)(2,1)} slice(bf16[6,14,12,1024]{3,1,0,2:T(8,128)(2,1)} %copy-done.87), slice={[0:6:2], [0:14:2], [0:12:1], [0:1024:1]} | slice | bytes 1032192 | tf_op jit(solution)/shard_map/slice | solution.py:306
  119.9 22.2 %slice.1763 = bf16[2,5,12,1024]{3,0,1,2:T(2,128)(2,1)S(1)} slice(bf16[4,10,12,1024]{3,0,1,2:T(4,128)(2,1)} %copy-done.131), slice={[0:4:2], [0:10:2], [0:12:1], [0:1024:1]} | slice | bytes 491520 | tf_op jit(solution)/shard_map/slice | solution.py:306
  290.9 10.6 sum_over_all.13
  314.1 13.4 sum_over_all.14
  343.1 11.8 sum_over_all.15
  394.6 12.7 sum_over_all.16
  419.2 11.2 sum_over_all.17
  447.8 12.5 sum_over_all.18
  475.7 10.8 sum_over_all.19
  555.6 13.6 sum_over_all.20
  583.1 8.6 multiply_reduce_fusion.2
  592.5 13.4 sum_over_all.21
  627.3 11.8 sum_over_all.22
  858.7 12.4 sum_over_all.23
  1001.4 10.3 scatter_fusion.29
  1019.9 26.0 %reduce-scatter.20.cloned.1.call-done = f32[64,2048]{1,0:T(8,128)} async-done(((f32[512,2048]{1,0:T(8,128)}), f32[64,2048]{1,0:T(8,128)}) %reduce-scatter.20.cloned.1.call-update) | async-done | bytes 524304 | tf_op jit(solution)/shard_map/reduce_scatter | solution.py:647
  1047.8 90.0 %reduce-scatter.16.cloned.1.call-done = f32[256,512]{1,0:T(8,128)} async-done(((f32[2048,512]{1,0:T(8,128)}), f32[256,512]{1,0:T(8,128)}) %reduce-scatter.16.cloned.1.call-update) | async-done | bytes 524304 | tf_op jit(solution)/shard_map/reduce_scatter | solution.py:645
  1139.6 89.4 %reduce-scatter.12.cloned.1.call-done = f32[64,2048]{1,0:T(8,128)} async-done(((f32[512,2048]{1,0:T(8,128)}), f32[64,2048]{1,0:T(8,128)}) %reduce-scatter.12.cloned.1.call-update) | async-done | bytes 524304 | tf_op jit(solution)/shard_map/reduce_scatter | solution.py:643
  1230.8 150.9 %reduce-scatter.14.cloned.1.call-done = f32[128,2048]{1,0:T(8,128)} async-done(((f32[1024,2048]{1,0:T(8,128)}), f32[128,2048]{1,0:T(8,128)}) %reduce-scatter.14.cloned.1.call-update) | async-done | bytes 1048592 | tf_op jit(solution)/shard_map/reduce_scatter | solution.py:644
  1383.8 164.1 %reduce-scatter.18.cloned.1.call-done = f32[3,3,64,512]{3,2,1,0:T(8,128)} async-done(((f32[3,3,512,512]{3,2,1,0:T(8,128)}), f32[3,3,64,512]{3,2,1,0:T(8,128)}) %reduce-scatter.18.cloned.1.call-update) | async-done | bytes 1179664 | tf_op jit(solution)/shard_map/reduce_scatter | solution.py:646
  1550.0 164.5 %reduce-scatter.10.cloned.1.call-done = f32[3,3,64,512]{3,2,1,0:T(8,128)} async-done(((f32[3,3,512,512]{3,2,1,0:T(8,128)}), f32[3,3,64,512]{3,2,1,0:T(8,128)}) %reduce-scatter.10.cloned.1.call-update) | async-done | bytes 1179664 | tf_op jit(solution)/shard_map/reduce_scatter | solution.py:642
  1748.2 33.9 %all-reduce.12.cloned.1.call-done = (bf16[3,12,2048]{2,1,0:T(8,128)(2,1)}, bf16[128,512]{1,0:T(8,128)(2,1)}, bf16[3,3,64,512]{3,2,1,0:T(8,128)(2,1)}, bf16[64,20...) async-done(((bf16[3,12,2048]{2,1,0:T(8,128)(2,1)}, ...) | async-done | bytes 2768912 | tf_op jit(solution)/shard_map/psum | solution.py:388
  (1357 shorter events, 802.4 us)
Async XLA Ops:
  7.2 326.4 %copy-start = (bf16[2048,512]{1,0:T(8,128)(2,1)S(1)}, bf16[2048,512]{1,0:T(8,128)(2,1)}, u32[]{:S(2)}) copy-start(bf16[2048,512]{1,0:T(8,128)(2,1)} %param.86) | copy-start | bytes 6291460
  7.2 1011.1 %reduce-scatter.8.cloned.1.call-start = ((), (), s32[]{:S(2)}) async-start(), calls=%async_computation.7 | async-start | bytes 2359296 | tf_op jit(solution)/shard_map/reduce_scatter | solution.py:641
  43.2 266.5 %copy-start.310 = (f32[1,512]{1,0:T(1,128)}, f32[1,512]{1,0:T(1,128)S(1)}, u32[]{:S(2)}) copy-start(f32[1,512]{1,0:T(1,128)S(1)} %get-tuple-element.613) | copy-start | bytes 6148
  43.2 313.9 %copy-start.238 = (f32[1,512]{1,0:T(1,128)}, f32[1,512]{1,0:T(1,128)S(1)}, u32[]{:S(2)}) copy-start(f32[1,512]{1,0:T(1,128)S(1)} %get-tuple-element.615) | copy-start | bytes 6148
  55.1 118.2 %collective-permute-start = (bf16[42,12,512]{2,0,1:T(8,128)(2,1)}, bf16[42,12,512]{2,0,1:T(8,128)(2,1)}, u32[]{:S(2)}, u32[]{:S(2)}) collective-permute-start(bf16[42,12,512]{2,0,1:T(8,128)(2,1)} %pad_maximum_fusion.1), channel_id=1, source_target_pairs={{0,1},{1,2},{2,3},{4,5},{5,6},{6,7},{8,9},{9,10},{10,11},{12,13},{... | collective-permute-start | bytes 1548296 | tf_op jit(solution)/shard_map/ppermute | solution.py:78
  58.2 271.3 %copy-start.250 = (f32[3]{0:T(128)}, f32[3]{0:T(128)S(1)}, u32[]{:S(2)}) copy-start(f32[3]{0:T(128)S(1)} %compare_convert_fusion.1) | copy-start | bytes 40
  58.9 298.1 %copy-start.256 = (f32[2]{0:T(128)}, f32[2]{0:T(128)S(1)}, u32[]{:S(2)}) copy-start(f32[2]{0:T(128)S(1)} %compare_convert_fusion.2) | copy-start | bytes 28
  162.9 173.8 %copy-start.221 = (f32[1,2048]{1,0:T(1,128)}, f32[1,2048]{1,0:T(1,128)S(1)}, u32[]{:S(2)}) copy-start(f32[1,2048]{1,0:T(1,128)S(1)} %get-tuple-element.598) | copy-start | bytes 24580
  162.9 173.8 %copy-start.223 = (f32[1,2048]{1,0:T(1,128)}, f32[1,2048]{1,0:T(1,128)S(1)}, u32[]{:S(2)}) copy-start(f32[1,2048]{1,0:T(1,128)S(1)} %get-tuple-element.599) | copy-start | bytes 24580
  168.6 168.2 %copy-start.245 = (f32[4]{0:T(128)}, f32[4]{0:T(128)S(1)}, u32[]{:S(2)}) copy-start(f32[4]{0:T(128)S(1)} %compare_convert_fusion) | copy-start | bytes 52
  360.3 10.1 collective-permute-start.1
  363.5 8.6 collective-permute-start.2
  408.0 104.5 %copy-start.280 = (f32[512]{0:T(512)}, f32[512]{0:T(512)S(1)}, u32[]{:S(2)}) copy-start(f32[512]{0:T(512)S(1)} %multiply_bitcast_fusion.20) | copy-start | bytes 6148
  523.4 22.3 %collective-permute-start.3 = (bf16[1,21,12,512]{3,2,1,0:T(8,128)(2,1)}, bf16[1,21,12,512]{3,2,1,0:T(8,128)(2,1)S(1)}, u32[]{:S(2)}, u32[]{:S(2)}) collective-permute-start(bf16[1,21,12,512]{3,2,1,0:T(8,128)(2,1)} %get-tuple-element.569), channel_id=1, source_target_pairs={{0,1},{1,2},{2,3},{4,5},{5,6},{6,7},{8,9},{9,10},{10,11},{12,13},{... | collective-permute-start | bytes 774152 | tf_op jit(solution)/shard_map/ppermute | solution.py:88
  524.7 21.0 %collective-permute-start.4 = (bf16[1,21,12,512]{3,2,1,0:T(8,128)(2,1)}, bf16[1,21,12,512]{3,2,1,0:T(8,128)(2,1)}, u32[]{:S(2)}, u32[]{:S(2)}) collective-permute-start(bf16[1,21,12,512]{3,2,1,0:T(8,128)(2,1)} %get-tuple-element.570), channel_id=1, source_target_pairs={{1,0},{2,1},{3,2},{5,4},{6,5},{7,6},{9,8},{10,9},{11,10},{13,12},{... | collective-permute-start | bytes 774152 | tf_op jit(solution)/shard_map/ppermute | solution.py:89
  839.8 7.9 collective-permute-start.5
  887.9 158.1 %reduce-scatter.20.cloned.1.call-start = ((), (), s32[]{:S(2)}) async-start(), calls=%async_computation.13 | async-start | bytes 4718592 | tf_op jit(solution)/shard_map/reduce_scatter | solution.py:647
  896.7 241.1 %reduce-scatter.16.cloned.1.call-start = ((), (), s32[]{:S(2)}) async-start(), calls=%async_computation.11 | async-start | bytes 4718592 | tf_op jit(solution)/shard_map/reduce_scatter | solution.py:645
  905.5 323.5 %reduce-scatter.12.cloned.1.call-start = ((), (), s32[]{:S(2)}) async-start(), calls=%async_computation.9 | async-start | bytes 4718592 | tf_op jit(solution)/shard_map/reduce_scatter | solution.py:643
  913.6 468.1 %reduce-scatter.14.cloned.1.call-start = ((), (), s32[]{:S(2)}) async-start(), calls=%async_computation.10 | async-start | bytes 9437184 | tf_op jit(solution)/shard_map/reduce_scatter | solution.py:644
  924.6 623.3 %reduce-scatter.18.cloned.1.call-start = ((), (), s32[]{:S(2)}) async-start(), calls=%async_computation.12 | async-start | bytes 10616832 | tf_op jit(solution)/shard_map/reduce_scatter | solution.py:646
  948.7 765.7 %reduce-scatter.10.cloned.1.call-start = ((), (), s32[]{:S(2)}) async-start(), calls=%async_computation.8 | async-start | bytes 10616832 | tf_op jit(solution)/shard_map/reduce_scatter | solution.py:642
  982.3 799.7 %all-reduce.12.cloned.1.call-start = ((), (), s32[]{:S(2)}) async-start(), calls=%async_computation.14 | async-start | bytes 5636096 | tf_op jit(solution)/shard_map/psum | solution.py:388
  1550.0 166.6 %copy-start.56 = (bf16[6,14,12,512]{3,1,2,0:T(8,128)(2,1)S(1)}, bf16[6,14,12,512]{3,1,2,0:T(8,128)(2,1)}, u32[]{:S(2)}) copy-start(bf16[6,14,12,512]{3,1,2,0:T(8,128)(2,1)} %copy-done.55) | copy-start | bytes 3096580
  (363 other events, 2355.3 us)
Sparse Core Ops, SparseCore 0:
  888.0 67.2 reduce-scatter.7
  958.9 87.0 reduce-scatter.19
  1050.1 87.6 reduce-scatter.15
  1141.3 87.6 reduce-scatter.11
  1232.9 148.7 reduce-scatter.13
  1385.1 162.6 reduce-scatter.17
  1551.5 162.9 reduce-scatter.9
  1718.5 63.4 all-reduce.11

commit v2 on v1

--- a/solution.py
+++ b/solution.py
@@ -70,6 +70,218 @@
         name="sum_over_all",
     )(stacked.reshape(flat))
     return summed.reshape(stacked.shape)
+
+
+N_CHUNKS = 10
+
+
+def grads_kernel(n_batch, local_ref, out_ref, g, r0, r1, r2, r3, load_sem, send_sem, recv_sem):
+    b, h = lax.axis_index("batch"), lax.axis_index("height")
+    core, high = lax.rem(h, 2), h // 2
+    low, rest = lax.rem(b, 2), b // 2
+    n_rest = n_batch // 2
+    first = core * low + (1 - core) * high
+    second = core * high + (1 - core) * low
+    core_peer = (b, h + 1 - 2 * core)
+    high_peer = (b, h + 2 - 4 * high)
+    low_peer = (b + 1 - 2 * low, h)
+    first_peer = (
+        core * low_peer[0] + (1 - core) * high_peer[0],
+        core * low_peer[1] + (1 - core) * high_peer[1],
+    )
+    second_peer = (
+        core * high_peer[0] + (1 - core) * low_peer[0],
+        core * high_peer[1] + (1 - core) * low_peer[1],
+    )
+
+    def rest_peer(k):
+        return (lax.rem(rest + k, n_rest) * 2 + low, h)
+
+    def load(c):
+        return pltpu.make_async_copy(local_ref.at[c], g.at[c], load_sem.at[c])
+
+    for c in range(N_CHUNKS):
+        load(c).start()
+    barrier = pltpu.get_barrier_semaphore()
+    for peer in (core_peer, high_peer, low_peer):
+        pl.semaphore_signal(barrier, inc=1, device_id=peer, device_id_type=MESH)
+
+    @pl.loop(1, n_rest)
+    def _(k):
+        pl.semaphore_signal(barrier, inc=1, device_id=rest_peer(k), device_id_type=MESH)
+
+    pl.semaphore_wait(barrier, 3 + n_rest - 1)
+
+    def copy(level, c, source, target, peer):
+        return pltpu.make_async_remote_copy(
+            src_ref=source,
+            dst_ref=target,
+            send_sem=send_sem.at[level, c],
+            recv_sem=recv_sem.at[level, c],
+            device_id=peer,
+            device_id_type=MESH,
+        )
+
+    def hop(level, c):
+        if level == 0:
+            return copy(0, c, g.at[c, 1 - core], r0.at[c], core_peer)
+        if level == 1:
+            return copy(1, c, g.at[c, core, 1 - first], r1.at[c], first_peer)
+        if level == 2:
+            return copy(2, c, g.at[c, core, first, 1 - second], r2.at[c], second_peer)
+        if level == 4:
+            mine = out_ref.at[c, core, high]
+            return copy(4, c, mine, mine, high_peer)
+        both = out_ref.at[c, core]
+        return copy(5, c, both, both, core_peer)
+
+    def add(target, source):
+        target[...] = (target[...].astype(jnp.float32) + source[...].astype(jnp.float32)).astype(
+            jnp.bfloat16
+        )
+
+    def others(c):
+        return r3.at[c, 0 : n_rest - 1]
+
+    @pl.loop(0, N_CHUNKS + 6)
+    def _(step):
+        @pl.when(step < N_CHUNKS)
+        def _():
+            load(step).wait()
+            hop(0, step).start()
+
+        c1 = step - 1
+
+        @pl.when(jnp.logical_and(c1 >= 0, c1 < N_CHUNKS))
+        def _():
+            hop(0, c1).wait_recv()
+
+            @pl.loop(0, 2)
+            def _(i):
+                @pl.loop(0, 2)
+                def _(j):
+                    @pl.loop(0, n_rest)
+                    def _(k):
+                        add(g.at[c1, core, i, j, k], r0.at[c1, i, j, k])
+
+            hop(1, c1).start()
+
+        c2 = step - 2
+
+        @pl.when(jnp.logical_and(c2 >= 0, c2 < N_CHUNKS))
+        def _():
+            hop(1, c2).wait_recv()
+
+            @pl.loop(0, 2)
+            def _(j):
+                @pl.loop(0, n_rest)
+                def _(k):
+                    add(g.at[c2, core, first, j, k], r1.at[c2, j, k])
+
+            hop(2, c2).start()
+
+        c3 = step - 3
+
+        @pl.when(jnp.logical_and(c3 >= 0, c3 < N_CHUNKS))
+        def _():
+            hop(2, c3).wait_recv()
+
+            @pl.loop(0, n_rest)
+            def _(k):
+                add(g.at[c3, core, first, second, k], r2.at[c3, k])
+
+            @pl.loop(1, n_rest)
+            def _(k):
+                copy(
+                    3,
+                    c3,
+                    g.at[c3, core, first, second, lax.rem(rest + k, n_rest)],
+                    r3.at[c3, n_rest - 1 - k],
+                    rest_peer(k),
+                ).start()
+
+        c4 = step - 4
+
+        @pl.when(jnp.logical_and(c4 >= 0, c4 < N_CHUNKS))
+        def _():
+            pltpu.make_async_copy(others(c4), others(c4), recv_sem.at[3, c4]).wait()
+            total = g[c4, core, first, second, rest].astype(jnp.float32)
+            for k in range(n_rest - 1):
+                total = total + r3[c4, k].astype(jnp.float32)
+            out_ref[c4, core, high] = total.astype(jnp.bfloat16)
+            hop(4, c4).start()
+
+        c5 = step - 5
+
+        @pl.when(jnp.logical_and(c5 >= 0, c5 < N_CHUNKS))
+        def _():
+            hop(4, c5).wait_recv()
+            hop(5, c5).start()
+
+        c6 = step - 6
+
+        @pl.when(jnp.logical_and(c6 >= 0, c6 < N_CHUNKS))
+        def _():
+            hop(5, c6).wait_recv()
+            for level in (0, 1, 2, 4, 5):
+                hop(level, c6).wait_send()
+            pltpu.make_async_copy(others(c6), others(c6), send_sem.at[3, c6]).wait()
+
+
+def by_piece(value, n_batch, n_height):
+    lead = value.shape[0] if value.ndim == 3 else 1
+    rows, columns = value.shape[-2:]
+    pieces = value.astype(jnp.bfloat16).reshape(
+        lead, n_batch // 2, 2, rows // n_batch, n_height // 2, 2, columns // (n_height * 128), 128
+    )
+    return jnp.transpose(pieces, (5, 4, 2, 1, 0, 3, 6, 7)).reshape(2, 2, 2, n_batch // 2, -1, 128)
+
+
+def from_piece(piece, shape, n_batch, n_height):
+    lead = shape[0] if len(shape) == 3 else 1
+    rows, columns = shape[-2:]
+    value = piece.reshape(2, 2, lead, rows // n_batch, columns // (n_height * 128), 128)
+    value = jnp.transpose(value, (2, 3, 1, 0, 4, 5)).astype(jnp.float32)
+    return value.reshape(shape[:-2] + (rows // n_batch, columns))
+
+
+def reduce_grads(grads):
+    n_batch, n_height = lax.axis_size("batch"), lax.axis_size("height")
+    shapes = [value.shape for value in grads]
+    pieces = [by_piece(value, n_batch, n_height) for value in grads]
+    counts = [piece.shape[4] for piece in pieces]
+    joined = jnp.concatenate(pieces, axis=4)
+    rows = joined.shape[4] // N_CHUNKS
+    n_rest = n_batch // 2
+    joined = jnp.stack([joined[0], jnp.swapaxes(joined[1], 0, 1)])
+    joined = joined.reshape(2, 2, 2, n_rest, N_CHUNKS, rows, 128)
+    joined = jnp.transpose(joined, (4, 0, 1, 2, 3, 5, 6))
+    summed = pl.pallas_call(
+        functools.partial(grads_kernel, n_batch),
+        out_shape=jax.ShapeDtypeStruct((N_CHUNKS, 2, 2, rows, 128), jnp.bfloat16),
+        in_specs=[pl.BlockSpec(memory_space=pl.ANY)],
+        out_specs=pl.BlockSpec(memory_space=pltpu.VMEM),
+        scratch_shapes=[
+            pltpu.VMEM((N_CHUNKS, 2, 2, 2, n_rest, rows, 128), jnp.bfloat16),
+            pltpu.VMEM((N_CHUNKS, 2, 2, n_rest, rows, 128), jnp.bfloat16),
+            pltpu.VMEM((N_CHUNKS, 2, n_rest, rows, 128), jnp.bfloat16),
+            pltpu.VMEM((N_CHUNKS, n_rest, rows, 128), jnp.bfloat16),
+            pltpu.VMEM((N_CHUNKS, n_rest - 1, rows, 128), jnp.bfloat16),
+            pltpu.SemaphoreType.DMA((N_CHUNKS,)),
+            pltpu.SemaphoreType.DMA((6, N_CHUNKS)),
+            pltpu.SemaphoreType.DMA((6, N_CHUNKS)),
+        ],
+        compiler_params=pltpu.CompilerParams(
+            collective_id=5, has_side_effects=True, vmem_limit_bytes=56 << 20
+        ),
+        name="reduce_grads",
+    )(joined)
+    summed = jnp.transpose(summed, (1, 2, 0, 3, 4)).reshape(2, 2, -1, 128)
+    result, start = [], 0
+    for shape, count in zip(shapes, counts):
+        result.append(from_piece(summed[:, :, start : start + count], shape, n_batch, n_height))
+        start += count
+    return result
 
 
 def passed_along(value, axis, steps):
@@ -637,24 +849,20 @@
             project_back(grad_side[picture_batches], shortcut_a)
         )
         backs.append(jnp.transpose(image_grad.astype(jnp.bfloat16), (2, 0, 1, 3)))
-    shards = (
-        lax.psum_scatter(reduce_a_local, "batch", scatter_dimension=0, tiled=True),
-        lax.psum_scatter(spatial_a_local, "batch", scatter_dimension=2, tiled=True),
-        lax.psum_scatter(expand_a_local, "batch", scatter_dimension=0, tiled=True),
-        lax.psum_scatter(shortcut_a_local, "batch", scatter_dimension=0, tiled=True),
-        lax.psum_scatter(reduce_b_local, "batch", scatter_dimension=0, tiled=True),
-        lax.psum_scatter(spatial_b_local, "batch", scatter_dimension=2, tiled=True),
-        lax.psum_scatter(expand_b_local, "batch", scatter_dimension=0, tiled=True),
-    )
-    shards = (
-        lax.psum(shards[0].astype(jnp.bfloat16), "height").astype(jnp.float32),
-        lax.psum(shards[1].astype(jnp.bfloat16), "height").astype(jnp.float32),
-        lax.psum(shards[2].astype(jnp.bfloat16), "height").astype(jnp.float32),
-        lax.psum(shards[3].astype(jnp.bfloat16), "height").astype(jnp.float32),
-        lax.psum(shards[4].astype(jnp.bfloat16), "height").astype(jnp.float32),
-        lax.psum(shards[5].astype(jnp.bfloat16), "height").astype(jnp.float32),
-        lax.psum(shards[6].astype(jnp.bfloat16), "height").astype(jnp.float32),
-    )
+    nine = (9,) + spatial_a_local.shape[2:]
+    shards = reduce_grads(
+        [
+            reduce_a_local,
+            spatial_a_local.reshape(nine),
+            expand_a_local,
+            shortcut_a_local,
+            reduce_b_local,
+            spatial_b_local.reshape(nine),
+            expand_b_local,
+        ]
+    )
+    for place in (1, 5):
+        shards[place] = shards[place].reshape((3, 3) + shards[place].shape[1:])
     gain_mid_grad = jnp.stack([sums_one[1], sums_two[1], sums_four[1], sums_five[1]])
     shift_mid_grad = jnp.stack([sums_one[0], sums_two[0], sums_four[0], sums_five[0]])
     gain_out_grad = jnp.stack([sums_three[1], sums_side[1], sums_six[1]])

time: 1820 us -> 1390 us (0.76)
  waiting for transfers between devices: 719 us -> 0.03 us
  local copies, waits for them, and re-layouts: 275 us -> 396 us
  Pallas kernels: 147 us -> 265 us
  matrix products: 275 us -> 334 us
    reduce_scatter x7 -> x0, waiting for transfers between devices: 685 us -> none  [the longest x1 164 us: per_device(): lax.psum_scatter(spatial_a_local, 'batch', scatter_dimension=2, tiled=True)]
    pallas_call x0 -> x1, Pallas kernels: none -> 119 us  [reduce_grads(): pl.pallas_call(functools.partial(grads_kernel, n_batch), out_shape=jax.Sh...]
    dot_general x69, matrix products: 62.5 us -> 138 us  [weight_term(): jnp.einsum('hwic,hwid->cd', values, grad_in, preferred_element_type=jnp.f...]
    reshape x0 -> x16, local copies, waits for them, and re-layouts: none -> 36.7 us  [the longest x8 31.6 us: by_piece(): value.astype(jnp.bfloat16)]
    psum x1, waiting for transfers between devices: 33.9 us -> 0.01 us  [per_device(): lax.psum(jnp.stack([jnp.sum(final[picture_batches], axis=(0, 1)) for pict...]
    convert_element_type x0 -> x4, local copies, waits for them, and re-layouts: none -> 27.3 us  [by_piece(): value.astype(jnp.bfloat16)]
    unnamed x752 -> x900, local copies, waits for them, and re-layouts: 48.7 us -> 69.6 us
    dot_general x69, matrix products: 130 us -> 112 us  [project_back(): jnp.einsum('hwid,cd->hwic', grad_in, weight, preferred_element_type=jnp.f...]
  transfers between devices with their start and end apart: 14 -> 7, of which waited for: 7 -> 0; matrix products, arithmetic and copies ran while one was open for 16% -> 18% of each run, Pallas kernels for 0% -> 0%
where the time goes in v2:
time: 1390 us; the launch traced here: 1370 us
  local copies, waits for them, and re-layouts  396 us (28%)
  other arithmetic  334 us (24%)
  matrix products  334 us (24%)
  Pallas kernels  265 us (19%)
  between operations  27.8 us (2%)
    pallas_call x12, Pallas kernels, sum_over_all(): pl.pallas_call(functools.partial(sum_kernel, n_batch, n_height), out_shap...  146 us
    scatter-add x27, other arithmetic, spatial_back(): padded_grad = padded_grad.at[row_tap:row_tap + stride * (out_rows - 1) +...  141 us
    dot_general x69, matrix products, weight_term(): jnp.einsum('hwic,hwid->cd', values, grad_in, preferred_element_type=jnp.f...  138 us
    pallas_call x1, Pallas kernels, reduce_grads(): pl.pallas_call(functools.partial(grads_kernel, n_batch), out_shape=jax.Sh...  119 us
    dot_general x69, matrix products, project_back(): jnp.einsum('hwid,cd->hwic', grad_in, weight, preferred_element_type=jnp.f...  112 us
    slice x18, local copies, waits for them, and re-layouts, tap_window(): padded[row_tap:row_tap + stride * (out_rows - 1) + 1:stride, col_tap:col_...  84.6 us
    dot_general x69, matrix products, project(): jnp.einsum('hwic,cd->hwid', values, weight, preferred_element_type=jnp.fl...  83.3 us
    slice x3, local copies, waits for them, and re-layouts, per_device(): entering_photos[picture_batches][::2, ::2]  83.3 us
  transfers between devices with their start and end apart: 7, of which 0 were waited for; matrix products, arithmetic and copies ran while one was open for 18% of the time, Pallas kernels for 0%

profile of v2, /device:TPU:0, one launch (start us, length us, event | category | flops | bytes accessed | tf_op | source)
XLA Modules:
  0.0 1366.9 jit_solution(8763388052814748271)
XLA Ops:
  13.1 8.4 fusion.580
  27.2 12.7 sum_over_all.12
  58.8 42.5 %slice.1792 = bf16[4,9,12,1024]{3,0,1,2:T(4,128)(2,1)S(1)} slice(bf16[8,18,12,1024]{3,0,1,2:T(8,128)(2,1)} %copy-done.55), slice={[0:8:2], [0:18:2], [0:12:1], [0:1024:1]} | slice | bytes 1769472 | tf_op jit(solution)/shard_map/slice | solution.py:518
  101.2 18.6 %slice.1791 = bf16[3,7,12,1024]{3,1,0,2:T(8,128)(2,1)} slice(bf16[6,14,12,1024]{3,1,0,2:T(8,128)(2,1)} %copy-done.88), slice={[0:6:2], [0:14:2], [0:12:1], [0:1024:1]} | slice | bytes 1032192 | tf_op jit(solution)/shard_map/slice | solution.py:518
  119.8 22.2 %slice.1790 = bf16[2,5,12,1024]{3,0,1,2:T(2,128)(2,1)S(1)} slice(bf16[4,10,12,1024]{3,0,1,2:T(4,128)(2,1)} %copy-done.144), slice={[0:4:2], [0:10:2], [0:12:1], [0:1024:1]} | slice | bytes 491520 | tf_op jit(solution)/shard_map/slice | solution.py:518
  283.9 10.6 sum_over_all.13
  307.1 13.4 sum_over_all.14
  336.2 11.8 sum_over_all.15
  406.1 12.8 sum_over_all.16
  431.0 11.2 sum_over_all.17
  459.6 12.5 sum_over_all.18
  489.6 10.8 sum_over_all.19
  647.3 13.1 sum_over_all.20
  671.6 9.2 multiply_reduce_fusion.2
  684.4 13.5 sum_over_all.21
  721.0 11.8 sum_over_all.22
  857.4 8.0 scatter_fusion.21
  872.7 8.1 scatter_fusion.23
  888.1 8.2 scatter_fusion.25
  1019.3 8.4 fusion.4
  1107.7 11.5 sum_over_all.23
  1156.4 8.3 fusion.610
  1172.1 119.0 %reduce_grads.1 = bf16[10,2,2,256,128]{4,3,2,1,0:T(8,128)(2,1)} custom-call(bf16[10,2,2,2,4,256,128]{6,5,4,3,2,1,0:T(8,128)(2,1)} %maximum_bitcast_fusion.local_ref), custom_call_target="tpu_custom_call" | custom-call | tf_op jit(solution)/shard_map/reduce_grads/pallas_call | solution.py:259
  1321.5 10.3 scatter_fusion.29
  (1502 shorter events, 922.2 us)
Async XLA Ops:
  7.2 319.4 %copy-start = (bf16[2048,512]{1,0:T(8,128)(2,1)S(1)}, bf16[2048,512]{1,0:T(8,128)(2,1)}, u32[]{:S(2)}) copy-start(bf16[2048,512]{1,0:T(8,128)(2,1)} %param.86) | copy-start | bytes 6291460
  7.2 626.6 %all-reduce.11.cloned.1.call-start = ((), (), s32[]{:S(2)}) async-start(), calls=%async_computation | async-start | bytes 393216 | tf_op jit(solution)/shard_map/psum | solution.py:600
  9.4 38.5 %copy-start.385 = (f32[8]{0:T(128)}, f32[8]{0:T(128)S(1)}, u32[]{:S(2)}) copy-start(f32[8]{0:T(128)S(1)} %get-tuple-element.769) | copy-start | bytes 100
  10.0 35.1 %copy-start.379 = (f32[6]{0:T(128)}, f32[6]{0:T(128)S(1)}, u32[]{:S(2)}) copy-start(f32[6]{0:T(128)S(1)} %get-tuple-element.773) | copy-start | bytes 76
  10.6 32.4 %copy-start.381 = (f32[4]{0:T(128)}, f32[4]{0:T(128)S(1)}, u32[]{:S(2)}) copy-start(f32[4]{0:T(128)S(1)} %get-tuple-element.771) | copy-start | bytes 52
  43.1 307.3 %copy-start.310 = (f32[1,512]{1,0:T(1,128)}, f32[1,512]{1,0:T(1,128)S(1)}, u32[]{:S(2)}) copy-start(f32[1,512]{1,0:T(1,128)S(1)} %get-tuple-element.631) | copy-start | bytes 6148
  55.1 114.3 %collective-permute-start = (bf16[42,12,512]{2,0,1:T(8,128)(2,1)}, bf16[42,12,512]{2,0,1:T(8,128)(2,1)}, u32[]{:S(2)}, u32[]{:S(2)}) collective-permute-start(bf16[42,12,512]{2,0,1:T(8,128)(2,1)} %pad_maximum_fusion.1), channel_id=1, source_target_pairs={{0,1},{1,2},{2,3},{4,5},{5,6},{6,7},{8,9},{9,10},{10,11},{12,13},{... | collective-permute-start | bytes 1548296 | tf_op jit(solution)/shard_map/ppermute | solution.py:290
  58.2 474.0 %copy-start.321 = (f32[3]{0:T(128)}, f32[3]{0:T(128)S(1)}, u32[]{:S(2)}) copy-start(f32[3]{0:T(128)S(1)} %compare_convert_fusion.1) | copy-start | bytes 40
  58.8 477.0 %copy-start.324 = (f32[2]{0:T(128)}, f32[2]{0:T(128)S(1)}, u32[]{:S(2)}) copy-start(f32[2]{0:T(128)S(1)} %compare_convert_fusion.2) | copy-start | bytes 28
  101.2 50.3 %copy-start.245 = (bf16[4,9,12,1024]{3,0,1,2:T(4,128)(2,1)}, bf16[4,9,12,1024]{3,0,1,2:T(4,128)(2,1)S(1)}, u32[]{:S(2)}) copy-start(bf16[4,9,12,1024]{3,0,1,2:T(4,128)(2,1)S(1)} %slice.1792) | copy-start | bytes 2654212
  157.1 172.7 %copy-start.294 = (f32[1,2048]{1,0:T(1,128)}, f32[1,2048]{1,0:T(1,128)S(1)}, u32[]{:S(2)}) copy-start(f32[1,2048]{1,0:T(1,128)S(1)} %get-tuple-element.614) | copy-start | bytes 24580
  157.1 172.7 %copy-start.296 = (f32[1,2048]{1,0:T(1,128)}, f32[1,2048]{1,0:T(1,128)S(1)}, u32[]{:S(2)}) copy-start(f32[1,2048]{1,0:T(1,128)S(1)} %get-tuple-element.615) | copy-start | bytes 24580
  164.8 439.3 %copy-start.317 = (f32[4]{0:T(128)}, f32[4]{0:T(128)S(1)}, u32[]{:S(2)}) copy-start(f32[4]{0:T(128)S(1)} %compare_convert_fusion) | copy-start | bytes 52
  240.2 30.5 %slice-start.4 = ((s8[4718592]{0:T(1024)(128)(4,1)}), s8[524288]{0:T(1024)(128)(4,1)S(1)}, s32[]{:S(2)}) async-start(s8[4718592]{0:T(1024)(128)(4,1)} %bitcast.1519), calls=%async_computation.5 | async-start | bytes 1048576
  350.7 29.9 %copy-start.365 = (s32[3,7,1]{1,0,2:T(4,128)S(1)}, s32[3,7,1]{1,0,2:T(4,128)}, u32[]{:S(2)}) copy-start(s32[3,7,1]{1,0,2:T(4,128)} %or_select_fusion.1) | copy-start | bytes 256
  350.7 39.1 %slice-start = ((s8[4718592]{0:T(1024)(128)(4,1)}), s8[524288]{0:T(1024)(128)(4,1)S(1)}, s32[]{:S(2)}) async-start(s8[4718592]{0:T(1024)(128)(4,1)} %bitcast.1515), calls=%async_computation.1 | async-start | bytes 1048576
  354.3 27.5 %collective-permute-start.1 = (bf16[1,21,12,512]{3,2,1,0:T(8,128)(2,1)}, bf16[1,21,12,512]{3,2,1,0:T(8,128)(2,1)}, u32[]{:S(2)}, u32[]{:S(2)}) collective-permute-start(bf16[1,21,12,512]{3,2,1,0:T(8,128)(2,1)} %get-tuple-element.588), channel_id=1, source_target_pairs={{0,1},{1,2},{2,3},{4,5},{5,6},{6,7},{8,9},{9,10},{10,11},{12,13},{... | collective-permute-start | bytes 774152 | tf_op jit(solution)/shard_map/ppermute | solution.py:300
  357.1 25.8 %collective-permute-start.2 = (bf16[1,21,12,512]{3,2,1,0:T(8,128)(2,1)}, bf16[1,21,12,512]{3,2,1,0:T(8,128)(2,1)}, u32[]{:S(2)}, u32[]{:S(2)}) collective-permute-start(bf16[1,21,12,512]{3,2,1,0:T(8,128)(2,1)} %get-tuple-element.587), channel_id=1, source_target_pairs={{1,0},{2,1},{3,2},{5,4},{6,5},{7,6},{9,8},{10,9},{11,10},{13,12},{... | collective-permute-start | bytes 774152 | tf_op jit(solution)/shard_map/ppermute | solution.py:301
  512.7 65.9 %copy-start.47 = (bf16[1,7,12,512]{3,2,1,0:T(8,128)(2,1)}, bf16[1,7,12,512]{3,2,1,0:T(8,128)(2,1)S(1)}, u32[]{:S(2)}) copy-start(bf16[1,7,12,512]{3,2,1,0:T(8,128)(2,1)S(1)} %slice.2676) | copy-start | bytes 258052
  522.3 56.3 %copy-start.39 = (bf16[1,9,12,512]{3,2,1,0:T(8,128)(2,1)}, bf16[1,9,12,512]{3,2,1,0:T(8,128)(2,1)S(1)}, u32[]{:S(2)}) copy-start(bf16[1,9,12,512]{3,2,1,0:T(8,128)(2,1)S(1)} %slice.2675) | copy-start | bytes 331780
  529.3 49.3 %copy-start.67 = (bf16[1,5,12,512]{3,2,1,0:T(8,128)(2,1)}, bf16[1,5,12,512]{3,2,1,0:T(8,128)(2,1)S(1)}, u32[]{:S(2)}) copy-start(bf16[1,5,12,512]{3,2,1,0:T(8,128)(2,1)S(1)} %slice.2677) | copy-start | bytes 184324
  579.7 56.1 %collective-permute-start.3 = (bf16[1,21,12,512]{3,2,1,0:T(8,128)(2,1)}, bf16[1,21,12,512]{3,2,1,0:T(8,128)(2,1)S(1)}, u32[]{:S(2)}, u32[]{:S(2)}) collective-permute-start(bf16[1,21,12,512]{3,2,1,0:T(8,128)(2,1)} %get-tuple-element.585), channel_id=1, source_target_pairs={{0,1},{1,2},{2,3},{4,5},{5,6},{6,7},{8,9},{9,10},{10,11},{12,13},{... | collective-permute-start | bytes 774152 | tf_op jit(solution)/shard_map/ppermute | solution.py:300
  581.0 54.7 %collective-permute-start.4 = (bf16[1,21,12,512]{3,2,1,0:T(8,128)(2,1)}, bf16[1,21,12,512]{3,2,1,0:T(8,128)(2,1)S(1)}, u32[]{:S(2)}, u32[]{:S(2)}) collective-permute-start(bf16[1,21,12,512]{3,2,1,0:T(8,128)(2,1)} %get-tuple-element.586), channel_id=1, source_target_pairs={{1,0},{2,1},{3,2},{5,4},{6,5},{7,6},{9,8},{10,9},{11,10},{13,12},{... | collective-permute-start | bytes 774152 | tf_op jit(solution)/shard_map/ppermute | solution.py:301
  1001.0 93.4 %collective-permute-start.5 = (bf16[42,12,512]{2,0,1:T(8,128)(2,1)}, bf16[42,12,512]{2,0,1:T(8,128)(2,1)}, u32[]{:S(2)}, u32[]{:S(2)}) collective-permute-start(bf16[42,12,512]{2,0,1:T(8,128)(2,1)} %copy.321), channel_id=1, source_target_pairs={{1,0},{2,1},{3,2},{5,4},{6,5},{7,6},{9,8},{10,9},{11,10},{13,12},{... | collective-permute-start | bytes 1548296 | tf_op jit(solution)/shard_map/ppermute | solution.py:290
  (426 other events, 2802.6 us)
Sparse Core Ops, SparseCore 0:
  583.2 34.7 all-reduce.10

commit v3 on v2

v3 whole, which is shorter than its diff:
```python
import functools

import jax
import jax.numpy as jnp
from jax import lax
from jax.experimental import pallas as pl
from jax.experimental.pallas import tpu as pltpu
from jax.sharding import PartitionSpec as P

epsilon = 1e-05
MESH = pl.DeviceIdType.MESH
N_CHUNKS = 10


def grads_kernel(n_batch, local_ref, out_ref, g, r0, r1, r2, r3, load_sem, send_sem, recv_sem):
    b, h = lax.axis_index("batch"), lax.axis_index("height")
    core, high = lax.rem(h, 2), h // 2
    low, rest = lax.rem(b, 2), b // 2
    n_rest = n_batch // 2
    first = core * low + (1 - core) * high
    second = core * high + (1 - core) * low
    core_peer = (b, h + 1 - 2 * core)
    high_peer = (b, h + 2 - 4 * high)
    low_peer = (b + 1 - 2 * low, h)
    first_peer = (
        core * low_peer[0] + (1 - core) * high_peer[0],
        core * low_peer[1] + (1 - core) * high_peer[1],
    )
    second_peer = (
        core * high_peer[0] + (1 - core) * low_peer[0],
        core * high_peer[1] + (1 - core) * low_peer[1],
    )

    def rest_peer(k):
        return (lax.rem(rest + k, n_rest) * 2 + low, h)

    def load(c):
        return pltpu.make_async_copy(local_ref.at[c], g.at[c], load_sem.at[c])

    for c in range(N_CHUNKS):
        load(c).start()
    barrier = pltpu.get_barrier_semaphore()
    for peer in (core_peer, high_peer, low_peer):
        pl.semaphore_signal(barrier, inc=1, device_id=peer, device_id_type=MESH)

    @pl.loop(1, n_rest)
    def _(k):
        pl.semaphore_signal(barrier, inc=1, device_id=rest_peer(k), device_id_type=MESH)

    pl.semaphore_wait(barrier, 3 + n_rest - 1)

    def copy(level, c, source, target, peer):
        return pltpu.make_async_remote_copy(
            src_ref=source,
            dst_ref=target,
            send_sem=send_sem.at[level, c],
            recv_sem=recv_sem.at[level, c],
            device_id=peer,
            device_id_type=MESH,
        )

    def hop(level, c):
        if level == 0:
            return copy(0, c, g.at[c, 1 - core], r0.at[c], core_peer)
        if level == 1:
            return copy(1, c, g.at[c, core, 1 - first], r1.at[c], first_peer)
        if level == 2:
            return copy(2, c, g.at[c, core, first, 1 - second], r2.at[c], second_peer)
        if level == 4:
            mine = out_ref.at[c, core, high]
            return copy(4, c, mine, mine, high_peer)
        both = out_ref.at[c, core]
        return copy(5, c, both, both, core_peer)

    def add(target, source):
        target[...] = (target[...].astype(jnp.float32) + source[...].astype(jnp.float32)).astype(
            jnp.bfloat16
        )

    def others(c):
        return r3.at[c, 0 : n_rest - 1]

    @pl.loop(0, N_CHUNKS + 6)
    def _(step):
        @pl.when(step < N_CHUNKS)
        def _():
            load(step).wait()
            hop(0, step).start()

        c1 = step - 1

        @pl.when(jnp.logical_and(c1 >= 0, c1 < N_CHUNKS))
        def _():
            hop(0, c1).wait_recv()

            @pl.loop(0, 2)
            def _(i):
                @pl.loop(0, 2)
                def _(j):
                    @pl.loop(0, n_rest)
                    def _(k):
                        add(g.at[c1, core, i, j, k], r0.at[c1, i, j, k])

            hop(1, c1).start()

        c2 = step - 2

        @pl.when(jnp.logical_and(c2 >= 0, c2 < N_CHUNKS))
        def _():
            hop(1, c2).wait_recv()

            @pl.loop(0, 2)
            def _(j):
                @pl.loop(0, n_rest)
                def _(k):
                    add(g.at[c2, core, first, j, k], r1.at[c2, j, k])

            hop(2, c2).start()

        c3 = step - 3

        @pl.when(jnp.logical_and(c3 >= 0, c3 < N_CHUNKS))
        def _():
            hop(2, c3).wait_recv()

            @pl.loop(0, n_rest)
            def _(k):
                add(g.at[c3, core, first, second, k], r2.at[c3, k])

            @pl.loop(1, n_rest)
            def _(k):
                copy(
                    3,
                    c3,
                    g.at[c3, core, first, second, lax.rem(rest + k, n_rest)],
                    r3.at[c3, n_rest - 1 - k],
                    rest_peer(k),
                ).start()

        c4 = step - 4

        @pl.when(jnp.logical_and(c4 >= 0, c4 < N_CHUNKS))
        def _():
            pltpu.make_async_copy(others(c4), others(c4), recv_sem.at[3, c4]).wait()
            total = g[c4, core, first, second, rest].astype(jnp.float32)
            for k in range(n_rest - 1):
                total = total + r3[c4, k].astype(jnp.float32)
            out_ref[c4, core, high] = total.astype(jnp.bfloat16)
            hop(4, c4).start()

        c5 = step - 5

        @pl.when(jnp.logical_and(c5 >= 0, c5 < N_CHUNKS))
        def _():
            hop(4, c5).wait_recv()
            hop(5, c5).start()

        c6 = step - 6

        @pl.when(jnp.logical_and(c6 >= 0, c6 < N_CHUNKS))
        def _():
            hop(5, c6).wait_recv()
            for level in (0, 1, 2, 4, 5):
                hop(level, c6).wait_send()
            pltpu.make_async_copy(others(c6), others(c6), send_sem.at[3, c6]).wait()


def by_piece(value, n_batch, n_height):
    lead = value.shape[0] if value.ndim == 3 else 1
    rows, columns = value.shape[-2:]
    pieces = value.astype(jnp.bfloat16).reshape(
        lead, n_batch // 2, 2, rows // n_batch, n_height // 2, 2, columns // (n_height * 128), 128
    )
    return jnp.transpose(pieces, (5, 4, 2, 1, 0, 3, 6, 7)).reshape(2, 2, 2, n_batch // 2, -1, 128)


def from_piece(piece, shape, n_batch, n_height):
    lead = shape[0] if len(shape) == 3 else 1
    rows, columns = shape[-2:]
    value = piece.reshape(2, 2, lead, rows // n_batch, columns // (n_height * 128), 128)
    value = jnp.transpose(value, (2, 3, 1, 0, 4, 5)).astype(jnp.float32)
    return value.reshape(shape[:-2] + (rows // n_batch, columns))


def reduce_grads(grads):
    n_batch, n_height = lax.axis_size("batch"), lax.axis_size("height")
    shapes = [value.shape for value in grads]
    pieces = [by_piece(value, n_batch, n_height) for value in grads]
    counts = [piece.shape[4] for piece in pieces]
    joined = jnp.concatenate(pieces, axis=4)
    rows = joined.shape[4] // N_CHUNKS
    n_rest = n_batch // 2
    joined = jnp.stack([joined[0], jnp.swapaxes(joined[1], 0, 1)])
    joined = joined.reshape(2, 2, 2, n_rest, N_CHUNKS, rows, 128)
    joined = jnp.transpose(joined, (4, 0, 1, 2, 3, 5, 6))
    summed = pl.pallas_call(
        functools.partial(grads_kernel, n_batch),
        out_shape=jax.ShapeDtypeStruct((N_CHUNKS, 2, 2, rows, 128), jnp.bfloat16),
        in_specs=[pl.BlockSpec(memory_space=pl.ANY)],
        out_specs=pl.BlockSpec(memory_space=pltpu.VMEM),
        scratch_shapes=[
            pltpu.VMEM((N_CHUNKS, 2, 2, 2, n_rest, rows, 128), jnp.bfloat16),
            pltpu.VMEM((N_CHUNKS, 2, 2, n_rest, rows, 128), jnp.bfloat16),
            pltpu.VMEM((N_CHUNKS, 2, n_rest, rows, 128), jnp.bfloat16),
            pltpu.VMEM((N_CHUNKS, n_rest, rows, 128), jnp.bfloat16),
            pltpu.VMEM((N_CHUNKS, n_rest - 1, rows, 128), jnp.bfloat16),
            pltpu.SemaphoreType.DMA((N_CHUNKS,)),
            pltpu.SemaphoreType.DMA((6, N_CHUNKS)),
            pltpu.SemaphoreType.DMA((6, N_CHUNKS)),
        ],
        compiler_params=pltpu.CompilerParams(
            collective_id=5, has_side_effects=True, vmem_limit_bytes=56 << 20
        ),
        name="reduce_grads",
    )(joined)
    summed = jnp.transpose(summed, (1, 2, 0, 3, 4)).reshape(2, 2, -1, 128)
    result, start = [], 0
    for shape, count in zip(shapes, counts):
        result.append(from_piece(summed[:, :, start : start + count], shape, n_batch, n_height))
        start += count
    return result


WIDE = 512
ROWS = 16
STEP = 64


def sigmoid(values):
    return 0.5 * jnp.tanh(0.5 * values) + 0.5


def up32(values):
    return values.astype(jnp.float32)


def low(values):
    return values.astype(jnp.bfloat16)


def times(left, right):
    return jnp.dot(left, right, preferred_element_type=jnp.float32)


def times_t(left, right):
    return lax.dot_general(
        left, right, (((1,), (1,)), ((), ())), preferred_element_type=jnp.float32
    )


def t_times(left, right):
    return lax.dot_general(
        left, right, (((0,), (0,)), ((), ())), preferred_element_type=jnp.float32
    )


def fold(values):
    return jnp.sum(values.reshape(-1, 8, values.shape[-1]), axis=0)


def one_row(values):
    return jnp.sum(values, axis=0, keepdims=True)


def wide_mask(mask):
    return jnp.concatenate([mask] * (WIDE // 128), axis=1)


def grids(heights, widths):
    counts = [k * (o + 1) for k, o in zip(heights, widths)]
    starts = [sum(counts[:g]) for g in range(3)]
    top_sizes = [(k + 1) * (o + 1) + 1 for k, o in zip(heights, widths)]
    top_starts = [sum(top_sizes[:g]) for g in range(3)]
    both_sizes = [(k + 2) * (o + 1) + 2 for k, o in zip(heights, widths)]
    both_starts = [sum(both_sizes[:g]) for g in range(3)]
    halo_starts = [sum(widths[:g]) for g in range(3)]
    return counts, starts, sum(top_sizes), top_starts, sum(both_sizes), both_starts, halo_starts


def main_kernel(
    n_batch, n_height, heights, widths, total_in, total_out,
    x, reduce_a, spatial_a, expand_a, shortcut_a, reduce_b, spatial_b, expand_b,
    edge_ref, mask_ref, gain_mid, shift_mid, gain_out, shift_out, up_ref,
    pooled, dx, g_reduce_a, g_spatial_a, g_expand_a, g_shortcut_a, g_reduce_b, g_spatial_b,
    g_expand_b, mid_sums, out_sums, h1_kept, a1_kept,
    big_b, big_a, h3, side, mb, h2, a2, h4, h5, a5, a4p, dhp, acc, wp, wq, w2,
    halo_a, halo_up, halo_down, halo_in, staged, pool_slots,
    thin_h, thin_b, wide_h, wide_b, stat_mid, stat_out,
    w_sem, x_sem, g_sem, dx_sem, spill_sem, ar_send, ar_recv, halo_send, halo_recv, pool_sem,
):
    b, h = lax.axis_index("batch"), lax.axis_index("height")
    counts, starts, top_total, top_starts, both_total, both_starts, halo_starts = grids(
        heights, widths
    )
    total = sum(counts) * ROWS
    half = total // 2
    groups = range(3)
    h1, dz, h6 = big_b, big_b, big_a

    def rows_at(start, count):
        return pl.ds(pl.multiple_of(start * ROWS, ROWS), count * ROWS)

    def steps(index):
        return pl.ds(pl.multiple_of(index * STEP, STEP), STEP)

    def fetch(source, target, sem):
        pltpu.make_async_copy(source, target, sem).start()

    def arrived(target, sem):
        pltpu.make_async_copy(target, target, sem).wait()

    def columns(k):
        return pl.ds(k * WIDE, WIDE)

    def fetch_columns(weight, target, first, sem):
        for n in range(4):
            fetch(weight.at[:, columns(n)], target.at[first + n], sem)

    def fetch_shortcut():
        for n in range(4):
            for k in range(2):
                fetch(shortcut_a.at[columns(k), columns(n)], wq.at[2 * n + k], w_sem.at[1])

    for k in range(2):
        fetch(x.at[:, :, columns(k)], (h3, mb)[k], x_sem.at[k])
    for k in range(2):
        fetch(reduce_a.at[columns(k)], w2.at[k], w_sem.at[3])
    fetch_shortcut()
    fetch(spatial_a, wp, w_sem.at[0])

    halo_down[...] = jnp.zeros_like(halo_down)
    halo_up[...] = jnp.zeros_like(halo_up)
    halo_in[...] = jnp.zeros_like(halo_in)

    @pl.loop(0, both_total // 2)
    def _(i):
        rows = rows_at(i * 2, 2)
        a4p[rows] = jnp.zeros((2 * ROWS, WIDE), jnp.bfloat16)
        dhp[rows] = jnp.zeros((2 * ROWS, WIDE), jnp.bfloat16)

    for g in groups:
        count = widths[g] + 2
        for p in range(4):
            big_a[p, top_starts[g] * ROWS : (top_starts[g] + count) * ROWS] = jnp.zeros(
                (count * ROWS, WIDE), jnp.bfloat16
            )

    barrier = pltpu.get_barrier_semaphore()
    for k in range(1, n_height):
        pl.semaphore_signal(
            barrier, inc=1, device_id=(b, lax.rem(h + k, n_height)), device_id_type=MESH
        )

    @pl.loop(1, n_batch)
    def _(k):
        pl.semaphore_signal(
            barrier, inc=1, device_id=(lax.rem(b + k, n_batch), h), device_id_type=MESH
        )

    pl.semaphore_wait(barrier, n_height + n_batch - 2)

    turn = {"thin": 0, "wide": 0}

    def ar_spread(slots, me, count, peer, level, slot, sem):
        @pl.loop(1, count)
        def _(k):
            pltpu.make_async_remote_copy(
                src_ref=slots.at[slot, me],
                dst_ref=slots.at[slot, me],
                send_sem=ar_send.at[sem, level, slot],
                recv_sem=ar_recv.at[sem, level, slot],
                device_id=peer(lax.rem(me + k, count)),
                device_id_type=MESH,
            ).start()

    def ar_wait(slots, count, level, slot, sem, sems):
        others = slots.at[slot, 0 : count - 1]
        pltpu.make_async_copy(others, others, sems.at[sem, level, slot]).wait()

    def sums_start(kind, vectors):
        slot = turn[kind] % 2
        turn[kind] += 1
        if kind == "thin":
            first, second, sem = thin_h, thin_b, 0
            for v, vector in enumerate(vectors):
                for j in range(4):
                    first[slot, h, 4 * v + j : 4 * v + j + 1, :] = vector[
                        :, 128 * j : 128 * (j + 1)
                    ]
        else:
            first, second, sem = wide_h, wide_b, 1
            first[slot, h] = stat_out[...]
        ar_spread(first, h, n_height, lambda p: (b, p), 0, slot, sem)
        return first, second, sem, slot

    def sums_middle(state):
        first, second, sem, slot = state
        ar_wait(first, n_height, 0, slot, sem, ar_recv)
        second[slot, b] = jnp.sum(first[slot], axis=0)
        ar_spread(second, b, n_batch, lambda p: (p, h), 1, slot, sem)

    def sums_end(state):
        first, second, sem, slot = state
        ar_wait(second, n_batch, 1, slot, sem, ar_recv)
        summed = jnp.sum(second[slot], axis=0)
        ar_wait(first, n_height, 0, slot, sem, ar_send)
        ar_wait(second, n_batch, 1, slot, sem, ar_send)
        if sem == 0:
            return [
                jnp.concatenate([summed[4 * v + j : 4 * v + j + 1] for j in range(4)], axis=1)
                for v in range(2)
            ]
        stat_out[...] = summed
        return None

    def keep_stats(kept, index, sums, number, gain, shift):
        centre = sums[0] * (1.0 / number)
        root = lax.rsqrt(sums[1] * (1.0 / number) - centre * centre + epsilon)
        scale = root * gain
        kept[index, 0:1] = centre
        kept[index, 1:2] = root
        kept[index, 2:3] = scale
        kept[index, 3:4] = shift - centre * scale
        kept[index, 4:5] = -centre * root

    def back_factors(kept, index, sums, number, gain):
        centre, root = kept[index, 0:1], kept[index, 1:2]
        main = gain * root
        slope = -main * root * sums[1] * (1.0 / number)
        return main, slope, -main * sums[0] * (1.0 / number) - slope * centre

    def halo_copy(source, target, sem, peer):
        return pltpu.make_async_remote_copy(
            src_ref=source,
            dst_ref=target,
            send_sem=halo_send.at[sem],
            recv_sem=halo_recv.at[sem],
            device_id=(b, peer),
            device_id_type=MESH,
        )

    def halo_rows(g):
        return slice(halo_starts[g] * ROWS, (halo_starts[g] + widths[g]) * ROWS)

    def top_row(padded, start, g):
        return padded.at[pl.ds((start + 1) * ROWS, widths[g] * ROWS)]

    def send_down(buffer, padded, sem):
        @pl.when(h < n_height - 1)
        def _():
            for g in groups:
                halo_copy(
                    buffer.at[halo_rows(g)], top_row(padded, both_starts[g], g), sem, h + 1
                ).start()

    def send_up(buffer, sem):
        @pl.when(h > 0)
        def _():
            halo_copy(buffer, halo_in, sem, h - 1).start()

    def halo_wait(buffer, sems, sem, condition):
        @pl.when(condition)
        def _():
            arrived(buffer, sems.at[sem])

    def place_below(padded):
        for g in groups:
            stride = widths[g] + 1
            for y in range(1, heights[g] + 1):
                is_edge = edge(g, y - 1)

                @pl.loop(0, widths[g])
                def _(col):
                    rows = rows_at(both_starts[g] + 1 + (y + 1) * stride + col, 1)
                    value = up32(halo_in[rows_at(halo_starts[g] + col, 1)]) * is_edge
                    if y < heights[g]:
                        value = value + up32(padded[rows])
                    padded[rows] = low(value)

    def edge(g, y):
        return wide_mask(edge_ref[g, y, 0:1])

    def first_row(source, g, row=0):
        start = (starts[g] + row * (widths[g] + 1)) * ROWS
        return up32(source[start : start + widths[g] * ROWS])

    def last_row(source, g):
        value = first_row(source, g) * edge(g, 0)
        for y in range(1, heights[g]):
            value = value + first_row(source, g, y) * edge(g, y)
        return value

    done = [0]

    def store_tile(index, value, target):
        slot = lax.rem(index, 2)

        @pl.when(index >= 2)
        def _():
            arrived(staged.at[slot], g_sem.at[slot])

        staged[slot] = low(value)
        fetch(staged.at[slot], target, g_sem.at[slot])

    def store_tiles(count, value_of, target_of):
        first = done[0]
        done[0] += count

        @pl.loop(0, count)
        def _(t):
            store_tile(first + t, value_of(t), target_of(t))

    def wide_rows(reference, t):
        return reference.at[pl.ds(pl.multiple_of(t * WIDE, WIDE), WIDE)]

    def wide_columns(reference, t):
        return reference.at[:, pl.ds(pl.multiple_of(t * WIDE, WIDE), WIDE)]

    zero8 = jnp.zeros((8, WIDE), jnp.float32)

    arrived(w2, w_sem.at[3])
    for k in range(2):
        arrived((h3, mb)[k], x_sem.at[k])

    def first_reduction(i, carry):
        p = i // 2
        rows = pl.ds(pl.multiple_of(lax.rem(i, 2) * half, ROWS), half)
        value = times(h3[p, rows], w2[0]) + times(mb[p, rows], w2[1])
        h1[p, rows] = low(value)
        return carry[0] + fold(value), carry[1] + fold(value * value)

    sums = lax.fori_loop(0, 8, first_reduction, (zero8, zero8))
    state = sums_start("thin", [one_row(v) for v in sums])

    arrived(wq, w_sem.at[1])

    def shortcut_product(n, carry):
        value = times(h3[0], wq[2 * n]) + times(mb[0], wq[2 * n + 1])
        side[n] = low(value)
        stat_out[pl.ds(8 + n, 1)] = one_row(fold(value))
        stat_out[pl.ds(12 + n, 1)] = one_row(fold(value * value))
        return carry

    lax.fori_loop(0, 2, shortcut_product, 0)
    sums_middle(state)
    lax.fori_loop(2, 4, shortcut_product, 0)
    fetch_columns(expand_a, wq, 0, w_sem.at[1])
    for k in range(4):
        fetch(reduce_b.at[columns(k)], wq.at[4 + k], w_sem.at[2])
    sums = sums_end(state)
    keep_stats(stat_mid, 0, sums, total_in, gain_mid[0:1], shift_mid[0:1])

    scale, offset = stat_mid[0, 2:3], stat_mid[0, 3:4]
    for column in range(2):
        for g in groups:
            pre = last_row(h1.at[2 + column], g) * scale + offset
            mask = wide_mask(mask_ref[starts[g] * ROWS : (starts[g] + widths[g]) * ROWS])
            halo_a[column, halo_rows(g)] = low(pre * sigmoid(pre) * mask)

    @pl.when(h < n_height - 1)
    def _():
        for column in range(2):
            for g in groups:
                halo_copy(
                    halo_a.at[column, halo_rows(g)],
                    top_row(big_a.at[2 + column], top_starts[g], g),
                    0,
                    h + 1,
                ).start()

    for g in groups:
        per = counts[g] * ROWS // STEP
        base = (top_starts[g] + 1 + widths[g] + 1) * ROWS

        @pl.loop(0, 4)
        def _(p):
            @pl.loop(0, per)
            def _(i):
                rows = pl.ds(pl.multiple_of(starts[g] * ROWS + i * STEP, ROWS), STEP)
                pre = up32(h1[p, rows]) * scale + offset
                value = pre * sigmoid(pre) * wide_mask(mask_ref[rows])
                big_a[p, pl.ds(pl.multiple_of(base + i * STEP, ROWS), STEP)] = low(value)

    fetch(h1, h1_kept, spill_sem.at[0])

    def group_rows(g):
        return slice(starts[g] * ROWS, (starts[g] + counts[g]) * ROWS)

    def window(padded, start, g, dy, dx_):
        first = start + 1 + (1 + dy) * (widths[g] + 1) + dx_
        return padded[rows_at(first, counts[g])]

    def window_a(g, a, c):
        py, dy = lax.rem(a + 1, 2), (a + 1) // 2 - 1
        px, dx_ = lax.rem(c + 1, 2), (c + 1) // 2 - 1
        first = top_starts[g] + 1 + (1 + dy) * (widths[g] + 1) + dx_
        return big_a[2 * py + px, rows_at(first, counts[g])]

    def clear_acc():
        @pl.loop(0, total // STEP)
        def _(i):
            acc[steps(i)] = jnp.zeros((STEP, WIDE), jnp.float32)

    def conv_taps(first, last, window_of, product):
        @pl.loop(first, last)
        def _(t):
            for g in groups:
                acc[group_rows(g)] += product(window_of(g, t // 3, lax.rem(t, 3)), wp[t])

    def masked_sums(target):
        def body(i, carry):
            rows = steps(i)
            value = acc[rows] * wide_mask(mask_ref[rows])
            target[rows] = low(value)
            return carry[0] + fold(value), carry[1] + fold(value * value)

        return lax.fori_loop(0, total // STEP, body, (zero8, zero8))

    clear_acc()
    arrived(wp, w_sem.at[0])
    conv_taps(3, 9, window_a, times)
    halo_wait(halo_a, halo_recv, 0, h > 0)
    conv_taps(0, 3, window_a, times)
    sums = masked_sums(h2)
    state = sums_start("thin", [one_row(v) for v in sums])
    fetch(spatial_b, wp, w_sem.at[0])
    fetch(big_a, a1_kept, spill_sem.at[1])
    halo_wait(halo_a, halo_send, 0, h < n_height - 1)
    sums_middle(state)
    sums = sums_end(state)
    keep_stats(stat_mid, 1, sums, total_out, gain_mid[1:2], shift_mid[1:2])

    def activate(source, target, index):
        scale, offset = stat_mid[index, 2:3], stat_mid[index, 3:4]

        @pl.loop(0, total // STEP)
        def _(i):
            rows = steps(i)
            pre = up32(source[rows]) * scale + offset
            target[rows] = low(pre * sigmoid(pre) * wide_mask(mask_ref[rows]))

    activate(h2, a2, 1)
    arrived(wq.at[0:4], w_sem.at[1])

    def expansion(source, target):
        @pl.loop(0, 4)
        def _(n):
            value = times(source[...], wq[n])
            target[n, 0:total] = low(value)
            stat_out[pl.ds(n, 1)] = one_row(fold(value))
            stat_out[pl.ds(4 + n, 1)] = one_row(fold(value * value))

    expansion(a2, h3)
    state = sums_start("wide", None)
    fetch_columns(expand_b, wq, 0, w_sem.at[1])
    sums_middle(state)
    sums_end(state)

    def out_stats(index, n, row):
        keep_stats(
            mid_or_out,
            4 * index + n,
            [stat_out[row + n : row + n + 1], stat_out[row + 4 + n : row + 5 + n]],
            total_out,
            gain_out[index, n : n + 1],
            shift_out[index, n : n + 1],
        )

    mid_or_out = stat_mid.at[4:16]
    for n in range(4):
        out_stats(0, n, 0)
        out_stats(1, n, 8)

    def out_stat(index, n, row):
        return stat_mid[4 + 4 * index + n, row : row + 1]

    def joint(n, rows):
        return (
            up32(h3[n, rows]) * out_stat(0, n, 2)
            + up32(side[n, rows]) * out_stat(1, n, 2)
            + (out_stat(0, n, 3) + out_stat(1, n, 3))
        )

    arrived(wq.at[4:8], w_sem.at[2])
    clear_acc()

    @pl.loop(0, 4)
    def _(n):
        @pl.loop(0, 2)
        def _(i):
            rows = pl.ds(pl.multiple_of(i * half, ROWS), half)
            value = joint(n, rows)
            value = low(value * sigmoid(value) * wide_mask(mask_ref[rows]))
            mb[n, rows] = value
            acc[rows] += times(value, wq[4 + n])

    def plain_sums(target):
        def body(i, carry):
            rows = steps(i)
            value = acc[rows]
            target[rows] = low(value)
            return carry[0] + fold(value), carry[1] + fold(value * value)

        return lax.fori_loop(0, total // STEP, body, (zero8, zero8))

    sums = plain_sums(h4)
    state = sums_start("thin", [one_row(v) for v in sums])
    sums_middle(state)
    clear_acc()
    sums = sums_end(state)
    keep_stats(stat_mid, 2, sums, total_out, gain_mid[2:3], shift_mid[2:3])

    scale, offset = stat_mid[2, 2:3], stat_mid[2, 3:4]
    for g in groups:
        pre = last_row(h4, g) * scale + offset
        mask = wide_mask(mask_ref[starts[g] * ROWS : (starts[g] + widths[g]) * ROWS])
        halo_down[halo_rows(g)] = low(pre * sigmoid(pre) * mask)
    send_down(halo_down, a4p, 1)
    for g in groups:
        pre = first_row(h4, g) * scale + offset
        mask = wide_mask(mask_ref[starts[g] * ROWS : (starts[g] + widths[g]) * ROWS])
        halo_up[halo_rows(g)] = low(pre * sigmoid(pre) * mask)
    send_up(halo_up, 2)

    def both_base(g):
        return (both_starts[g] + 1 + widths[g] + 1) * ROWS

    for g in groups:

        @pl.loop(0, counts[g] * ROWS // STEP)
        def _(i):
            rows = pl.ds(pl.multiple_of(starts[g] * ROWS + i * STEP, ROWS), STEP)
            pre = up32(h4[rows]) * scale + offset
            value = low(pre * sigmoid(pre) * wide_mask(mask_ref[rows]))
            a4p[pl.ds(pl.multiple_of(both_base(g) + i * STEP, ROWS), STEP)] = value

    def window_b(g, a, c):
        return window(a4p, both_starts[g], g, a - 1, c - 1)

    def window_b_back(g, a, c):
        return window(dhp, both_starts[g], g, 1 - a, 1 - c)

    arrived(wp, w_sem.at[0])
    conv_taps(3, 6, window_b, times)
    halo_wait(halo_down, halo_recv, 1, h > 0)
    halo_wait(halo_in, halo_recv, 2, h < n_height - 1)
    place_below(a4p)
    conv_taps(0, 3, window_b, times)
    conv_taps(6, 9, window_b, times)
    sums = masked_sums(h5)
    state = sums_start("thin", [one_row(v) for v in sums])
    halo_wait(halo_down, halo_send, 1, h < n_height - 1)
    halo_wait(halo_up, halo_send, 2, h > 0)
    sums_middle(state)
    sums = sums_end(state)
    keep_stats(stat_mid, 3, sums, total_out, gain_mid[3:4], shift_mid[3:4])

    activate(h5, a5, 3)
    arrived(wq.at[0:4], w_sem.at[1])
    arrived(big_a, spill_sem.at[1])
    expansion(a5, h6)
    for row in range(8, 16):
        stat_out[row : row + 1] = jnp.zeros((1, WIDE), jnp.float32)
    state = sums_start("wide", None)
    sums_middle(state)
    arrived(h1, spill_sem.at[0])
    sums_end(state)
    for n in range(4):
        out_stats(2, n, 0)

    @pl.loop(0, 4)
    def _(n):
        index = 12 + n
        root, scale = stat_mid[index, 1:2], stat_mid[index, 2:3]
        offset, back = stat_mid[index, 3:4], stat_mid[index, 4:5]
        zero = jnp.zeros((ROWS, WIDE), jnp.float32)
        total_grad, total_dot = zero, zero
        for g in groups:

            def body(i, carry):
                rows = rows_at(starts[g] + i, 1)
                value = up32(h6[n, rows])
                mask = wide_mask(mask_ref[rows])
                z = value * scale + offset + up32(mb[n, rows])
                s = sigmoid(z)
                grad = up_ref[g, n] * (s * (1.0 + z * (1.0 - s))) * mask
                dz[n, rows] = low(grad)
                return (
                    carry[0] + z * s * mask,
                    carry[1] + grad,
                    carry[2] + grad * (value * root + back),
                )

            pool, total_grad, total_dot = lax.fori_loop(
                0, counts[g], body, (zero, total_grad, total_dot)
            )
            pool_slots[h, n, g * ROWS : (g + 1) * ROWS] = low(pool)
        stat_out[pl.ds(n, 1)] = one_row(fold(total_grad))
        stat_out[pl.ds(4 + n, 1)] = one_row(fold(total_dot))

    state = sums_start("wide", None)

    for k in range(1, n_height):
        pltpu.make_async_remote_copy(
            src_ref=pool_slots.at[h],
            dst_ref=pool_slots.at[h],
            send_sem=pool_sem.at[0],
            recv_sem=pool_sem.at[1],
            device_id=(b, lax.rem(h + k, n_height)),
            device_id_type=MESH,
        ).start()
    sums_middle(state)
    clear_acc()
    sums_end(state)

    def out_back(index, sum_row, dot_row, n):
        sums = [stat_out[pl.ds(sum_row + n, 1)], stat_out[pl.ds(dot_row + n, 1)]]
        out_sums[index, 0, pl.ds(n, 1)] = sums[0]
        out_sums[index, 1, pl.ds(n, 1)] = sums[1]
        return back_factors(
            stat_mid, 4 + 4 * index + n, sums, total_out, gain_out[index, pl.ds(n, 1)]
        )

    def mid_back(index, place, sums, number):
        mid_sums[place, 0:1] = sums[0]
        mid_sums[place, 1:2] = sums[1]
        return back_factors(stat_mid, index, sums, number, gain_mid[place : place + 1])

    def mid_gradient(source, index):
        root, scale = stat_mid[index, 1:2], stat_mid[index, 2:3]
        offset, back = stat_mid[index, 3:4], stat_mid[index, 4:5]

        def body(i, carry):
            rows = steps(i)
            value = up32(source[rows])
            pre = value * scale + offset
            s = sigmoid(pre)
            grad = acc[rows] * (s * (1.0 + pre * (1.0 - s))) * wide_mask(mask_ref[rows])
            acc[rows] = grad
            return carry[0] + fold(grad), carry[1] + fold(grad * (value * root + back))

        sums = lax.fori_loop(0, total // STEP, body, (zero8, zero8))
        return [one_row(v) for v in sums]

    @pl.loop(0, 4)
    def _(n):
        main, slope, constant = out_back(2, 0, 4, n)

        @pl.loop(0, 2)
        def _(i):
            rows = pl.ds(pl.multiple_of(i * half, ROWS), half)
            grad = main * up32(dz[n, rows]) + slope * up32(h6[n, rows]) + constant
            grad = low(grad * wide_mask(mask_ref[rows]))
            h6[n, rows] = grad
            acc[rows] += times_t(grad, wq[n])

    sums = mid_gradient(h5, 3)
    state = sums_start("thin", sums)
    fetch_columns(expand_a, wq, 0, w_sem.at[1])
    sums_middle(state)
    store_tiles(
        4, lambda t: t_times(a5[...], h6[t, 0:total]), lambda t: wide_columns(g_expand_b, t)
    )
    fetch(a1_kept, big_a, spill_sem.at[1])
    sums = sums_end(state)

    def mid_step(target, factors, padded):
        main, slope, constant = factors

        def tile(rows):
            grad = main * acc[rows] + slope * up32(target[rows]) + constant
            return low(grad * wide_mask(mask_ref[rows]))

        for g in groups:

            @pl.loop(0, counts[g] * ROWS // STEP)
            def _(i):
                rows = pl.ds(pl.multiple_of(starts[g] * ROWS + i * STEP, ROWS), STEP)
                grad = tile(rows)
                target[rows] = grad
                if padded is not None:
                    padded[pl.ds(pl.multiple_of(both_base(g) + i * STEP, ROWS), STEP)] = grad

    mid_step(h5, mid_back(3, 3, sums, total_out), dhp)
    for g in groups:
        halo_down[halo_rows(g)] = low(last_row(h5, g))
        halo_up[halo_rows(g)] = low(first_row(h5, g))
    send_down(halo_down, dhp, 1)
    send_up(halo_up, 2)
    clear_acc()
    conv_taps(3, 6, window_b_back, times_t)
    halo_wait(halo_down, halo_recv, 1, h > 0)
    halo_wait(halo_in, halo_recv, 2, h < n_height - 1)
    place_below(dhp)
    conv_taps(0, 3, window_b_back, times_t)
    conv_taps(6, 9, window_b_back, times_t)
    fetch(spatial_a, wp, w_sem.at[0])
    sums = mid_gradient(h4, 2)
    state = sums_start("thin", sums)
    halo_wait(halo_down, halo_send, 1, h < n_height - 1)
    halo_wait(halo_up, halo_send, 2, h > 0)
    sums_middle(state)

    def spatial_tile(window_of, grads):
        def value_of(t):
            parts = [
                t_times(window_of(g, t // 3, lax.rem(t, 3)), grads[group_rows(g)]) for g in groups
            ]
            return parts[0] + parts[1] + parts[2]

        return value_of

    store_tiles(9, spatial_tile(window_b, h5), lambda t: g_spatial_b.at[t])
    sums = sums_end(state)

    mid_step(h4, mid_back(2, 2, sums, total_out), None)
    fetch(x.at[0, :, columns(1)], a4p.at[0:total], x_sem.at[1])

    @pl.loop(0, 4)
    def _(n):
        def body(i, carry):
            rows = pl.ds(pl.multiple_of(i * half, ROWS), half)
            grad = times_t(h4[rows], wq[4 + n]) + up32(dz[n, rows])
            z = joint(n, rows)
            s = sigmoid(z)
            grad = grad * (s * (1.0 + z * (1.0 - s))) * wide_mask(mask_ref[rows])
            dz[n, rows] = low(grad)
            main_hat = up32(h3[n, rows]) * out_stat(0, n, 1) + out_stat(0, n, 4)
            side_hat = up32(side[n, rows]) * out_stat(1, n, 1) + out_stat(1, n, 4)
            return (
                carry[0] + fold(grad),
                carry[1] + fold(grad * main_hat),
                carry[2] + fold(grad * side_hat),
            )

        sums = lax.fori_loop(0, 2, body, (zero8, zero8, zero8))
        for v in range(3):
            stat_out[pl.ds(4 * v + n, 1)] = one_row(sums[v])

    state = sums_start("wide", None)
    sums_middle(state)
    store_tiles(
        4, lambda t: t_times(mb[t], h4[...]), lambda t: wide_rows(g_reduce_b, t)
    )
    fetch(x.at[:, :, columns(0)], mb, x_sem.at[0])
    clear_acc()
    sums_end(state)

    arrived(wq.at[0:4], w_sem.at[1])

    @pl.loop(0, 4)
    def _(n):
        main, slope, constant = out_back(0, 0, 4, n)
        main2, slope2, constant2 = out_back(1, 0, 8, n)

        @pl.loop(0, 2)
        def _(i):
            rows = pl.ds(pl.multiple_of(i * half, ROWS), half)
            grad_in = up32(dz[n, rows])
            mask = wide_mask(mask_ref[rows])
            grad = low((main * grad_in + slope * up32(h3[n, rows]) + constant) * mask)
            h3[n, rows] = grad
            acc[rows] += times_t(grad, wq[n])
            other = main2 * grad_in + slope2 * up32(side[n, rows]) + constant2
            side[n, rows] = low(other * mask)

    fetch(h1_kept, h1, spill_sem.at[0])
    fetch_shortcut()
    sums = mid_gradient(h2, 1)
    state = sums_start("thin", sums)
    sums_middle(state)
    store_tiles(4, lambda t: t_times(a2[...], h3[t]), lambda t: wide_columns(g_expand_a, t))
    arrived(mb, x_sem.at[0])
    arrived(a4p.at[0:total], x_sem.at[1])
    store_tiles(
        4,
        lambda t: t_times(mb[0], side[t]),
        lambda t: wide_columns(g_shortcut_a.at[0:WIDE], t),
    )
    store_tiles(
        4,
        lambda t: t_times(a4p[0:total], side[t]),
        lambda t: wide_columns(g_shortcut_a.at[WIDE : 2 * WIDE], t),
    )
    sums = sums_end(state)

    mid_step(h2, mid_back(1, 1, sums, total_out), dhp)
    for g in groups:
        halo_up[halo_rows(g)] = low(first_row(h2, g))
    send_up(halo_up, 2)
    arrived(wp, w_sem.at[0])
    arrived(h1, spill_sem.at[0])
    root, scale = stat_mid[0, 1:2], stat_mid[0, 2:3]
    offset, back = stat_mid[0, 3:4], stat_mid[0, 4:5]
    carry = (zero8, zero8)
    for p in range(4):
        py, px = p // 2, p % 2
        row_taps = ((1, 0),) if py == 0 else ((0, 1), (2, 0))
        column_taps = ((1, 0),) if px == 0 else ((0, 1), (2, 0))
        if p == 2:
            halo_wait(halo_in, halo_recv, 2, h < n_height - 1)
            place_below(dhp)
        for g in groups:
            value = None
            for a, dy in row_taps:
                for c, dx_ in column_taps:
                    product = times_t(window(dhp, both_starts[g], g, dy, dx_), wp[3 * a + c])
                    value = product if value is None else value + product
            acc[group_rows(g)] = value

        def body(i, carry):
            rows = steps(i)
            value = up32(h1[p, rows])
            pre = value * scale + offset
            s = sigmoid(pre)
            grad = acc[rows] * (s * (1.0 + pre * (1.0 - s))) * wide_mask(mask_ref[rows])
            h3[p, rows] = low(grad)
            return carry[0] + fold(grad), carry[1] + fold(grad * (value * root + back))

        carry = lax.fori_loop(0, total // STEP, body, carry)
    state = sums_start("thin", [one_row(v) for v in carry])
    halo_wait(halo_up, halo_send, 2, h > 0)
    sums_middle(state)
    arrived(big_a, spill_sem.at[1])
    store_tiles(9, spatial_tile(window_a, h2), lambda t: g_spatial_a.at[t])
    fetch(x.at[:, :, columns(1)], big_a.at[:, 0:total], x_sem.at[1])
    sums = sums_end(state)

    main, slope, constant = mid_back(0, 0, sums, total_in)

    @pl.loop(0, 4)
    def _(p):
        @pl.loop(0, total // STEP)
        def _(i):
            rows = steps(i)
            grad = main * up32(h3[p, rows]) + slope * up32(h1[p, rows]) + constant
            h1[p, rows] = low(grad * wide_mask(mask_ref[rows]))

    arrived(wq, w_sem.at[1])
    for k in range(2):

        @pl.loop(0, 2)
        def _(i):
            rows = pl.ds(pl.multiple_of(i * half, ROWS), half)
            value = times_t(h1[0, rows], w2[k])
            for n in range(4):
                value = value + times_t(side[n, rows], wq[2 * n + k])
            if k == 0:
                h3[0, rows] = low(value)
            else:
                a4p[rows] = low(value)

    fetch(h3.at[0], dx.at[0, :, columns(0)], dx_sem.at[0])
    fetch(a4p.at[0:total], dx.at[0, :, columns(1)], dx_sem.at[0])

    @pl.loop(1, 4)
    def _(p):
        h3[p] = low(times_t(h1[p], w2[0]))
        side[p] = low(times_t(h1[p], w2[1]))
        fetch(h3.at[p], dx.at[p, :, columns(0)], dx_sem.at[0])
        fetch(side.at[p], dx.at[p, :, columns(1)], dx_sem.at[0])

    arrived(big_a.at[:, 0:total], x_sem.at[1])

    def last_tile(chunk):
        def value_of(t):
            value = t_times(chunk(0), h1[0])
            for p in range(1, 4):
                value = value + t_times(chunk(p), h1[p])
            return value

        return value_of

    store_tiles(1, last_tile(lambda p: mb[p]), lambda t: g_reduce_a.at[0:WIDE])
    store_tiles(
        1, last_tile(lambda p: big_a[p, 0:total]), lambda t: g_reduce_a.at[WIDE : 2 * WIDE]
    )

    others = pool_slots.at[0 : n_height - 1]
    pltpu.make_async_copy(others, others, pool_sem.at[1]).wait()
    pltpu.make_async_copy(others, others, pool_sem.at[0]).wait()
    for g in groups:
        for n in range(4):
            value = None
            for k in range(n_height):
                part = up32(pool_slots[k, n, g * ROWS : (g + 1) * ROWS])
                value = part if value is None else value + part
            pooled[g, n] = value * (1.0 / (widths[g] * widths[g]))

    for slot in range(2):
        arrived(staged.at[slot], g_sem.at[slot])
    arrived(h3, dx_sem.at[0])
    arrived(h3, dx_sem.at[0])


def to_planes(image, live, images):
    count, rows, cols, channels = image.shape
    value = image.reshape(count, rows // 2, 2, cols // 2, 2, channels)
    value = jnp.transpose(value, (2, 4, 1, 3, 0, 5))
    keep = (jnp.arange(rows // 2, dtype=jnp.int32) < live)[None, None, :, None, None, None]
    value = jnp.where(keep, value, jnp.zeros((), value.dtype))
    value = jnp.pad(value, ((0, 0), (0, 0), (0, 0), (0, 1), (0, images - count), (0, 0)))
    return value.reshape(4, -1, channels)


def from_planes(planes, shape):
    count, rows, cols, channels = shape
    value = planes.reshape(2, 2, rows // 2, cols // 2 + 1, -1, channels)
    value = value[:, :, :, : cols // 2, :count]
    return jnp.transpose(value, (4, 2, 0, 3, 1, 5)).reshape(shape)


def per_device(
    image_small, image_medium, image_large, row_counts, reduce_a, first_spatial_weight, expand_a,
    shortcut_a, reduce_b, second_spatial_weight, expand_b, gain_mid, shift_mid, gain_out,
    shift_out, upstream_small, upstream_medium, upstream_large,
):
    images = (image_small, image_medium, image_large)
    upstreams = (upstream_small, upstream_medium, upstream_large)
    n_batch, n_height = lax.axis_size("batch"), lax.axis_size("height")
    heights = [value.shape[1] // 2 for value in images]
    widths = [value.shape[2] // 2 for value in images]
    count = images[0].shape[0]
    live = row_counts[:, lax.axis_index("height")]
    pixels = sum(o * o for o in widths) * count * n_batch
    counts, starts, top_total, _, both_total, _, _ = grids(heights, widths)
    total = sum(counts) * ROWS
    x = jnp.concatenate([to_planes(images[g], live[g], ROWS) for g in range(3)], axis=1)
    masks = []
    for g in range(3):
        row_ok = (jnp.arange(heights[g], dtype=jnp.int32) < live[g])[:, None, None]
        column_ok = (jnp.arange(widths[g] + 1) < widths[g])[None, :, None]
        image_ok = (jnp.arange(ROWS) < count)[None, None, :]
        masks.append(jnp.logical_and(jnp.logical_and(row_ok, column_ok), image_ok).reshape(-1))
    mask = jnp.concatenate(masks).astype(jnp.float32)
    mask = jnp.broadcast_to(mask[:, None], (total, 128))
    edges = (jnp.arange(max(heights))[None, :] == live[:, None] - 1).astype(jnp.float32)
    edges = jnp.broadcast_to(edges[:, :, None, None], edges.shape + (8, 128))
    up = jnp.stack(
        [
            jnp.pad(
                upstreams[g].astype(jnp.float32) / (widths[g] * widths[g]),
                ((0, ROWS - count), (0, 0)),
            )
            for g in range(3)
        ]
    )
    up = jnp.transpose(up.reshape(3, ROWS, 4, WIDE), (0, 2, 1, 3))
    halo = sum(widths) * ROWS
    bf, f32 = jnp.bfloat16, jnp.float32
    dma = pltpu.SemaphoreType.DMA
    vmem = pl.BlockSpec(memory_space=pltpu.VMEM)
    anywhere = pl.BlockSpec(memory_space=pl.ANY)
    flat_a = first_spatial_weight.reshape(9, WIDE, WIDE)
    flat_b = second_spatial_weight.reshape(9, WIDE, WIDE)
    big = pltpu.VMEM((4, total, WIDE), bf)
    thin = pltpu.VMEM((total, WIDE), bf)
    results = pl.pallas_call(
        functools.partial(
            main_kernel, n_batch, n_height, heights, widths, float(4 * pixels), float(pixels)
        ),
        out_shape=[
            jax.ShapeDtypeStruct((3, 4, ROWS, WIDE), f32),
            jax.ShapeDtypeStruct(x.shape, bf),
            jax.ShapeDtypeStruct(reduce_a.shape, bf),
            jax.ShapeDtypeStruct(flat_a.shape, bf),
            jax.ShapeDtypeStruct(expand_a.shape, bf),
            jax.ShapeDtypeStruct(shortcut_a.shape, bf),
            jax.ShapeDtypeStruct(reduce_b.shape, bf),
            jax.ShapeDtypeStruct(flat_b.shape, bf),
            jax.ShapeDtypeStruct(expand_b.shape, bf),
            jax.ShapeDtypeStruct((4, 2, WIDE), f32),
            jax.ShapeDtypeStruct((3, 2, 4, WIDE), f32),
            jax.ShapeDtypeStruct((4, total, WIDE), bf),
            jax.ShapeDtypeStruct((4, top_total * ROWS, WIDE), bf),
        ],
        in_specs=[anywhere] * 8 + [vmem] * 7,
        out_specs=[vmem] + [anywhere] * 8 + [vmem] * 2 + [anywhere] * 2,
        scratch_shapes=[
            big,
            pltpu.VMEM((4, top_total * ROWS, WIDE), bf),
            big, big, big,
            thin, thin, thin, thin, thin,
            pltpu.VMEM((both_total * ROWS, WIDE), bf),
            pltpu.VMEM((both_total * ROWS, WIDE), bf),
            pltpu.VMEM((total, WIDE), f32),
            pltpu.VMEM((9, WIDE, WIDE), bf),
            pltpu.VMEM((8, WIDE, WIDE), bf),
            pltpu.VMEM((2, WIDE, WIDE), bf),
            pltpu.VMEM((2, halo, WIDE), bf),
            pltpu.VMEM((halo, WIDE), bf),
            pltpu.VMEM((halo, WIDE), bf),
            pltpu.VMEM((halo, WIDE), bf),
            pltpu.VMEM((2, WIDE, WIDE), bf),
            pltpu.VMEM((n_height, 4, 3 * ROWS, WIDE), bf),
            pltpu.VMEM((2, n_height, 8, 128), f32),
            pltpu.VMEM((2, n_batch, 8, 128), f32),
            pltpu.VMEM((2, n_height, 16, WIDE), f32),
            pltpu.VMEM((2, n_batch, 16, WIDE), f32),
            pltpu.VMEM((16, 8, WIDE), f32),
            pltpu.VMEM((16, WIDE), f32),
            dma((4,)), dma((2,)), dma((2,)), dma((1,)), dma((2,)),
            dma((2, 2, 2)), dma((2, 2, 2)), dma((3,)), dma((3,)), dma((2,)),
        ],
        compiler_params=pltpu.CompilerParams(
            collective_id=0, has_side_effects=True, vmem_limit_bytes=63 << 20
        ),
        name="both_blocks",
    )(
        x, reduce_a, flat_a, expand_a, shortcut_a, reduce_b, flat_b, expand_b,
        edges, mask, gain_mid, shift_mid,
        gain_out.reshape(3, 4, WIDE), shift_out.reshape(3, 4, WIDE), up,
    )
    pooled = jnp.transpose(results[0], (0, 2, 1, 3)).reshape(3, ROWS, -1)[:, :count]
    backs = [
        from_planes(
            results[1][:, starts[g] * ROWS : (starts[g] + counts[g]) * ROWS], images[g].shape
        )
        for g in range(3)
    ]
    shards = reduce_grads(results[2:9])
    for place in (1, 5):
        shards[place] = shards[place].reshape((3, 3) + shards[place].shape[1:])
    mid, out = results[9], results[10].reshape(3, 2, -1)
    return (
        pooled[0], pooled[1], pooled[2], backs[0], backs[1], backs[2], *shards,
        mid[:, 1], mid[:, 0], out[:, 1], out[:, 0],
    )


def solution(mesh):
    placed = (
        P("batch", "height", None, None),
        P("batch", "height", None, None),
        P("batch", "height", None, None),
        P(),
        P(),
        P(),
        P(),
        P(),
        P(),
        P(),
        P(),
        P(),
        P(),
        P(),
        P(),
        P("batch", None),
        P("batch", None),
        P("batch", None),
    )
    return jax.shard_map(
        per_device,
        mesh=mesh,
        in_specs=placed,
        out_specs=(
            P("batch", None),
            P("batch", None),
            P("batch", None),
            P("batch", "height", None, None),
            P("batch", "height", None, None),
            P("batch", "height", None, None),
            P("batch", None),
            P(None, None, "batch", None),
            P("batch", None),
            P("batch", None),
            P("batch", None),
            P(None, None, "batch", None),
            P("batch", None),
            P(),
            P(),
            P(),
            P(),
        ),
        check_vma=False,
    )
```

time: 1390 us -> 562 us (0.40)
  matrix products: 334 us -> 0 us
  other arithmetic: 334 us -> 30.7 us
  local copies, waits for them, and re-layouts: 396 us -> 138 us
  Pallas kernels: 265 us -> 382 us
  between operations: 27.8 us -> 1.63 us
    dot_general x207 -> x0, matrix products: 334 us -> none  [the longest x69 138 us: weight_term(): jnp.einsum('hwic,hwid->cd', values, grad_in, preferred_element_type=jnp.f...]
    slice x45 -> x6, local copies, waits for them, and re-layouts: 189 us -> 7.39 us  [the longest x3 6.82 us: per_device(): results[1][:, starts[g] * ROWS:(starts[g] + counts[g]) * ROWS]]
    scatter-add x33 -> x0, other arithmetic: 164 us -> none  [the longest x27 141 us: spatial_back(): padded_grad = padded_grad.at[row_tap:row_tap + stride * (out_rows - 1) +...]
    pallas_call x12 -> x1, Pallas kernels: 146 us -> 261 us  [per_device(): pl.pallas_call(functools.partial(main_kernel, n_batch, n_height, heights,...]
    convert_element_type x34 -> x2, other arithmetic: 59.3 us -> 0.08 us  [the longest x1 0.07 us: per_device(): (jnp.arange(max(heights))[None, :] == live[:, None] - 1).astype(jnp.float32)]
    unnamed x900 -> x27, local copies, waits for them, and re-layouts: 69.6 us -> 16.2 us
    reduce_sum x9 -> x0, other arithmetic: 29.2 us -> none  [the longest x3 15.1 us: grad_stats(): jnp.sum(grad_list[picture_batches] * (value_list[picture_batches] - centr...]
    convert_element_type x4 -> x0, local copies, waits for them, and re-layouts: 27.3 us -> none  [by_piece(): value.astype(jnp.bfloat16)]
  transfers between devices with their start and end apart: 7 -> 0, of which waited for: 0 -> 0; matrix products, arithmetic and copies ran while one was open for 18% -> 0% of each run, Pallas kernels for 0% -> 0%
where the time goes in v3:
time: 562 us; the launch traced here: 553 us
  Pallas kernels  382 us (68%)
  local copies, waits for them, and re-layouts  138 us (25%)
  other arithmetic  30.7 us (5%)
    pallas_call x1, Pallas kernels, per_device(): pl.pallas_call(functools.partial(main_kernel, n_batch, n_height, heights,...  261 us
    pallas_call x1, Pallas kernels, reduce_grads(): pl.pallas_call(functools.partial(grads_kernel, n_batch), out_shape=jax.Sh...  121 us
    reshape x12, local copies, waits for them, and re-layouts, by_piece(): value.astype(jnp.bfloat16)  47.5 us
    unnamed x27, local copies, waits for them, and re-layouts  16.2 us
    reshape x3, local copies, waits for them, and re-layouts, to_planes(): value = image.reshape(count, rows // 2, 2, cols // 2, 2, channels)  14.8 us

profile of v3, /device:TPU:0, one launch (start us, length us, event | category | flops | bytes accessed | tf_op | source)
XLA Modules:
  0.0 552.6 jit_solution(13227844499054196262)
XLA Ops:
  0.7 6.9 %reshape.404 = bf16[12,4,2,9,2,1024]{5,2,1,4,3,0:T(2,128)(2,1)S(1)} reshape(bf16[12,8,18,1024]{3,1,2,0:T(8,128)(2,1)} %param.20) | data formatting | bytes 7077888 | tf_op jit(solution)/shard_map/reshape | solution.py:1098
  8.9 4.2 fusion
  13.1 3.4 pad.24
  16.5 4.6 reshape.402
  23.7 3.3 reshape.400
  30.4 10.6 %pad_maximum_fusion.x = bf16[4,1216,1024]{2,1,0:T(8,128)(2,1)} fusion(bf16[4,640,1024]{2,1,0:T(8,128)(2,1)} %bitcast.130, bf16[4,384,1024]{2,1,0:T(8,128)(2,1)S(1)} %bitcast.135, bf16[4,192,1024]{2,1,0:T(8,128)(2,1)S(1)} %bitcast.144), kind=kLoop, calls=%fused_computation.1 | loop fusion | flops 29884416 | bytes 19922944 | tf_op jit(solution)/shard_map/concatenate | solution.py:1128
  46.3 261.2 %both_blocks.1 = (f32[3,4,16,512]{3,2,1,0:T(8,128)}, bf16[4,1216,1024]{2,1,0:T(8,128)(2,1)}, bf16[1024,512]{1,0:T(8,128)(2,1)}, bf16[9,512,512]{2,1,0:T(8,128)(2...) custom-call(bf16[4,1216,1024]{2,1,0:T(8,128)(2,1)} %pad_maximum_fusi, ...), custom_call_target="tpu_custom_call" | custom-call | tf_op jit(solution)/shard_map/both_blocks/pallas_call | solution.py:1158
  320.4 3.1 slice.95
  324.0 3.7 copy.83
  327.7 3.4 reshape.416
  333.6 7.8 %reshape.419 = bf16[9,4,2,64,2,2,1,128]{7,5,4,3,2,1,0,6:T(2,128)(2,1)} reshape(bf16[9,512,512]{2,1,0:T(8,128)(2,1)} %get-tuple-element.31) | data formatting | bytes 9437184 | tf_op jit(solution)/shard_map/reshape | solution.py:171
  341.4 3.6 copy.85
  345.0 3.0 constant_dynamic-update-slice_fusion.4
  348.0 3.2 reshape.421
  354.1 7.7 %reshape.423 = bf16[1,4,2,128,2,2,4,128]{7,6,5,4,3,2,1,0:T(4,128)(2,1)} reshape(bf16[1024,2048]{1,0:T(8,128)(2,1)} %get-tuple-element.33) | data formatting | bytes 8388608 | tf_op jit(solution)/shard_map/reshape | solution.py:171
  361.8 4.4 copy.87
  373.3 8.0 %reshape.427 = bf16[9,4,2,64,2,2,1,128]{7,5,4,3,2,1,0,6:T(2,128)(2,1)} reshape(bf16[9,512,512]{2,1,0:T(8,128)(2,1)} %get-tuple-element.35) | data formatting | bytes 9437184 | tf_op jit(solution)/shard_map/reshape | solution.py:171
  381.3 3.6 copy.89
  384.9 3.1 constant_dynamic-update-slice_fusion.1
  388.0 3.2 reshape.429
  394.0 8.3 %fusion.4 = (bf16[1,2,2,4,2560,128]{5,4,3,2,1,0:T(8,128)(2,1)S(1)}, bf16[1,2,2,4,2560,128]{5,4,3,2,1,0:T(8,128)(2,1)S(1)}) fusion(bf16[2,2,2,4,2560,128]{5,4,3,2,1,0:T(8,128)(2,1)} %constant_dynamic-update-slice_fusion), kind=kLoop, calls=%fused_computation.55 | loop fusion | bytes 41943040 | tf_op jit(solution)/shard_map/slice | solution.py:193
  402.3 7.3 %maximum_bitcast_fusion.local_ref = bf16[10,2,2,2,4,256,128]{6,5,4,3,2,1,0:T(8,128)(2,1)} fusion(bf16[1,2,2,4,10,256,128]{6,5,4,3,2,1,0:T(8,128)(2,1)S(1)} %bitcast.128, bf16[1,2,2,4,10,256,128]{6,5,4,3,1,2,0:T(8,128)(2,1)S(1)} %bitcast.129), kind=kLoop, calls=%fused_computation | loop fusion | flops 41943040 | bytes 41943040 | tf_op jit(solution)/shard_map/transpose | solution.py:195
  409.6 120.9 %reduce_grads.1 = bf16[10,2,2,256,128]{4,3,2,1,0:T(8,128)(2,1)} custom-call(bf16[10,2,2,2,4,256,128]{6,5,4,3,2,1,0:T(8,128)(2,1)} %maximum_bitcast_fusion.local_ref), custom_call_target="tpu_custom_call" | custom-call | tf_op jit(solution)/shard_map/reduce_grads/pallas_call | solution.py:196
  535.6 3.1 reshape.445
  (105 shorter events, 59.6 us)
Async XLA Ops:
  0.7 6.9 %copy-start.8 = (s32[3,4]{1,0:T(4,128)S(1)}, s32[3,4]{1,0:T(4,128)}, u32[]{:S(2)}) copy-start(s32[3,4]{1,0:T(4,128)} %param.21) | copy-start | bytes 148
  30.3 13.4 %copy-start.5 = (f32[3,2048]{1,0:T(4,128)S(1)}, f32[3,2048]{1,0:T(4,128)}, u32[]{:S(2)}) copy-start(f32[3,2048]{1,0:T(4,128)} %param.31) | copy-start | bytes 73732
  30.3 14.0 %copy-start.6 = (f32[3,2048]{1,0:T(4,128)S(1)}, f32[3,2048]{1,0:T(4,128)}, u32[]{:S(2)}) copy-start(f32[3,2048]{1,0:T(4,128)} %param.32) | copy-start | bytes 73732
  30.3 14.6 %copy-start.1 = (bf16[12,2048]{1,0:T(8,128)(2,1)S(1)}, bf16[12,2048]{1,0:T(8,128)(2,1)}, u32[]{:S(2)}) copy-start(bf16[12,2048]{1,0:T(8,128)(2,1)} %param.35) | copy-start | bytes 147460
  30.4 14.8 %copy-start.2 = (bf16[12,2048]{1,0:T(8,128)(2,1)S(1)}, bf16[12,2048]{1,0:T(8,128)(2,1)}, u32[]{:S(2)}) copy-start(bf16[12,2048]{1,0:T(8,128)(2,1)} %param.34) | copy-start | bytes 147460
  30.4 15.0 %copy-start.3 = (bf16[12,2048]{1,0:T(8,128)(2,1)S(1)}, bf16[12,2048]{1,0:T(8,128)(2,1)}, u32[]{:S(2)}) copy-start(bf16[12,2048]{1,0:T(8,128)(2,1)} %param.33) | copy-start | bytes 147460
  544.3 5.3 copy-start
  545.6 5.1 copy-start.7
  545.6 5.7 %copy-start.4 = (f32[3,2,4,512]{3,2,1,0:T(4,128)S(1)}, f32[3,2,4,512]{3,2,1,0:T(4,128)}, u32[]{:S(2)}) copy-start(f32[3,2,4,512]{3,2,1,0:T(4,128)} %get-tuple-element.38) | copy-start | bytes 147460

commit v4 on v3

--- a/solution.py
+++ b/solution.py
@@ -9,217 +9,6 @@
 
 epsilon = 1e-05
 MESH = pl.DeviceIdType.MESH
-N_CHUNKS = 10
-
-
-def grads_kernel(n_batch, local_ref, out_ref, g, r0, r1, r2, r3, load_sem, send_sem, recv_sem):
-    b, h = lax.axis_index("batch"), lax.axis_index("height")
-    core, high = lax.rem(h, 2), h // 2
-    low, rest = lax.rem(b, 2), b // 2
-    n_rest = n_batch // 2
-    first = core * low + (1 - core) * high
-    second = core * high + (1 - core) * low
-    core_peer = (b, h + 1 - 2 * core)
-    high_peer = (b, h + 2 - 4 * high)
-    low_peer = (b + 1 - 2 * low, h)
-    first_peer = (
-        core * low_peer[0] + (1 - core) * high_peer[0],
-        core * low_peer[1] + (1 - core) * high_peer[1],
-    )
-    second_peer = (
-        core * high_peer[0] + (1 - core) * low_peer[0],
-        core * high_peer[1] + (1 - core) * low_peer[1],
-    )
-
-    def rest_peer(k):
-        return (lax.rem(rest + k, n_rest) * 2 + low, h)
-
-    def load(c):
-        return pltpu.make_async_copy(local_ref.at[c], g.at[c], load_sem.at[c])
-
-    for c in range(N_CHUNKS):
-        load(c).start()
-    barrier = pltpu.get_barrier_semaphore()
-    for peer in (core_peer, high_peer, low_peer):
-        pl.semaphore_signal(barrier, inc=1, device_id=peer, device_id_type=MESH)
-
-    @pl.loop(1, n_rest)
-    def _(k):
-        pl.semaphore_signal(barrier, inc=1, device_id=rest_peer(k), device_id_type=MESH)
-
-    pl.semaphore_wait(barrier, 3 + n_rest - 1)
-
-    def copy(level, c, source, target, peer):
-        return pltpu.make_async_remote_copy(
-            src_ref=source,
-            dst_ref=target,
-            send_sem=send_sem.at[level, c],
-            recv_sem=recv_sem.at[level, c],
-            device_id=peer,
-            device_id_type=MESH,
-        )
-
-    def hop(level, c):
-        if level == 0:
-            return copy(0, c, g.at[c, 1 - core], r0.at[c], core_peer)
-        if level == 1:
-            return copy(1, c, g.at[c, core, 1 - first], r1.at[c], first_peer)
-        if level == 2:
-            return copy(2, c, g.at[c, core, first, 1 - second], r2.at[c], second_peer)
-        if level == 4:
-            mine = out_ref.at[c, core, high]
-            return copy(4, c, mine, mine, high_peer)
-        both = out_ref.at[c, core]
-        return copy(5, c, both, both, core_peer)
-
-    def add(target, source):
-        target[...] = (target[...].astype(jnp.float32) + source[...].astype(jnp.float32)).astype(
-            jnp.bfloat16
-        )
-
-    def others(c):
-        return r3.at[c, 0 : n_rest - 1]
-
-    @pl.loop(0, N_CHUNKS + 6)
-    def _(step):
-        @pl.when(step < N_CHUNKS)
-        def _():
-            load(step).wait()
-            hop(0, step).start()
-
-        c1 = step - 1
-
-        @pl.when(jnp.logical_and(c1 >= 0, c1 < N_CHUNKS))
-        def _():
-            hop(0, c1).wait_recv()
-
-            @pl.loop(0, 2)
-            def _(i):
-                @pl.loop(0, 2)
-                def _(j):
-                    @pl.loop(0, n_rest)
-                    def _(k):
-                        add(g.at[c1, core, i, j, k], r0.at[c1, i, j, k])
-
-            hop(1, c1).start()
-
-        c2 = step - 2
-
-        @pl.when(jnp.logical_and(c2 >= 0, c2 < N_CHUNKS))
-        def _():
-            hop(1, c2).wait_recv()
-
-            @pl.loop(0, 2)
-            def _(j):
-                @pl.loop(0, n_rest)
-                def _(k):
-                    add(g.at[c2, core, first, j, k], r1.at[c2, j, k])
-
-            hop(2, c2).start()
-
-        c3 = step - 3
-
-        @pl.when(jnp.logical_and(c3 >= 0, c3 < N_CHUNKS))
-        def _():
-            hop(2, c3).wait_recv()
-
-            @pl.loop(0, n_rest)
-            def _(k):
-                add(g.at[c3, core, first, second, k], r2.at[c3, k])
-
-            @pl.loop(1, n_rest)
-            def _(k):
-                copy(
-                    3,
-                    c3,
-                    g.at[c3, core, first, second, lax.rem(rest + k, n_rest)],
-                    r3.at[c3, n_rest - 1 - k],
-                    rest_peer(k),
-                ).start()
-
-        c4 = step - 4
-
-        @pl.when(jnp.logical_and(c4 >= 0, c4 < N_CHUNKS))
-        def _():
-            pltpu.make_async_copy(others(c4), others(c4), recv_sem.at[3, c4]).wait()
-            total = g[c4, core, first, second, rest].astype(jnp.float32)
-            for k in range(n_rest - 1):
-                total = total + r3[c4, k].astype(jnp.float32)
-            out_ref[c4, core, high] = total.astype(jnp.bfloat16)
-            hop(4, c4).start()
-
-        c5 = step - 5
-
-        @pl.when(jnp.logical_and(c5 >= 0, c5 < N_CHUNKS))
-        def _():
-            hop(4, c5).wait_recv()
-            hop(5, c5).start()
-
-        c6 = step - 6
-
-        @pl.when(jnp.logical_and(c6 >= 0, c6 < N_CHUNKS))
-        def _():
-            hop(5, c6).wait_recv()
-            for level in (0, 1, 2, 4, 5):
-                hop(level, c6).wait_send()
-            pltpu.make_async_copy(others(c6), others(c6), send_sem.at[3, c6]).wait()
-
-
-def by_piece(value, n_batch, n_height):
-    lead = value.shape[0] if value.ndim == 3 else 1
-    rows, columns = value.shape[-2:]
-    pieces = value.astype(jnp.bfloat16).reshape(
-        lead, n_batch // 2, 2, rows // n_batch, n_height // 2, 2, columns // (n_height * 128), 128
-    )
-    return jnp.transpose(pieces, (5, 4, 2, 1, 0, 3, 6, 7)).reshape(2, 2, 2, n_batch // 2, -1, 128)
-
-
-def from_piece(piece, shape, n_batch, n_height):
-    lead = shape[0] if len(shape) == 3 else 1
-    rows, columns = shape[-2:]
-    value = piece.reshape(2, 2, lead, rows // n_batch, columns // (n_height * 128), 128)
-    value = jnp.transpose(value, (2, 3, 1, 0, 4, 5)).astype(jnp.float32)
-    return value.reshape(shape[:-2] + (rows // n_batch, columns))
-
-
-def reduce_grads(grads):
-    n_batch, n_height = lax.axis_size("batch"), lax.axis_size("height")
-    shapes = [value.shape for value in grads]
-    pieces = [by_piece(value, n_batch, n_height) for value in grads]
-    counts = [piece.shape[4] for piece in pieces]
-    joined = jnp.concatenate(pieces, axis=4)
-    rows = joined.shape[4] // N_CHUNKS
-    n_rest = n_batch // 2
-    joined = jnp.stack([joined[0], jnp.swapaxes(joined[1], 0, 1)])
-    joined = joined.reshape(2, 2, 2, n_rest, N_CHUNKS, rows, 128)
-    joined = jnp.transpose(joined, (4, 0, 1, 2, 3, 5, 6))
-    summed = pl.pallas_call(
-        functools.partial(grads_kernel, n_batch),
-        out_shape=jax.ShapeDtypeStruct((N_CHUNKS, 2, 2, rows, 128), jnp.bfloat16),
-        in_specs=[pl.BlockSpec(memory_space=pl.ANY)],
-        out_specs=pl.BlockSpec(memory_space=pltpu.VMEM),
-        scratch_shapes=[
-            pltpu.VMEM((N_CHUNKS, 2, 2, 2, n_rest, rows, 128), jnp.bfloat16),
-            pltpu.VMEM((N_CHUNKS, 2, 2, n_rest, rows, 128), jnp.bfloat16),
-            pltpu.VMEM((N_CHUNKS, 2, n_rest, rows, 128), jnp.bfloat16),
-            pltpu.VMEM((N_CHUNKS, n_rest, rows, 128), jnp.bfloat16),
-            pltpu.VMEM((N_CHUNKS, n_rest - 1, rows, 128), jnp.bfloat16),
-            pltpu.SemaphoreType.DMA((N_CHUNKS,)),
-            pltpu.SemaphoreType.DMA((6, N_CHUNKS)),
-            pltpu.SemaphoreType.DMA((6, N_CHUNKS)),
-        ],
-        compiler_params=pltpu.CompilerParams(
-            collective_id=5, has_side_effects=True, vmem_limit_bytes=56 << 20
-        ),
-        name="reduce_grads",
-    )(joined)
-    summed = jnp.transpose(summed, (1, 2, 0, 3, 4)).reshape(2, 2, -1, 128)
-    result, start = [], 0
-    for shape, count in zip(shapes, counts):
-        result.append(from_piece(summed[:, :, start : start + count], shape, n_batch, n_height))
-        start += count
-    return result
-
 
 WIDE = 512
 ROWS = 16
@@ -263,7 +52,7 @@
 
 
 def wide_mask(mask):
-    return jnp.concatenate([mask] * (WIDE // 128), axis=1)
+    return jnp.concatenate([up32(mask)] * (WIDE // 128), axis=1)
 
 
 def grids(heights, widths):
@@ -279,14 +68,13 @@
 
 def main_kernel(
     n_batch, n_height, heights, widths, total_in, total_out,
-    x, reduce_a, spatial_a, expand_a, shortcut_a, reduce_b, spatial_b, expand_b,
+    x_small, x_medium, x_large, reduce_a, spatial_a, expand_a, shortcut_a, reduce_b, spatial_b, expand_b,
     edge_ref, mask_ref, gain_mid, shift_mid, gain_out, shift_out, up_ref,
-    pooled, dx, g_reduce_a, g_spatial_a, g_expand_a, g_shortcut_a, g_reduce_b, g_spatial_b,
-    g_expand_b, mid_sums, out_sums, h1_kept, a1_kept,
+    pooled, dx_small, dx_medium, dx_large, g_units, mid_sums, out_sums, h1_kept, a1_kept,
     big_b, big_a, h3, side, mb, h2, a2, h4, h5, a5, a4p, dhp, acc, wp, wq, w2,
-    halo_a, halo_up, halo_down, halo_in, staged, pool_slots,
+    halo_up, halo_down, halo_in, keep, away, r0, r1, r2, r3, final, ready, pool_slots,
     thin_h, thin_b, wide_h, wide_b, stat_mid, stat_out,
-    w_sem, x_sem, g_sem, dx_sem, spill_sem, ar_send, ar_recv, halo_send, halo_recv, pool_sem,
+    w_sem, x_sem, u_send, u_recv, ready_sem, dx_sem, spill_sem, ar_send, ar_recv, halo_send, halo_recv, pool_sem,
 ):
     b, h = lax.axis_index("batch"), lax.axis_index("height")
     counts, starts, top_total, top_starts, both_total, both_starts, halo_starts = grids(
@@ -296,6 +84,7 @@
     half = total // 2
     groups = range(3)
     h1, dz, h6 = big_b, big_b, big_a
+    halo_a = mb.at[0:2, 0 : sum(widths) * ROWS]
 
     def rows_at(start, count):
         return pl.ds(pl.multiple_of(start * ROWS, ROWS), count * ROWS)
@@ -321,8 +110,45 @@
             for k in range(2):
                 fetch(shortcut_a.at[columns(k), columns(n)], wq.at[2 * n + k], w_sem.at[1])
 
+    xs, dxs = (x_small, x_medium, x_large), (dx_small, dx_medium, dx_large)
+
+    def band_row(buffer, g, y):
+        return buffer.at[pl.ds(starts[g] + y * (widths[g] + 1), widths[g])]
+
+    def by_position(buffer):
+        return buffer.reshape(buffer.shape[0] // ROWS, ROWS, WIDE)
+
+    def fetch_plane(p, k, target, sem):
+        for g in groups:
+            for y in range(heights[g]):
+                fetch(
+                    xs[g].at[y, p // 2, :, p % 2, :, columns(k)],
+                    band_row(by_position(target), g, y),
+                    sem,
+                )
+
+    def plane_arrived(target, sem):
+        pixels = sum(k * o for k, o in zip(heights, widths)) * ROWS
+        arrived(target.at[0:pixels], sem)
+
+    def put_plane(p, k, source):
+        for g in groups:
+            for y in range(heights[g]):
+                fetch(
+                    band_row(by_position(source), g, y),
+                    dxs[g].at[y, p // 2, :, p % 2, :, columns(k)],
+                    dx_sem.at[0],
+                )
+
     for k in range(2):
-        fetch(x.at[:, :, columns(k)], (h3, mb)[k], x_sem.at[k])
+        for p in range(4):
+            for g in groups:
+                for y in range(heights[g]):
+                    edge_place = (starts[g] + y * (widths[g] + 1) + widths[g]) * ROWS
+                    (h3, mb)[k][p, edge_place : edge_place + ROWS] = jnp.zeros(
+                        (ROWS, WIDE), jnp.bfloat16
+                    )
+            fetch_plane(p, k, (h3, mb)[k].at[p], x_sem.at[k])
     for k in range(2):
         fetch(reduce_a.at[columns(k)], w2.at[k], w_sem.at[3])
     fetch_shortcut()
@@ -359,58 +185,60 @@
 
     pl.semaphore_wait(barrier, n_height + n_batch - 2)
 
-    turn = {"thin": 0, "wide": 0}
-
-    def ar_spread(slots, me, count, peer, level, slot, sem):
+    turn = [0]
+
+    def ar_spread(slots, me, count, peer, sems):
         @pl.loop(1, count)
         def _(k):
             pltpu.make_async_remote_copy(
-                src_ref=slots.at[slot, me],
-                dst_ref=slots.at[slot, me],
-                send_sem=ar_send.at[sem, level, slot],
-                recv_sem=ar_recv.at[sem, level, slot],
+                src_ref=slots.at[me],
+                dst_ref=slots.at[me],
+                send_sem=ar_send.at[sems],
+                recv_sem=ar_recv.at[sems],
                 device_id=peer(lax.rem(me + k, count)),
                 device_id_type=MESH,
             ).start()
 
-    def ar_wait(slots, count, level, slot, sem, sems):
-        others = slots.at[slot, 0 : count - 1]
-        pltpu.make_async_copy(others, others, sems.at[sem, level, slot]).wait()
-
-    def sums_start(kind, vectors):
-        slot = turn[kind] % 2
-        turn[kind] += 1
-        if kind == "thin":
-            first, second, sem = thin_h, thin_b, 0
-            for v, vector in enumerate(vectors):
-                for j in range(4):
-                    first[slot, h, 4 * v + j : 4 * v + j + 1, :] = vector[
-                        :, 128 * j : 128 * (j + 1)
-                    ]
-        else:
-            first, second, sem = wide_h, wide_b, 1
-            first[slot, h] = stat_out[...]
-        ar_spread(first, h, n_height, lambda p: (b, p), 0, slot, sem)
-        return first, second, sem, slot
+    def ar_wait(slots, count, sems, which):
+        others = slots.at[0 : count - 1]
+        pltpu.make_async_copy(others, others, which.at[sems]).wait()
+
+    def sums_start(vectors):
+        slot = turn[0] % 2
+        turn[0] += 1
+        first, second = thin_h.at[slot], thin_b.at[slot]
+        for v, vector in enumerate(vectors):
+            for j in range(4):
+                first[h, 4 * v + j : 4 * v + j + 1, :] = vector[:, 128 * j : 128 * (j + 1)]
+        ar_spread(first, h, n_height, lambda p: (b, p), (0, 0, slot))
+        return first, second, 0, slot
+
+    def wide_start(part):
+        count = 16 if part is None else 8
+        rows = pl.ds(8 * (part or 0), count)
+        first, second = wide_h.at[:, rows], wide_b.at[:, rows]
+        first[h] = stat_out[0:count]
+        ar_spread(first, h, n_height, lambda p: (b, p), (1, 0, part or 0))
+        return first, second, 1, part or 0
 
     def sums_middle(state):
-        first, second, sem, slot = state
-        ar_wait(first, n_height, 0, slot, sem, ar_recv)
-        second[slot, b] = jnp.sum(first[slot], axis=0)
-        ar_spread(second, b, n_batch, lambda p: (p, h), 1, slot, sem)
+        first, second, kind, slot = state
+        ar_wait(first, n_height, (kind, 0, slot), ar_recv)
+        second[b] = jnp.sum(first[...], axis=0)
+        ar_spread(second, b, n_batch, lambda p: (p, h), (kind, 1, slot))
 
     def sums_end(state):
-        first, second, sem, slot = state
-        ar_wait(second, n_batch, 1, slot, sem, ar_recv)
-        summed = jnp.sum(second[slot], axis=0)
-        ar_wait(first, n_height, 0, slot, sem, ar_send)
-        ar_wait(second, n_batch, 1, slot, sem, ar_send)
-        if sem == 0:
+        first, second, kind, slot = state
+        ar_wait(second, n_batch, (kind, 1, slot), ar_recv)
+        summed = jnp.sum(second[...], axis=0)
+        ar_wait(first, n_height, (kind, 0, slot), ar_send)
+        ar_wait(second, n_batch, (kind, 1, slot), ar_send)
+        if kind == 0:
             return [
                 jnp.concatenate([summed[4 * v + j : 4 * v + j + 1] for j in range(4)], axis=1)
                 for v in range(2)
             ]
-        stat_out[...] = summed
+        stat_out[0 : summed.shape[0]] = summed
         return None
 
     def keep_stats(kept, index, sums, number, gain, shift):
@@ -490,52 +318,230 @@
             value = value + first_row(source, g, y) * edge(g, y)
         return value
 
-    done = [0]
-
-    def store_tile(index, value, target):
-        slot = lax.rem(index, 2)
-
-        @pl.when(index >= 2)
+    core, high = lax.rem(h, 2), h // 2
+    low_bit, rest = lax.rem(b, 2), b // 2
+    n_rest = n_batch // 2
+    unit_rows = WIDE // n_batch
+
+    def either(is_one, one, zero):
+        return is_one * one + (1 - is_one) * zero
+
+    first, second = either(core, low_bit, high), either(core, high, low_bit)
+    core_peer = (b, h + 1 - 2 * core)
+    high_peer = (b, h + 2 - 4 * high)
+    low_peer = (b + 1 - 2 * low_bit, h)
+    first_peer = [either(core, low_peer[i], high_peer[i]) for i in range(2)]
+    second_peer = [either(core, high_peer[i], low_peer[i]) for i in range(2)]
+
+    def ring(buffer, unit):
+        return lax.rem(unit, buffer.shape[0])
+
+    def unit_copy(level, unit, source, target, peer):
+        return pltpu.make_async_remote_copy(
+            src_ref=source,
+            dst_ref=target,
+            send_sem=u_send.at[level, lax.rem(unit, 16)],
+            recv_sem=u_recv.at[level, lax.rem(unit, 16)],
+            device_id=tuple(peer),
+            device_id_type=MESH,
+        )
+
+    def hop(level, unit):
+        kept = keep.at[ring(keep, unit)]
+        if level == 0:
+            return unit_copy(
+                0, unit, away.at[ring(away, unit)], r0.at[ring(r0, unit)], core_peer
+            )
+        if level == 1:
+            return unit_copy(1, unit, kept.at[1 - first], r1.at[ring(r1, unit)], first_peer)
+        if level == 2:
+            return unit_copy(
+                2, unit, kept.at[first, 1 - second], r2.at[ring(r2, unit)], second_peer
+            )
+        if level == 4:
+            mine = final.at[ring(final, unit), core, high]
+            return unit_copy(4, unit, mine, mine, high_peer)
+        both = final.at[ring(final, unit), core]
+        return unit_copy(5, unit, both, both, core_peer)
+
+    def add_to(target, source):
+        target[...] = low(up32(target[...]) + up32(source[...]))
+
+    def rest_wait(unit, sems):
+        others = r3.at[ring(r3, unit)]
+        pltpu.make_async_copy(others, others, sems.at[3, lax.rem(unit, 16)]).wait()
+
+    def round_0(unit):
+        hop(0, unit).start()
+
+    def round_1(unit):
+        hop(0, unit).wait()
+        kept, got = keep.at[ring(keep, unit)], r0.at[ring(r0, unit)]
+
+        @pl.loop(0, n_rest)
+        def _(k):
+            for i in range(2):
+                for j in range(2):
+                    add_to(kept.at[i, j, k], got.at[i, j, k])
+
+        hop(1, unit).start()
+
+    def round_2(unit):
+        hop(1, unit).wait_recv()
+        kept, got = keep.at[ring(keep, unit), first], r1.at[ring(r1, unit)]
+
+        @pl.loop(0, n_rest)
+        def _(k):
+            for j in range(2):
+                add_to(kept.at[j, k], got.at[j, k])
+
+        hop(2, unit).start()
+
+    def round_3(unit):
+        hop(2, unit).wait_recv()
+        kept, got = keep.at[ring(keep, unit), first, second], r2.at[ring(r2, unit)]
+
+        @pl.loop(0, n_rest)
+        def _(k):
+            add_to(kept.at[k], got.at[k])
+
+        @pl.loop(1, n_rest)
+        def _(k):
+            unit_copy(
+                3,
+                unit,
+                kept.at[lax.rem(rest + k, n_rest)],
+                r3.at[ring(r3, unit), n_rest - 1 - k],
+                (lax.rem(rest + k, n_rest) * 2 + low_bit, h),
+            ).start()
+
+    def round_4(unit):
+        rest_wait(unit, u_recv)
+        value = up32(keep[ring(keep, unit), first, second, rest])
+        for k in range(n_rest - 1):
+            value = value + up32(r3[ring(r3, unit), k])
+        final[ring(final, unit), core, high] = low(value)
+        hop(4, unit).start()
+
+    def round_5(unit):
+        hop(4, unit).wait_recv()
+        hop(5, unit).start()
+
+    def round_6(unit):
+        hop(5, unit).wait_recv()
+        for level in (1, 2, 4, 5):
+            hop(level, unit).wait_send()
+        rest_wait(unit, u_send)
+        slot = ring(ready, unit)
+
+        @pl.when(unit >= ready.shape[0])
         def _():
-            arrived(staged.at[slot], g_sem.at[slot])
-
-        staged[slot] = low(value)
-        fetch(staged.at[slot], target, g_sem.at[slot])
-
-    def store_tiles(count, value_of, target_of):
-        first = done[0]
-        done[0] += count
+            arrived(ready.at[slot], ready_sem.at[slot])
+
+        for c in range(2):
+            for i in range(2):
+                lane = 128 * (2 * c + i)
+                ready[slot, :, lane : lane + 128] = up32(final[ring(final, unit), c, i])
+        fetch(ready.at[slot], g_units.at[unit], ready_sem.at[slot])
+
+    rounds = (
+        (0, round_0), (2, round_1), (4, round_2), (5, round_3), (7, round_4), (8, round_5),
+        (10, round_6),
+    )
+    clock, made, produced = [0], [0], []
+
+    def advance(index, base, count):
+        for lag, act in rounds:
+            for start, size, unit in produced:
+                from_, to = max(base - lag, start), min(base - lag + count, start + size)
+                if from_ >= to:
+                    continue
+                target = base - lag - start + unit + index
+                if to - from_ == count:
+                    act(target)
+                else:
+                    shift = base - lag
+                    inside = jnp.logical_and(index >= from_ - shift, index < to - shift)
+                    pl.when(inside)(functools.partial(act, target))
+
+    def idle(count):
+        base = clock[0]
+        clock[0] += count
+
+        @pl.loop(0, count)
+        def _(i):
+            advance(i, base, count)
+
+    def ticks(count):
+        base = clock[0]
+        clock[0] += count
+        return lambda i: advance(i, base, count)
+
+    def put(value, unit, units, first_shard):
+        shard_rows = units * unit_rows
+        own_side = core == 0
+        left, right = low(value[:, : WIDE // 2]), low(value[:, WIDE // 2 :])
+        own, other = jnp.where(own_side, left, right), jnp.where(own_side, right, left)
+        for s in range(WIDE // shard_rows):
+            shard = first_shard + s
+            shard_low, shard_rest = s % 2, shard // 2
+            for q in range(units):
+                rows = slice(s * shard_rows + q * unit_rows, s * shard_rows + (q + 1) * unit_rows)
+                for i in range(2):
+                    lanes = slice(128 * i, 128 * (i + 1))
+                    keep[
+                        ring(keep, unit + q),
+                        either(core, shard_low, i),
+                        either(core, i, shard_low),
+                        shard_rest,
+                    ] = own[rows, lanes]
+                    away[
+                        ring(away, unit + q),
+                        either(core, i, shard_low),
+                        either(core, shard_low, i),
+                        shard_rest,
+                    ] = other[rows, lanes]
+
+    def produce(count, units, make):
+        base, unit = clock[0], made[0]
+        produced.append((base, count * units, unit))
+        clock[0] += count * units
+        made[0] += count * units
 
         @pl.loop(0, count)
         def _(t):
-            store_tile(first + t, value_of(t), target_of(t))
-
-    def wide_rows(reference, t):
-        return reference.at[pl.ds(pl.multiple_of(t * WIDE, WIDE), WIDE)]
-
-    def wide_columns(reference, t):
-        return reference.at[:, pl.ds(pl.multiple_of(t * WIDE, WIDE), WIDE)]
+            make(t, unit + t * units)
+            if units == 1:
+                advance(t, base, count)
+            else:
+
+                @pl.loop(0, units)
+                def _(q):
+                    advance(t * units + q, base, count * units)
 
     zero8 = jnp.zeros((8, WIDE), jnp.float32)
 
     arrived(w2, w_sem.at[3])
     for k in range(2):
-        arrived((h3, mb)[k], x_sem.at[k])
+        for p in range(4):
+            plane_arrived((h3, mb)[k].at[p], x_sem.at[k])
 
     def first_reduction(i, carry):
         p = i // 2
         rows = pl.ds(pl.multiple_of(lax.rem(i, 2) * half, ROWS), half)
         value = times(h3[p, rows], w2[0]) + times(mb[p, rows], w2[1])
+        value = value * wide_mask(mask_ref[rows])
         h1[p, rows] = low(value)
         return carry[0] + fold(value), carry[1] + fold(value * value)
 
     sums = lax.fori_loop(0, 8, first_reduction, (zero8, zero8))
-    state = sums_start("thin", [one_row(v) for v in sums])
+    state = sums_start([one_row(v) for v in sums])
 
     arrived(wq, w_sem.at[1])
 
     def shortcut_product(n, carry):
         value = times(h3[0], wq[2 * n]) + times(mb[0], wq[2 * n + 1])
+        value = value * wide_mask(mask_ref[...])
         side[n] = low(value)
         stat_out[pl.ds(8 + n, 1)] = one_row(fold(value))
         stat_out[pl.ds(12 + n, 1)] = one_row(fold(value * value))
@@ -601,11 +607,15 @@
         def _(i):
             acc[steps(i)] = jnp.zeros((STEP, WIDE), jnp.float32)
 
-    def conv_taps(first, last, window_of, product):
-        @pl.loop(first, last)
+    def conv_taps(start, last, window_of, product):
+        tick = ticks(last - start) if produced else None
+
+        @pl.loop(start, last)
         def _(t):
             for g in groups:
                 acc[group_rows(g)] += product(window_of(g, t // 3, lax.rem(t, 3)), wp[t])
+            if tick is not None:
+                tick(t - start)
 
     def masked_sums(target):
         def body(i, carry):
@@ -622,7 +632,7 @@
     halo_wait(halo_a, halo_recv, 0, h > 0)
     conv_taps(0, 3, window_a, times)
     sums = masked_sums(h2)
-    state = sums_start("thin", [one_row(v) for v in sums])
+    state = sums_start([one_row(v) for v in sums])
     fetch(spatial_b, wp, w_sem.at[0])
     fetch(big_a, a1_kept, spill_sem.at[1])
     halo_wait(halo_a, halo_send, 0, h < n_height - 1)
@@ -651,7 +661,7 @@
             stat_out[pl.ds(4 + n, 1)] = one_row(fold(value * value))
 
     expansion(a2, h3)
-    state = sums_start("wide", None)
+    state = wide_start(None)
     fetch_columns(expand_b, wq, 0, w_sem.at[1])
     sums_middle(state)
     sums_end(state)
@@ -704,7 +714,7 @@
         return lax.fori_loop(0, total // STEP, body, (zero8, zero8))
 
     sums = plain_sums(h4)
-    state = sums_start("thin", [one_row(v) for v in sums])
+    state = sums_start([one_row(v) for v in sums])
     sums_middle(state)
     clear_acc()
     sums = sums_end(state)
@@ -748,7 +758,7 @@
     conv_taps(0, 3, window_b, times)
     conv_taps(6, 9, window_b, times)
     sums = masked_sums(h5)
-    state = sums_start("thin", [one_row(v) for v in sums])
+    state = sums_start([one_row(v) for v in sums])
     halo_wait(halo_down, halo_send, 1, h < n_height - 1)
     halo_wait(halo_up, halo_send, 2, h > 0)
     sums_middle(state)
@@ -759,9 +769,7 @@
     arrived(wq.at[0:4], w_sem.at[1])
     arrived(big_a, spill_sem.at[1])
     expansion(a5, h6)
-    for row in range(8, 16):
-        stat_out[row : row + 1] = jnp.zeros((1, WIDE), jnp.float32)
-    state = sums_start("wide", None)
+    state = wide_start(0)
     sums_middle(state)
     arrived(h1, spill_sem.at[0])
     sums_end(state)
@@ -776,6 +784,7 @@
         zero = jnp.zeros((ROWS, WIDE), jnp.float32)
         total_grad, total_dot = zero, zero
         for g in groups:
+            share = 1.0 / (widths[g] * widths[g])
 
             def body(i, carry):
                 rows = rows_at(starts[g] + i, 1)
@@ -783,7 +792,7 @@
                 mask = wide_mask(mask_ref[rows])
                 z = value * scale + offset + up32(mb[n, rows])
                 s = sigmoid(z)
-                grad = up_ref[g, n] * (s * (1.0 + z * (1.0 - s))) * mask
+                grad = up32(up_ref[g, n]) * (s * (1.0 + z * (1.0 - s))) * (mask * share)
                 dz[n, rows] = low(grad)
                 return (
                     carry[0] + z * s * mask,
@@ -798,7 +807,7 @@
         stat_out[pl.ds(n, 1)] = one_row(fold(total_grad))
         stat_out[pl.ds(4 + n, 1)] = one_row(fold(total_dot))
 
-    state = sums_start("wide", None)
+    state = wide_start(1)
 
     for k in range(1, n_height):
         pltpu.make_async_remote_copy(
@@ -855,12 +864,10 @@
             acc[rows] += times_t(grad, wq[n])
 
     sums = mid_gradient(h5, 3)
-    state = sums_start("thin", sums)
+    state = sums_start(sums)
     fetch_columns(expand_a, wq, 0, w_sem.at[1])
     sums_middle(state)
-    store_tiles(
-        4, lambda t: t_times(a5[...], h6[t, 0:total]), lambda t: wide_columns(g_expand_b, t)
-    )
+    produce(4, 1, lambda t, unit: put(t_times(a5[...], h6[t, 0:total]), unit, 1, 0))
     fetch(a1_kept, big_a, spill_sem.at[1])
     sums = sums_end(state)
 
@@ -896,7 +903,7 @@
     conv_taps(6, 9, window_b_back, times_t)
     fetch(spatial_a, wp, w_sem.at[0])
     sums = mid_gradient(h4, 2)
-    state = sums_start("thin", sums)
+    state = sums_start(sums)
     halo_wait(halo_down, halo_send, 1, h < n_height - 1)
     halo_wait(halo_up, halo_send, 2, h > 0)
     sums_middle(state)
@@ -910,15 +917,19 @@
 
         return value_of
 
-    store_tiles(9, spatial_tile(window_b, h5), lambda t: g_spatial_b.at[t])
+    tile_b = spatial_tile(window_b, h5)
+    produce(9, 1, lambda t, unit: put(tile_b(t), unit, 1, 0))
     sums = sums_end(state)
 
     mid_step(h4, mid_back(2, 2, sums, total_out), None)
-    fetch(x.at[0, :, columns(1)], a4p.at[0:total], x_sem.at[1])
+    fetch_plane(0, 1, a4p, x_sem.at[1])
+
+    tick = ticks(8)
 
     @pl.loop(0, 4)
     def _(n):
         def body(i, carry):
+            tick(2 * n + i)
             rows = pl.ds(pl.multiple_of(i * half, ROWS), half)
             grad = times_t(h4[rows], wq[4 + n]) + up32(dz[n, rows])
             z = joint(n, rows)
@@ -937,16 +948,22 @@
         for v in range(3):
             stat_out[pl.ds(4 * v + n, 1)] = one_row(sums[v])
 
-    state = sums_start("wide", None)
+    state = wide_start(None)
     sums_middle(state)
-    store_tiles(
-        4, lambda t: t_times(mb[t], h4[...]), lambda t: wide_rows(g_reduce_b, t)
-    )
-    fetch(x.at[:, :, columns(0)], mb, x_sem.at[0])
+
+    def tile_reduce_b(step, unit):
+        @pl.loop(0, 4)
+        def _(t):
+            put(t_times(mb[t], h4[...]), unit, 4, t * (n_batch // 4))
+
+    produce(1, 4, tile_reduce_b)
+    for p in range(4):
+        fetch_plane(p, 0, mb.at[p], x_sem.at[0])
     clear_acc()
     sums_end(state)
 
     arrived(wq.at[0:4], w_sem.at[1])
+    tick_11 = ticks(8)
 
     @pl.loop(0, 4)
     def _(n):
@@ -955,6 +972,7 @@
 
         @pl.loop(0, 2)
         def _(i):
+            tick_11(2 * n + i)
             rows = pl.ds(pl.multiple_of(i * half, ROWS), half)
             grad_in = up32(dz[n, rows])
             mask = wide_mask(mask_ref[rows])
@@ -967,21 +985,18 @@
     fetch(h1_kept, h1, spill_sem.at[0])
     fetch_shortcut()
     sums = mid_gradient(h2, 1)
-    state = sums_start("thin", sums)
+    state = sums_start(sums)
     sums_middle(state)
-    store_tiles(4, lambda t: t_times(a2[...], h3[t]), lambda t: wide_columns(g_expand_a, t))
-    arrived(mb, x_sem.at[0])
-    arrived(a4p.at[0:total], x_sem.at[1])
-    store_tiles(
-        4,
-        lambda t: t_times(mb[0], side[t]),
-        lambda t: wide_columns(g_shortcut_a.at[0:WIDE], t),
-    )
-    store_tiles(
-        4,
-        lambda t: t_times(a4p[0:total], side[t]),
-        lambda t: wide_columns(g_shortcut_a.at[WIDE : 2 * WIDE], t),
-    )
+    produce(4, 1, lambda t, unit: put(t_times(a2[...], h3[t]), unit, 1, 0))
+    for p in range(4):
+        plane_arrived(mb.at[p], x_sem.at[0])
+    plane_arrived(a4p, x_sem.at[1])
+
+    def tile_shortcut(t, unit):
+        put(t_times(mb[0], side[t]), unit, 2, 0)
+        put(t_times(a4p[0:total], side[t]), unit, 2, n_batch // 2)
+
+    produce(4, 2, tile_shortcut)
     sums = sums_end(state)
 
     mid_step(h2, mid_back(1, 1, sums, total_out), dhp)
@@ -1018,12 +1033,15 @@
             return carry[0] + fold(grad), carry[1] + fold(grad * (value * root + back))
 
         carry = lax.fori_loop(0, total // STEP, body, carry)
-    state = sums_start("thin", [one_row(v) for v in carry])
+        idle(2)
+    state = sums_start([one_row(v) for v in carry])
     halo_wait(halo_up, halo_send, 2, h > 0)
     sums_middle(state)
     arrived(big_a, spill_sem.at[1])
-    store_tiles(9, spatial_tile(window_a, h2), lambda t: g_spatial_a.at[t])
-    fetch(x.at[:, :, columns(1)], big_a.at[:, 0:total], x_sem.at[1])
+    tile_a = spatial_tile(window_a, h2)
+    produce(9, 1, lambda t, unit: put(tile_a(t), unit, 1, 0))
+    for p in range(4):
+        fetch_plane(p, 1, big_a.at[p], x_sem.at[1])
     sums = sums_end(state)
 
     main, slope, constant = mid_back(0, 0, sums, total_in)
@@ -1036,8 +1054,23 @@
             grad = main * up32(h3[p, rows]) + slope * up32(h1[p, rows]) + constant
             h1[p, rows] = low(grad * wide_mask(mask_ref[rows]))
 
+    for p in range(4):
+        plane_arrived(big_a.at[p], x_sem.at[1])
+
+    def last_tile(chunk):
+        value = t_times(chunk(0), h1[0])
+        for p in range(1, 4):
+            value = value + t_times(chunk(p), h1[p])
+        return value
+
+    def tile_reduce_a(step, unit):
+        put(last_tile(lambda p: mb[p]), unit, 2, 0)
+        put(last_tile(lambda p: big_a[p, 0:total]), unit, 2, n_batch // 2)
+
+    produce(1, 2, tile_reduce_a)
     arrived(wq, w_sem.at[1])
     for k in range(2):
+        tick_13 = ticks(2)
 
         @pl.loop(0, 2)
         def _(i):
@@ -1049,33 +1082,21 @@
                 h3[0, rows] = low(value)
             else:
                 a4p[rows] = low(value)
-
-    fetch(h3.at[0], dx.at[0, :, columns(0)], dx_sem.at[0])
-    fetch(a4p.at[0:total], dx.at[0, :, columns(1)], dx_sem.at[0])
+            tick_13(i)
+
+    put_plane(0, 0, h3.at[0])
+    put_plane(0, 1, a4p)
+    tick_13p = ticks(3)
 
     @pl.loop(1, 4)
     def _(p):
         h3[p] = low(times_t(h1[p], w2[0]))
         side[p] = low(times_t(h1[p], w2[1]))
-        fetch(h3.at[p], dx.at[p, :, columns(0)], dx_sem.at[0])
-        fetch(side.at[p], dx.at[p, :, columns(1)], dx_sem.at[0])
-
-    arrived(big_a.at[:, 0:total], x_sem.at[1])
-
-    def last_tile(chunk):
-        def value_of(t):
-            value = t_times(chunk(0), h1[0])
-            for p in range(1, 4):
-                value = value + t_times(chunk(p), h1[p])
-            return value
-
-        return value_of
-
-    store_tiles(1, last_tile(lambda p: mb[p]), lambda t: g_reduce_a.at[0:WIDE])
-    store_tiles(
-        1, last_tile(lambda p: big_a[p, 0:total]), lambda t: g_reduce_a.at[WIDE : 2 * WIDE]
-    )
-
+        put_plane(p, 0, h3.at[p])
+        put_plane(p, 1, side.at[p])
+        tick_13p(p - 1)
+
+    idle(rounds[-1][0] - 6)
     others = pool_slots.at[0 : n_height - 1]
     pltpu.make_async_copy(others, others, pool_sem.at[1]).wait()
     pltpu.make_async_copy(others, others, pool_sem.at[0]).wait()
@@ -1087,27 +1108,23 @@
                 value = part if value is None else value + part
             pooled[g, n] = value * (1.0 / (widths[g] * widths[g]))
 
-    for slot in range(2):
-        arrived(staged.at[slot], g_sem.at[slot])
-    arrived(h3, dx_sem.at[0])
-    arrived(h3, dx_sem.at[0])
-
-
-def to_planes(image, live, images):
+    for slot in range(ready.shape[0]):
+        arrived(ready.at[slot], ready_sem.at[slot])
+    for p in range(8):
+        plane_arrived(a4p, dx_sem.at[0])
+
+
+def to_planes(image):
     count, rows, cols, channels = image.shape
-    value = image.reshape(count, rows // 2, 2, cols // 2, 2, channels)
-    value = jnp.transpose(value, (2, 4, 1, 3, 0, 5))
-    keep = (jnp.arange(rows // 2, dtype=jnp.int32) < live)[None, None, :, None, None, None]
-    value = jnp.where(keep, value, jnp.zeros((), value.dtype))
-    value = jnp.pad(value, ((0, 0), (0, 0), (0, 0), (0, 1), (0, images - count), (0, 0)))
-    return value.reshape(4, -1, channels)
+    value = jnp.pad(image, ((0, ROWS - count), (0, 0), (0, 0), (0, 0)))
+    value = jnp.transpose(value, (1, 2, 0, 3))
+    return value.reshape(rows // 2, 2, cols // 2, 2, ROWS, channels)
 
 
 def from_planes(planes, shape):
     count, rows, cols, channels = shape
-    value = planes.reshape(2, 2, rows // 2, cols // 2 + 1, -1, channels)
-    value = value[:, :, :, : cols // 2, :count]
-    return jnp.transpose(value, (4, 2, 0, 3, 1, 5)).reshape(shape)
+    value = planes.reshape(rows, cols, ROWS, channels)[:, :, :count]
+    return jnp.transpose(value, (2, 0, 1, 3))
 
 
 def per_device(
@@ -1125,29 +1142,26 @@
     pixels = sum(o * o for o in widths) * count * n_batch
     counts, starts, top_total, _, both_total, _, _ = grids(heights, widths)
     total = sum(counts) * ROWS
-    x = jnp.concatenate([to_planes(images[g], live[g], ROWS) for g in range(3)], axis=1)
+    planes = [to_planes(image) for image in images]
     masks = []
     for g in range(3):
         row_ok = (jnp.arange(heights[g], dtype=jnp.int32) < live[g])[:, None, None]
         column_ok = (jnp.arange(widths[g] + 1) < widths[g])[None, :, None]
         image_ok = (jnp.arange(ROWS) < count)[None, None, :]
         masks.append(jnp.logical_and(jnp.logical_and(row_ok, column_ok), image_ok).reshape(-1))
-    mask = jnp.concatenate(masks).astype(jnp.float32)
+    mask = jnp.concatenate(masks).astype(jnp.bfloat16)
     mask = jnp.broadcast_to(mask[:, None], (total, 128))
     edges = (jnp.arange(max(heights))[None, :] == live[:, None] - 1).astype(jnp.float32)
     edges = jnp.broadcast_to(edges[:, :, None, None], edges.shape + (8, 128))
-    up = jnp.stack(
-        [
-            jnp.pad(
-                upstreams[g].astype(jnp.float32) / (widths[g] * widths[g]),
-                ((0, ROWS - count), (0, 0)),
-            )
-            for g in range(3)
-        ]
-    )
+    up = jnp.stack([jnp.pad(value, ((0, ROWS - count), (0, 0))) for value in upstreams])
     up = jnp.transpose(up.reshape(3, ROWS, 4, WIDE), (0, 2, 1, 3))
     halo = sum(widths) * ROWS
     bf, f32 = jnp.bfloat16, jnp.float32
+    unit_rows, n_rest = WIDE // n_batch, n_batch // 2
+    n_units = sum(
+        w.size for w in (reduce_a, first_spatial_weight, expand_a, shortcut_a, reduce_b,
+                         second_spatial_weight, expand_b)
+    ) // (WIDE * WIDE)
     dma = pltpu.SemaphoreType.DMA
     vmem = pl.BlockSpec(memory_space=pltpu.VMEM)
     anywhere = pl.BlockSpec(memory_space=pl.ANY)
@@ -1161,21 +1175,15 @@
         ),
         out_shape=[
             jax.ShapeDtypeStruct((3, 4, ROWS, WIDE), f32),
-            jax.ShapeDtypeStruct(x.shape, bf),
-            jax.ShapeDtypeStruct(reduce_a.shape, bf),
-            jax.ShapeDtypeStruct(flat_a.shape, bf),
-            jax.ShapeDtypeStruct(expand_a.shape, bf),
-            jax.ShapeDtypeStruct(shortcut_a.shape, bf),
-            jax.ShapeDtypeStruct(reduce_b.shape, bf),
-            jax.ShapeDtypeStruct(flat_b.shape, bf),
-            jax.ShapeDtypeStruct(expand_b.shape, bf),
+            *[jax.ShapeDtypeStruct(value.shape, bf) for value in planes],
+            jax.ShapeDtypeStruct((n_units, unit_rows, WIDE), f32),
             jax.ShapeDtypeStruct((4, 2, WIDE), f32),
             jax.ShapeDtypeStruct((3, 2, 4, WIDE), f32),
             jax.ShapeDtypeStruct((4, total, WIDE), bf),
             jax.ShapeDtypeStruct((4, top_total * ROWS, WIDE), bf),
         ],
-        in_specs=[anywhere] * 8 + [vmem] * 7,
-        out_specs=[vmem] + [anywhere] * 8 + [vmem] * 2 + [anywhere] * 2,
+        in_specs=[anywhere] * 10 + [vmem] * 7,
+        out_specs=[vmem] + [anywhere] * 4 + [vmem] * 2 + [anywhere] * 2,
         scratch_shapes=[
             big,
             pltpu.VMEM((4, top_total * ROWS, WIDE), bf),
@@ -1187,19 +1195,25 @@
             pltpu.VMEM((9, WIDE, WIDE), bf),
             pltpu.VMEM((8, WIDE, WIDE), bf),
             pltpu.VMEM((2, WIDE, WIDE), bf),
-            pltpu.VMEM((2, halo, WIDE), bf),
             pltpu.VMEM((halo, WIDE), bf),
             pltpu.VMEM((halo, WIDE), bf),
             pltpu.VMEM((halo, WIDE), bf),
-            pltpu.VMEM((2, WIDE, WIDE), bf),
+            pltpu.VMEM((12, 2, 2, n_rest, unit_rows, 128), bf),
+            pltpu.VMEM((5, 2, 2, n_rest, unit_rows, 128), bf),
+            pltpu.VMEM((6, 2, 2, n_rest, unit_rows, 128), bf),
+            pltpu.VMEM((6, 2, n_rest, unit_rows, 128), bf),
+            pltpu.VMEM((6, n_rest, unit_rows, 128), bf),
+            pltpu.VMEM((6, n_rest - 1, unit_rows, 128), bf),
+            pltpu.VMEM((8, 2, 2, unit_rows, 128), bf),
+            pltpu.VMEM((3, unit_rows, WIDE), f32),
             pltpu.VMEM((n_height, 4, 3 * ROWS, WIDE), bf),
             pltpu.VMEM((2, n_height, 8, 128), f32),
             pltpu.VMEM((2, n_batch, 8, 128), f32),
-            pltpu.VMEM((2, n_height, 16, WIDE), f32),
-            pltpu.VMEM((2, n_batch, 16, WIDE), f32),
+            pltpu.VMEM((n_height, 16, WIDE), f32),
+            pltpu.VMEM((n_batch, 16, WIDE), f32),
             pltpu.VMEM((16, 8, WIDE), f32),
             pltpu.VMEM((16, WIDE), f32),
-            dma((4,)), dma((2,)), dma((2,)), dma((1,)), dma((2,)),
+            dma((4,)), dma((2,)), dma((6, 16)), dma((6, 16)), dma((3,)), dma((1,)), dma((2,)),
             dma((2, 2, 2)), dma((2, 2, 2)), dma((3,)), dma((3,)), dma((2,)),
         ],
         compiler_params=pltpu.CompilerParams(
@@ -1207,23 +1221,40 @@
         ),
         name="both_blocks",
     )(
-        x, reduce_a, flat_a, expand_a, shortcut_a, reduce_b, flat_b, expand_b,
+        *planes, reduce_a, flat_a, expand_a, shortcut_a, reduce_b, flat_b, expand_b,
         edges, mask, gain_mid, shift_mid,
         gain_out.reshape(3, 4, WIDE), shift_out.reshape(3, 4, WIDE), up,
     )
     pooled = jnp.transpose(results[0], (0, 2, 1, 3)).reshape(3, ROWS, -1)[:, :count]
-    backs = [
-        from_planes(
-            results[1][:, starts[g] * ROWS : (starts[g] + counts[g]) * ROWS], images[g].shape
-        )
-        for g in range(3)
-    ]
-    shards = reduce_grads(results[2:9])
-    for place in (1, 5):
-        shards[place] = shards[place].reshape((3, 3) + shards[place].shape[1:])
-    mid, out = results[9], results[10].reshape(3, 2, -1)
+    backs = [from_planes(results[1 + g], images[g].shape) for g in range(3)]
+    units, place, shards = results[4], 0, {}
+    for name, shape in (
+        ("expand_b", expand_b.shape),
+        ("spatial_b", second_spatial_weight.shape),
+        ("reduce_b", reduce_b.shape),
+        ("expand_a", expand_a.shape),
+        ("shortcut_a", shortcut_a.shape),
+        ("spatial_a", first_spatial_weight.shape),
+        ("reduce_a", reduce_a.shape),
+    ):
+        lead = shape[:-2]
+        count_units = shape[-2] * shape[-1] // (WIDE * WIDE)
+        for size in lead:
+            count_units *= size
+        value = units[place : place + count_units]
+        place += count_units
+        rows = shape[-2] // n_batch
+        if lead:
+            shards[name] = value.reshape(lead + (rows, WIDE))
+        else:
+            value = value.reshape(shape[1] // WIDE, rows, WIDE)
+            shards[name] = jnp.transpose(value, (1, 0, 2)).reshape(rows, shape[1])
+    order = (
+        "reduce_a", "spatial_a", "expand_a", "shortcut_a", "reduce_b", "spatial_b", "expand_b"
+    )
+    mid, out = results[5], results[6].reshape(3, 2, -1)
     return (
-        pooled[0], pooled[1], pooled[2], backs[0], backs[1], backs[2], *shards,
+        pooled[0], pooled[1], pooled[2], backs[0], backs[1], backs[2], *[shards[name] for name in order],
         mid[:, 1], mid[:, 0], out[:, 1], out[:, 0],
     )
 

time: 562 us -> 415 us (0.74)
  local copies, waits for them, and re-layouts: 138 us -> 44.9 us
  other arithmetic: 30.7 us -> 4.08 us
  Pallas kernels: 382 us -> 358 us
    pallas_call x1 -> x0, Pallas kernels: 121 us -> none  [reduce_grads(): pl.pallas_call(functools.partial(grads_kernel, n_batch), out_shape=jax.Sh...]
    pallas_call x1, Pallas kernels: 261 us -> 358 us  [per_device(): pl.pallas_call(functools.partial(main_kernel, n_batch, n_height, heights,...]
    reshape x27 -> x4, local copies, waits for them, and re-layouts: 76.4 us -> 2.79 us  [the longest x3 2.73 us: per_device(): shards[name] = jnp.transpose(value, (1, 0, 2)).reshape(rows, shape[1])]
    concatenate x1 -> x0, other arithmetic: 10.6 us -> none  [per_device(): jnp.concatenate([to_planes(images[g], live[g], ROWS) for g in range(3)],...]
    slice x6 -> x4, local copies, waits for them, and re-layouts: 15.8 us -> 6.96 us  [the longest x3 6.44 us: per_device(): value = units[place:place + count_units]]
    another operation x10 -> x6, local copies, waits for them, and re-layouts: 8.29 us -> 0.15 us  [per_device(): jnp.stack([jnp.pad(value, ((0, ROWS - count), (0, 0))) for value in upstr...]
    select_n x3 -> x0, other arithmetic: 7.91 us -> none  [to_planes(): value = jnp.where(keep, value, jnp.zeros((), value.dtype))]
    transpose x1 -> x0, other arithmetic: 7.25 us -> none  [reduce_grads(): joined = jnp.transpose(joined, (4, 0, 1, 2, 3, 5, 6))]
where the time goes in v4:
time: 415 us; the launch traced here: 408 us
  Pallas kernels  358 us (86%)
  local copies, waits for them, and re-layouts  44.9 us (11%)
    pallas_call x1, Pallas kernels, per_device(): pl.pallas_call(functools.partial(main_kernel, n_batch, n_height, heights,...  358 us
    transpose x6, local copies, waits for them, and re-layouts, to_planes(): value = jnp.transpose(value, (1, 2, 0, 3))  12.6 us
    unnamed x19, local copies, waits for them, and re-layouts  12.4 us

profile of v4, /device:TPU:0, one launch (start us, length us, event | category | flops | bytes accessed | tf_op | source)
XLA Modules:
  0.0 408.2 jit_solution(15669357177462802035)
XLA Ops:
  0.7 0.9 add_reduce_fusion
  5.0 1.4 reshape.293.gain_out
  6.4 1.4 reshape.294.shift_out
  8.5 0.8 pad.25
  9.4 0.9 pad.26
  10.3 1.0 pad.27
  12.1 0.9 broadcast_in_dim.5.mask_ref
  13.0 1.8 pad_bitcast_fusion.2
  14.8 1.8 copy.44
  17.2 3.1 copy.45
  20.9 4.8 %copy.46 = bf16[8,18,16,1024]{3,2,1,0:T(8,128)(2,1)} copy(bf16[8,18,16,1024]{3,0,1,2:T(8,128)(2,1)S(1)} %pad_bitcast_fusion) | data formatting | bytes 9437184 | tf_op jit(solution)/shard_map/transpose | solution.py:1120
  25.7 357.9 %both_blocks.1 = (f32[3,4,16,512]{3,2,1,0:T(8,128)}, bf16[2,2,5,2,16,1024]{5,4,3,2,1,0:T(8,128)(2,1)}, bf16[3,2,7,2,16,1024]{5,4,3,2,1,0:T(8,128)(2,1)}, bf16[4,...) custom-call(bf16[2,2,5,2,16,1024]{5,4,3,2,1,0:T(8,128)(2,1)} %bitcas, ...), custom_call_target="tpu_custom_call" | custom-call | tf_op jit(solution)/shard_map/both_blocks/pallas_call | solution.py:1172
  383.6 1.0 copy.66
  384.7 3.0 copy.79
  387.7 0.8 slice_bitcast_fusion.2
  389.8 1.7 slice.76
  391.5 1.3 slice.79
  392.8 1.1 copy.68
  393.9 2.5 slice_bitcast_fusion
  396.3 3.5 fusion.1
  399.8 0.8 copy.69
  400.6 0.8 copy.67
  401.5 2.5 copy.78
  404.0 3.7 copy.77
  (50 shorter events, 7.4 us)
Async XLA Ops:
  10.2 6.4 %copy-start.2 = (bf16[12,6,14,1024]{3,2,1,0:T(8,128)(2,1)S(1)}, bf16[12,6,14,1024]{3,2,1,0:T(8,128)(2,1)}, u32[]{:S(2)}) copy-start(bf16[12,6,14,1024]{3,2,1,0:T(8,128)(2,1)} %param.19) | copy-start | bytes 6193156
  17.2 3.2 copy-start
  383.6 4.8 %copy-start.4 = (f32[4,2,512]{2,1,0:T(2,128)S(1)}, f32[4,2,512]{2,1,0:T(2,128)}, u32[]{:S(2)}) copy-start(f32[4,2,512]{2,1,0:T(2,128)} %get-tuple-element.29) | copy-start | bytes 49156
  383.6 5.5 %copy-start.3 = (f32[3,2,4,512]{3,2,1,0:T(4,128)S(1)}, f32[3,2,4,512]{3,2,1,0:T(4,128)}, u32[]{:S(2)}) copy-start(f32[3,2,4,512]{3,2,1,0:T(4,128)} %get-tuple-element.30) | copy-start | bytes 147460
  393.9 10.2 %slice-start = ((s8[4718592]{0:T(1024)(128)(4,1)}), s8[4194304]{0:T(1024)(128)(4,1)S(1)}, s32[]{:S(2)}) async-start(s8[4718592]{0:T(1024)(128)(4,1)} %bitcast.68), calls=%async_computation | async-start | bytes 8388608
  396.3 5.2 %copy-start.1 = (bf16[3,2,7,2,16,1024]{5,4,3,2,1,0:T(8,128)(2,1)S(1)}, bf16[3,2,7,2,16,1024]{5,4,3,2,1,0:T(8,128)(2,1)}, u32[]{:S(2)}) copy-start(bf16[3,2,7,2,16,1024]{5,4,3,2,1,0:T(8,128)(2,1)} %get-tuple-element.26) | copy-start | bytes 8257540
  396.3 7.7 %slice-start.1 = ((s8[4718592]{0:T(1024)(128)(4,1)}), s8[524288]{0:T(1024)(128)(4,1)S(1)}, s32[]{:S(2)}) async-start(s8[4718592]{0:T(1024)(128)(4,1)} %bitcast.68), calls=%async_computation.1 | async-start | bytes 1048576

commit v5 on v4

--- a/solution.py
+++ b/solution.py
@@ -502,6 +502,18 @@
                         shard_rest,
                     ] = other[rows, lanes]
 
+    def run(count, body, make):
+        base, unit = clock[0], made[0]
+        clock[0] += count
+        made[0] += count
+        produced.append((base, count, unit))
+
+        @pl.loop(0, count)
+        def _(i):
+            body(i)
+            make(i, unit + i)
+            advance(i, base, count)
+
     def produce(count, units, make):
         base, unit = clock[0], made[0]
         produced.append((base, count * units, unit))
@@ -607,13 +619,19 @@
         def _(i):
             acc[steps(i)] = jnp.zeros((STEP, WIDE), jnp.float32)
 
-    def conv_taps(start, last, window_of, product):
+    def conv_taps(start, last, window_of, product, make=None):
+        def tap(t):
+            for g in groups:
+                acc[group_rows(g)] += product(window_of(g, t // 3, lax.rem(t, 3)), wp[t])
+
+        if make is not None:
+            run(last - start, lambda i: tap(start + i), make)
+            return
         tick = ticks(last - start) if produced else None
 
         @pl.loop(start, last)
         def _(t):
-            for g in groups:
-                acc[group_rows(g)] += product(window_of(g, t // 3, lax.rem(t, 3)), wp[t])
+            tap(t)
             if tick is not None:
                 tick(t - start)
 
@@ -782,30 +800,33 @@
         root, scale = stat_mid[index, 1:2], stat_mid[index, 2:3]
         offset, back = stat_mid[index, 3:4], stat_mid[index, 4:5]
         zero = jnp.zeros((ROWS, WIDE), jnp.float32)
-        total_grad, total_dot = zero, zero
+        total_grad, total_dot = zero8, zero8
         for g in groups:
             share = 1.0 / (widths[g] * widths[g])
 
+            up = jnp.concatenate([up32(up_ref[g, n]) * share] * (STEP // ROWS), axis=0)
+
             def body(i, carry):
-                rows = rows_at(starts[g] + i, 1)
+                rows = pl.ds(pl.multiple_of(starts[g] * ROWS + i * STEP, ROWS), STEP)
                 value = up32(h6[n, rows])
                 mask = wide_mask(mask_ref[rows])
                 z = value * scale + offset + up32(mb[n, rows])
                 s = sigmoid(z)
-                grad = up32(up_ref[g, n]) * (s * (1.0 + z * (1.0 - s))) * (mask * share)
+                grad = up * (s * (1.0 + z * (1.0 - s))) * mask
                 dz[n, rows] = low(grad)
+                last = (z * s * mask).reshape(STEP // ROWS, ROWS, WIDE)
                 return (
-                    carry[0] + z * s * mask,
-                    carry[1] + grad,
-                    carry[2] + grad * (value * root + back),
+                    carry[0] + jnp.sum(last, axis=0),
+                    carry[1] + fold(grad),
+                    carry[2] + fold(grad * (value * root + back)),
                 )
 
             pool, total_grad, total_dot = lax.fori_loop(
-                0, counts[g], body, (zero, total_grad, total_dot)
+                0, counts[g] * ROWS // STEP, body, (zero, total_grad, total_dot)
             )
             pool_slots[h, n, g * ROWS : (g + 1) * ROWS] = low(pool)
-        stat_out[pl.ds(n, 1)] = one_row(fold(total_grad))
-        stat_out[pl.ds(4 + n, 1)] = one_row(fold(total_dot))
+        stat_out[pl.ds(n, 1)] = one_row(total_grad)
+        stat_out[pl.ds(4 + n, 1)] = one_row(total_dot)
 
     state = wide_start(1)
 
@@ -894,12 +915,26 @@
         halo_up[halo_rows(g)] = low(first_row(h5, g))
     send_down(halo_down, dhp, 1)
     send_up(halo_up, 2)
+    def spatial_tile(window_of, grads):
+        def value_of(t):
+            parts = [
+                t_times(window_of(g, t // 3, lax.rem(t, 3)), grads[group_rows(g)]) for g in groups
+            ]
+            return parts[0] + parts[1] + parts[2]
+
+        return value_of
+
+    def spatial_maker(window_of, grads):
+        tile = spatial_tile(window_of, grads)
+        return lambda done: lambda i, unit: put(tile(done + i), unit, 1, 0)
+
+    make_b = spatial_maker(window_b, h5)
     clear_acc()
-    conv_taps(3, 6, window_b_back, times_t)
+    conv_taps(3, 6, window_b_back, times_t, make_b(0))
     halo_wait(halo_down, halo_recv, 1, h > 0)
     halo_wait(halo_in, halo_recv, 2, h < n_height - 1)
     place_below(dhp)
-    conv_taps(0, 3, window_b_back, times_t)
+    conv_taps(0, 3, window_b_back, times_t, make_b(3))
     conv_taps(6, 9, window_b_back, times_t)
     fetch(spatial_a, wp, w_sem.at[0])
     sums = mid_gradient(h4, 2)
@@ -908,17 +943,7 @@
     halo_wait(halo_up, halo_send, 2, h > 0)
     sums_middle(state)
 
-    def spatial_tile(window_of, grads):
-        def value_of(t):
-            parts = [
-                t_times(window_of(g, t // 3, lax.rem(t, 3)), grads[group_rows(g)]) for g in groups
-            ]
-            return parts[0] + parts[1] + parts[2]
-
-        return value_of
-
-    tile_b = spatial_tile(window_b, h5)
-    produce(9, 1, lambda t, unit: put(tile_b(t), unit, 1, 0))
+    produce(3, 1, make_b(6))
     sums = sums_end(state)
 
     mid_step(h4, mid_back(2, 2, sums, total_out), None)
@@ -963,16 +988,13 @@
     sums_end(state)
 
     arrived(wq.at[0:4], w_sem.at[1])
-    tick_11 = ticks(8)
-
-    @pl.loop(0, 4)
-    def _(n):
+
+    def expansion_back(n):
         main, slope, constant = out_back(0, 0, 4, n)
         main2, slope2, constant2 = out_back(1, 0, 8, n)
 
         @pl.loop(0, 2)
         def _(i):
-            tick_11(2 * n + i)
             rows = pl.ds(pl.multiple_of(i * half, ROWS), half)
             grad_in = up32(dz[n, rows])
             mask = wide_mask(mask_ref[rows])
@@ -982,12 +1004,12 @@
             other = main2 * grad_in + slope2 * up32(side[n, rows]) + constant2
             side[n, rows] = low(other * mask)
 
+    run(4, expansion_back, lambda n, unit: put(t_times(a2[...], h3[n]), unit, 1, 0))
     fetch(h1_kept, h1, spill_sem.at[0])
     fetch_shortcut()
     sums = mid_gradient(h2, 1)
     state = sums_start(sums)
     sums_middle(state)
-    produce(4, 1, lambda t, unit: put(t_times(a2[...], h3[t]), unit, 1, 0))
     for p in range(4):
         plane_arrived(mb.at[p], x_sem.at[0])
     plane_arrived(a4p, x_sem.at[1])
@@ -996,7 +1018,7 @@
         put(t_times(mb[0], side[t]), unit, 2, 0)
         put(t_times(a4p[0:total], side[t]), unit, 2, n_batch // 2)
 
-    produce(4, 2, tile_shortcut)
+    produce(1, 2, lambda step, unit: tile_shortcut(0, unit))
     sums = sums_end(state)
 
     mid_step(h2, mid_back(1, 1, sums, total_out), dhp)
@@ -1033,29 +1055,31 @@
             return carry[0] + fold(grad), carry[1] + fold(grad * (value * root + back))
 
         carry = lax.fori_loop(0, total // STEP, body, carry)
-        idle(2)
+        if p > 0:
+            produce(1, 2, lambda step, unit: tile_shortcut(p, unit))
     state = sums_start([one_row(v) for v in carry])
     halo_wait(halo_up, halo_send, 2, h > 0)
     sums_middle(state)
     arrived(big_a, spill_sem.at[1])
-    tile_a = spatial_tile(window_a, h2)
-    produce(9, 1, lambda t, unit: put(tile_a(t), unit, 1, 0))
-    for p in range(4):
-        fetch_plane(p, 1, big_a.at[p], x_sem.at[1])
+    make_a = spatial_maker(window_a, h2)
+    produce(3, 1, make_a(0))
     sums = sums_end(state)
 
     main, slope, constant = mid_back(0, 0, sums, total_in)
 
-    @pl.loop(0, 4)
-    def _(p):
+    def first_back(p):
         @pl.loop(0, total // STEP)
         def _(i):
             rows = steps(i)
             grad = main * up32(h3[p, rows]) + slope * up32(h1[p, rows]) + constant
             h1[p, rows] = low(grad * wide_mask(mask_ref[rows]))
 
+        fetch_plane(p, 1, h3.at[p], x_sem.at[1])
+
+    run(4, first_back, make_a(3))
+    produce(2, 1, make_a(7))
     for p in range(4):
-        plane_arrived(big_a.at[p], x_sem.at[1])
+        plane_arrived(h3.at[p], x_sem.at[1])
 
     def last_tile(chunk):
         value = t_times(chunk(0), h1[0])
@@ -1065,7 +1089,7 @@
 
     def tile_reduce_a(step, unit):
         put(last_tile(lambda p: mb[p]), unit, 2, 0)
-        put(last_tile(lambda p: big_a[p, 0:total]), unit, 2, n_batch // 2)
+        put(last_tile(lambda p: h3[p]), unit, 2, n_batch // 2)
 
     produce(1, 2, tile_reduce_a)
     arrived(wq, w_sem.at[1])
@@ -1079,20 +1103,20 @@
             for n in range(4):
                 value = value + times_t(side[n, rows], wq[2 * n + k])
             if k == 0:
-                h3[0, rows] = low(value)
+                big_a[0, rows] = low(value)
             else:
                 a4p[rows] = low(value)
             tick_13(i)
 
-    put_plane(0, 0, h3.at[0])
+    put_plane(0, 0, big_a.at[0])
     put_plane(0, 1, a4p)
     tick_13p = ticks(3)
 
     @pl.loop(1, 4)
     def _(p):
-        h3[p] = low(times_t(h1[p], w2[0]))
+        big_a[p, 0:total] = low(times_t(h1[p], w2[0]))
         side[p] = low(times_t(h1[p], w2[1]))
-        put_plane(p, 0, h3.at[p])
+        put_plane(p, 0, big_a.at[p])
         put_plane(p, 1, side.at[p])
         tick_13p(p - 1)
 

time: 415 us -> 387 us (0.933)
  Pallas kernels: 358 us -> 330 us
    pallas_call x1, Pallas kernels: 358 us -> 330 us  [per_device(): pl.pallas_call(functools.partial(main_kernel, n_batch, n_height, heights,...]
where the time goes in v5:
time: 387 us; the launch traced here: 381 us
  Pallas kernels  330 us (85%)
  local copies, waits for them, and re-layouts  44.9 us (12%)
  other arithmetic  4.08 us (1%)
    pallas_call x1, Pallas kernels, per_device(): pl.pallas_call(functools.partial(main_kernel, n_batch, n_height, heights,...  330 us
    transpose x6, local copies, waits for them, and re-layouts, to_planes(): value = jnp.transpose(value, (1, 2, 0, 3))  12.6 us
    unnamed x19, local copies, waits for them, and re-layouts  12.4 us

profile of v5, /device:TPU:0, one launch (start us, length us, event | category | flops | bytes accessed | tf_op | source)
XLA Modules:
  0.0 380.5 jit_solution(6368049904767427817)
XLA Ops:
  0.7 0.9 add_reduce_fusion
  5.0 1.4 reshape.293.gain_out
  6.4 1.4 reshape.294.shift_out
  8.5 0.8 pad.25
  9.4 0.9 pad.26
  10.3 1.0 pad.27
  12.1 0.9 broadcast_in_dim.5.mask_ref
  13.0 1.8 pad_bitcast_fusion.2
  14.8 1.8 copy.44
  17.2 3.1 copy.45
  20.9 4.8 %copy.46 = bf16[8,18,16,1024]{3,2,1,0:T(8,128)(2,1)} copy(bf16[8,18,16,1024]{3,0,1,2:T(8,128)(2,1)S(1)} %pad_bitcast_fusion) | data formatting | bytes 9437184 | tf_op jit(solution)/shard_map/transpose | solution.py:1144
  25.7 330.1 %both_blocks.1 = (f32[3,4,16,512]{3,2,1,0:T(8,128)}, bf16[2,2,5,2,16,1024]{5,4,3,2,1,0:T(8,128)(2,1)}, bf16[3,2,7,2,16,1024]{5,4,3,2,1,0:T(8,128)(2,1)}, bf16[4,...) custom-call(bf16[2,2,5,2,16,1024]{5,4,3,2,1,0:T(8,128)(2,1)} %bitcas, ...), custom_call_target="tpu_custom_call" | custom-call | tf_op jit(solution)/shard_map/both_blocks/pallas_call | solution.py:1196
  355.8 1.0 copy.66
  356.9 3.0 copy.79
  359.9 0.8 slice_bitcast_fusion.2
  362.1 1.7 slice.76
  363.7 1.3 slice.79
  365.0 1.1 copy.68
  366.1 2.5 slice_bitcast_fusion
  368.6 3.5 fusion.1
  372.0 0.8 copy.69
  372.9 0.8 copy.67
  373.7 2.5 copy.78
  376.3 3.7 copy.77
  (50 shorter events, 7.4 us)
Async XLA Ops:
  10.2 6.4 %copy-start.2 = (bf16[12,6,14,1024]{3,2,1,0:T(8,128)(2,1)S(1)}, bf16[12,6,14,1024]{3,2,1,0:T(8,128)(2,1)}, u32[]{:S(2)}) copy-start(bf16[12,6,14,1024]{3,2,1,0:T(8,128)(2,1)} %param.19) | copy-start | bytes 6193156
  17.2 3.2 copy-start
  355.8 4.8 %copy-start.4 = (f32[4,2,512]{2,1,0:T(2,128)S(1)}, f32[4,2,512]{2,1,0:T(2,128)}, u32[]{:S(2)}) copy-start(f32[4,2,512]{2,1,0:T(2,128)} %get-tuple-element.29) | copy-start | bytes 49156
  355.8 5.5 %copy-start.3 = (f32[3,2,4,512]{3,2,1,0:T(4,128)S(1)}, f32[3,2,4,512]{3,2,1,0:T(4,128)}, u32[]{:S(2)}) copy-start(f32[3,2,4,512]{3,2,1,0:T(4,128)} %get-tuple-element.30) | copy-start | bytes 147460
  366.1 10.2 %slice-start = ((s8[4718592]{0:T(1024)(128)(4,1)}), s8[4194304]{0:T(1024)(128)(4,1)S(1)}, s32[]{:S(2)}) async-start(s8[4718592]{0:T(1024)(128)(4,1)} %bitcast.68), calls=%async_computation | async-start | bytes 8388608
  368.5 5.2 %copy-start.1 = (bf16[3,2,7,2,16,1024]{5,4,3,2,1,0:T(8,128)(2,1)S(1)}, bf16[3,2,7,2,16,1024]{5,4,3,2,1,0:T(8,128)(2,1)}, u32[]{:S(2)}) copy-start(bf16[3,2,7,2,16,1024]{5,4,3,2,1,0:T(8,128)(2,1)} %get-tuple-element.26) | copy-start | bytes 8257540
  368.5 7.7 %slice-start.1 = ((s8[4718592]{0:T(1024)(128)(4,1)}), s8[524288]{0:T(1024)(128)(4,1)S(1)}, s32[]{:S(2)}) async-start(s8[4718592]{0:T(1024)(128)(4,1)} %bitcast.68), calls=%async_computation.1 | async-start | bytes 1048576

commit v6 on v5

--- a/solution.py
+++ b/solution.py
@@ -73,7 +73,7 @@
     pooled, dx_small, dx_medium, dx_large, g_units, mid_sums, out_sums, h1_kept, a1_kept,
     big_b, big_a, h3, side, mb, h2, a2, h4, h5, a5, a4p, dhp, acc, wp, wq, w2,
     halo_up, halo_down, halo_in, keep, away, r0, r1, r2, r3, final, ready, pool_slots,
-    thin_h, thin_b, wide_h, wide_b, stat_mid, stat_out,
+    thin, wide_h, wide_b, stat_mid, stat_out,
     w_sem, x_sem, u_send, u_recv, ready_sem, dx_sem, spill_sem, ar_send, ar_recv, halo_send, halo_recv, pool_sem,
 ):
     b, h = lax.axis_index("batch"), lax.axis_index("height")
@@ -82,6 +82,7 @@
     )
     total = sum(counts) * ROWS
     half = total // 2
+    part = total // 4
     groups = range(3)
     h1, dz, h6 = big_b, big_b, big_a
     halo_a = mb.at[0:2, 0 : sum(widths) * ROWS]
@@ -90,7 +91,7 @@
         return pl.ds(pl.multiple_of(start * ROWS, ROWS), count * ROWS)
 
     def steps(index):
-        return pl.ds(pl.multiple_of(index * STEP, STEP), STEP)
+        return pl.ds(pl.multiple_of(index * part, ROWS), part)
 
     def fetch(source, target, sem):
         pltpu.make_async_copy(source, target, sem).start()
@@ -172,20 +173,21 @@
             )
 
     barrier = pltpu.get_barrier_semaphore()
-    for k in range(1, n_height):
+
+    @pl.loop(1, n_batch * n_height)
+    def _(k):
+        other = lax.rem(b * n_height + h + k, n_batch * n_height)
         pl.semaphore_signal(
-            barrier, inc=1, device_id=(b, lax.rem(h + k, n_height)), device_id_type=MESH
+            barrier,
+            inc=1,
+            device_id=(other // n_height, lax.rem(other, n_height)),
+            device_id_type=MESH,
         )
 
-    @pl.loop(1, n_batch)
-    def _(k):
-        pl.semaphore_signal(
-            barrier, inc=1, device_id=(lax.rem(b + k, n_batch), h), device_id_type=MESH
-        )
-
-    pl.semaphore_wait(barrier, n_height + n_batch - 2)
+    pl.semaphore_wait(barrier, n_batch * n_height - 1)
 
     turn = [0]
+    direct = thin.shape[1] == n_batch * n_height
 
     def ar_spread(slots, me, count, peer, sems):
         @pl.loop(1, count)
@@ -206,12 +208,24 @@
     def sums_start(vectors):
         slot = turn[0] % 2
         turn[0] += 1
-        first, second = thin_h.at[slot], thin_b.at[slot]
+        if not direct:
+            first, second = thin.at[slot, 0:n_height], thin.at[slot, n_height:]
+            put_rows(first, h, vectors)
+            ar_spread(first, h, n_height, lambda p: (b, p), (0, 0, slot))
+            return first, second, 2, slot
+        slots = thin.at[slot]
+        me = b * n_height + h
+        put_rows(slots, me, vectors)
+        ar_spread(
+            slots, me, n_batch * n_height, lambda p: (p // n_height, lax.rem(p, n_height)),
+            (0, 0, slot),
+        )
+        return slots, None, 0, slot
+
+    def put_rows(slots, me, vectors):
         for v, vector in enumerate(vectors):
             for j in range(4):
-                first[h, 4 * v + j : 4 * v + j + 1, :] = vector[:, 128 * j : 128 * (j + 1)]
-        ar_spread(first, h, n_height, lambda p: (b, p), (0, 0, slot))
-        return first, second, 0, slot
+                slots[me, 4 * v + j : 4 * v + j + 1, :] = vector[:, 128 * j : 128 * (j + 1)]
 
     def wide_start(part):
         count = 16 if part is None else 8
@@ -223,23 +237,30 @@
 
     def sums_middle(state):
         first, second, kind, slot = state
-        ar_wait(first, n_height, (kind, 0, slot), ar_recv)
+        if kind == 0:
+            return
+        ar_wait(first, n_height, (kind % 2, 0, slot), ar_recv)
         second[b] = jnp.sum(first[...], axis=0)
-        ar_spread(second, b, n_batch, lambda p: (p, h), (kind, 1, slot))
+        ar_spread(second, b, n_batch, lambda p: (p, h), (kind % 2, 1, slot))
 
     def sums_end(state):
         first, second, kind, slot = state
-        ar_wait(second, n_batch, (kind, 1, slot), ar_recv)
-        summed = jnp.sum(second[...], axis=0)
-        ar_wait(first, n_height, (kind, 0, slot), ar_send)
-        ar_wait(second, n_batch, (kind, 1, slot), ar_send)
         if kind == 0:
-            return [
-                jnp.concatenate([summed[4 * v + j : 4 * v + j + 1] for j in range(4)], axis=1)
-                for v in range(2)
-            ]
-        stat_out[0 : summed.shape[0]] = summed
-        return None
+            ar_wait(first, n_batch * n_height, (0, 0, slot), ar_recv)
+            summed = jnp.sum(first[...], axis=0)
+            ar_wait(first, n_batch * n_height, (0, 0, slot), ar_send)
+        else:
+            ar_wait(second, n_batch, (kind % 2, 1, slot), ar_recv)
+            summed = jnp.sum(second[...], axis=0)
+            ar_wait(first, n_height, (kind % 2, 0, slot), ar_send)
+            ar_wait(second, n_batch, (kind % 2, 1, slot), ar_send)
+        if kind == 1:
+            stat_out[0 : summed.shape[0]] = summed
+            return None
+        return [
+            jnp.concatenate([summed[4 * v + j : 4 * v + j + 1] for j in range(4)], axis=1)
+            for v in range(2)
+        ]
 
     def keep_stats(kept, index, sums, number, gain, shift):
         centre = sums[0] * (1.0 / number)
@@ -426,12 +447,14 @@
     def round_5(unit):
         hop(4, unit).wait_recv()
         hop(5, unit).start()
+        for level in (1, 2):
+            hop(level, unit).wait_send()
+        rest_wait(unit, u_send)
 
     def round_6(unit):
         hop(5, unit).wait_recv()
-        for level in (1, 2, 4, 5):
+        for level in (4, 5):
             hop(level, unit).wait_send()
-        rest_wait(unit, u_send)
         slot = ring(ready, unit)
 
         @pl.when(unit >= ready.shape[0])
@@ -445,8 +468,8 @@
         fetch(ready.at[slot], g_units.at[unit], ready_sem.at[slot])
 
     rounds = (
-        (0, round_0), (2, round_1), (4, round_2), (5, round_3), (7, round_4), (8, round_5),
-        (10, round_6),
+        (0, round_0), (2, round_1), (4, round_2), (6, round_3), (8, round_4), (10, round_5),
+        (12, round_6),
     )
     clock, made, produced = [0], [0], []
 
@@ -615,9 +638,9 @@
         return big_a[2 * py + px, rows_at(first, counts[g])]
 
     def clear_acc():
-        @pl.loop(0, total // STEP)
+        @pl.loop(0, total // part)
         def _(i):
-            acc[steps(i)] = jnp.zeros((STEP, WIDE), jnp.float32)
+            acc[steps(i)] = jnp.zeros((part, WIDE), jnp.float32)
 
     def conv_taps(start, last, window_of, product, make=None):
         def tap(t):
@@ -642,7 +665,7 @@
             target[rows] = low(value)
             return carry[0] + fold(value), carry[1] + fold(value * value)
 
-        return lax.fori_loop(0, total // STEP, body, (zero8, zero8))
+        return lax.fori_loop(0, total // part, body, (zero8, zero8))
 
     clear_acc()
     arrived(wp, w_sem.at[0])
@@ -661,7 +684,7 @@
     def activate(source, target, index):
         scale, offset = stat_mid[index, 2:3], stat_mid[index, 3:4]
 
-        @pl.loop(0, total // STEP)
+        @pl.loop(0, total // part)
         def _(i):
             rows = steps(i)
             pre = up32(source[rows]) * scale + offset
@@ -729,7 +752,7 @@
             target[rows] = low(value)
             return carry[0] + fold(value), carry[1] + fold(value * value)
 
-        return lax.fori_loop(0, total // STEP, body, (zero8, zero8))
+        return lax.fori_loop(0, total // part, body, (zero8, zero8))
 
     sums = plain_sums(h4)
     state = sums_start([one_row(v) for v in sums])
@@ -869,7 +892,7 @@
             acc[rows] = grad
             return carry[0] + fold(grad), carry[1] + fold(grad * (value * root + back))
 
-        sums = lax.fori_loop(0, total // STEP, body, (zero8, zero8))
+        sums = lax.fori_loop(0, total // part, body, (zero8, zero8))
         return [one_row(v) for v in sums]
 
     @pl.loop(0, 4)
@@ -1054,7 +1077,7 @@
             h3[p, rows] = low(grad)
             return carry[0] + fold(grad), carry[1] + fold(grad * (value * root + back))
 
-        carry = lax.fori_loop(0, total // STEP, body, carry)
+        carry = lax.fori_loop(0, total // part, body, carry)
         if p > 0:
             produce(1, 2, lambda step, unit: tile_shortcut(p, unit))
     state = sums_start([one_row(v) for v in carry])
@@ -1068,7 +1091,7 @@
     main, slope, constant = mid_back(0, 0, sums, total_in)
 
     def first_back(p):
-        @pl.loop(0, total // STEP)
+        @pl.loop(0, total // part)
         def _(i):
             rows = steps(i)
             grad = main * up32(h3[p, rows]) + slope * up32(h1[p, rows]) + constant
@@ -1182,6 +1205,7 @@
     halo = sum(widths) * ROWS
     bf, f32 = jnp.bfloat16, jnp.float32
     unit_rows, n_rest = WIDE // n_batch, n_batch // 2
+    n_thin = n_batch * n_height if n_batch * n_height <= 64 else n_batch + n_height
     n_units = sum(
         w.size for w in (reduce_a, first_spatial_weight, expand_a, shortcut_a, reduce_b,
                          second_spatial_weight, expand_b)
@@ -1231,8 +1255,7 @@
             pltpu.VMEM((8, 2, 2, unit_rows, 128), bf),
             pltpu.VMEM((3, unit_rows, WIDE), f32),
             pltpu.VMEM((n_height, 4, 3 * ROWS, WIDE), bf),
-            pltpu.VMEM((2, n_height, 8, 128), f32),
-            pltpu.VMEM((2, n_batch, 8, 128), f32),
+            pltpu.VMEM((2, n_thin, 8, 128), f32),
             pltpu.VMEM((n_height, 16, WIDE), f32),
             pltpu.VMEM((n_batch, 16, WIDE), f32),
             pltpu.VMEM((16, 8, WIDE), f32),

time: 387 us -> 343 us (0.89)
  Pallas kernels: 330 us -> 286 us
    pallas_call x1, Pallas kernels: 330 us -> 286 us  [per_device(): pl.pallas_call(functools.partial(main_kernel, n_batch, n_height, heights,...]
where the time goes in v6:
time: 343 us; the launch traced here: 336 us
  Pallas kernels  286 us (83%)
  local copies, waits for them, and re-layouts  44.9 us (13%)
  other arithmetic  4.08 us (1%)
    pallas_call x1, Pallas kernels, per_device(): pl.pallas_call(functools.partial(main_kernel, n_batch, n_height, heights,...  286 us
    transpose x6, local copies, waits for them, and re-layouts, to_planes(): value = jnp.transpose(value, (1, 2, 0, 3))  12.6 us
    unnamed x19, local copies, waits for them, and re-layouts  12.4 us

profile of v6, /device:TPU:0, one launch (start us, length us, event | category | flops | bytes accessed | tf_op | source)
XLA Modules:
  0.0 336.3 jit_solution(995567804643041184)
XLA Ops:
  0.7 0.9 add_reduce_fusion
  5.0 1.4 reshape.293.gain_out
  6.4 1.4 reshape.294.shift_out
  8.5 0.8 pad.25
  9.4 0.9 pad.26
  10.3 1.0 pad.27
  12.1 0.9 broadcast_in_dim.5.mask_ref
  13.0 1.8 pad_bitcast_fusion.2
  14.8 1.8 copy.44
  17.2 3.1 copy.45
  20.9 4.8 %copy.46 = bf16[8,18,16,1024]{3,2,1,0:T(8,128)(2,1)} copy(bf16[8,18,16,1024]{3,0,1,2:T(8,128)(2,1)S(1)} %pad_bitcast_fusion) | data formatting | bytes 9437184 | tf_op jit(solution)/shard_map/transpose | solution.py:1167
  25.7 286.3 %both_blocks.1 = (f32[3,4,16,512]{3,2,1,0:T(8,128)}, bf16[2,2,5,2,16,1024]{5,4,3,2,1,0:T(8,128)(2,1)}, bf16[3,2,7,2,16,1024]{5,4,3,2,1,0:T(8,128)(2,1)}, bf16[4,...) custom-call(bf16[2,2,5,2,16,1024]{5,4,3,2,1,0:T(8,128)(2,1)} %bitcas, ...), custom_call_target="tpu_custom_call" | custom-call | tf_op jit(solution)/shard_map/both_blocks/pallas_call | solution.py:1220
  311.9 1.0 copy.66
  313.0 3.0 copy.79
  316.0 0.8 slice_bitcast_fusion.2
  318.2 1.7 slice.76
  319.8 1.3 slice.79
  321.1 1.1 copy.68
  322.2 2.5 slice_bitcast_fusion
  324.7 3.5 %fusion.1 = (f32[9,64,512]{2,1,0:T(8,128)}, f32[9,64,512]{2,1,0:T(8,128)}) fusion(f32[40,64,512]{2,1,0:T(8,128)} %get-tuple-element.28), kind=kLoop, calls=%fused_computation.33 | loop fusion | bytes 4718592 | tf_op jit(solution)/shard_map/slice | solution.py:1291
  328.1 0.8 copy.69
  329.0 0.8 copy.67
  329.8 2.5 copy.78
  332.4 3.7 %copy.77 = bf16[8,18,12,1024]{3,0,1,2:T(8,128)(2,1)} copy(bf16[8,18,12,1024]{3,2,1,0:T(8,128)(2,1)S(1)} %bitcast.70) | data formatting | bytes 7077888
  (50 shorter events, 7.4 us)
Async XLA Ops:
  10.2 6.4 %copy-start.2 = (bf16[12,6,14,1024]{3,2,1,0:T(8,128)(2,1)S(1)}, bf16[12,6,14,1024]{3,2,1,0:T(8,128)(2,1)}, u32[]{:S(2)}) copy-start(bf16[12,6,14,1024]{3,2,1,0:T(8,128)(2,1)} %param.19) | copy-start | bytes 6193156
  17.2 3.2 copy-start
  311.9 4.8 %copy-start.4 = (f32[4,2,512]{2,1,0:T(2,128)S(1)}, f32[4,2,512]{2,1,0:T(2,128)}, u32[]{:S(2)}) copy-start(f32[4,2,512]{2,1,0:T(2,128)} %get-tuple-element.29) | copy-start | bytes 49156
  311.9 5.5 %copy-start.3 = (f32[3,2,4,512]{3,2,1,0:T(4,128)S(1)}, f32[3,2,4,512]{3,2,1,0:T(4,128)}, u32[]{:S(2)}) copy-start(f32[3,2,4,512]{3,2,1,0:T(4,128)} %get-tuple-element.30) | copy-start | bytes 147460
  322.2 10.2 %slice-start = ((s8[4718592]{0:T(1024)(128)(4,1)}), s8[4194304]{0:T(1024)(128)(4,1)S(1)}, s32[]{:S(2)}) async-start(s8[4718592]{0:T(1024)(128)(4,1)} %bitcast.68), calls=%async_computation | async-start | bytes 8388608
  324.7 5.2 %copy-start.1 = (bf16[3,2,7,2,16,1024]{5,4,3,2,1,0:T(8,128)(2,1)S(1)}, bf16[3,2,7,2,16,1024]{5,4,3,2,1,0:T(8,128)(2,1)}, u32[]{:S(2)}) copy-start(bf16[3,2,7,2,16,1024]{5,4,3,2,1,0:T(8,128)(2,1)} %get-tuple-element.26) | copy-start | bytes 8257540
  324.7 7.7 %slice-start.1 = ((s8[4718592]{0:T(1024)(128)(4,1)}), s8[524288]{0:T(1024)(128)(4,1)S(1)}, s32[]{:S(2)}) async-start(s8[4718592]{0:T(1024)(128)(4,1)} %bitcast.68), calls=%async_computation.1 | async-start | bytes 1048576

commit v7 on v6

--- a/solution.py
+++ b/solution.py
@@ -15,8 +15,13 @@
 STEP = 64
 
 
-def sigmoid(values):
-    return 0.5 * jnp.tanh(0.5 * values) + 0.5
+def silu_of(half):
+    return half + half * jnp.tanh(half)
+
+
+def slope_of(half):
+    t = jnp.tanh(half)
+    return (1.0 + t) + half * (1.0 - t * t)
 
 
 def up32(values):
@@ -67,11 +72,13 @@
 
 
 def main_kernel(
-    n_batch, n_height, heights, widths, total_in, total_out,
+    n_batch, n_height, heights, widths, images, total_in, total_out,
     x_small, x_medium, x_large, reduce_a, spatial_a, expand_a, shortcut_a, reduce_b, spatial_b, expand_b,
-    edge_ref, mask_ref, gain_mid, shift_mid, gain_out, shift_out, up_ref,
-    pooled, dx_small, dx_medium, dx_large, g_units, mid_sums, out_sums, h1_kept, a1_kept,
-    big_b, big_a, h3, side, mb, h2, a2, h4, h5, a5, a4p, dhp, acc, wp, wq, w2,
+    row_counts, gain_mid, shift_mid, gain_out, shift_out, up_ref,
+    pooled, dx_small, dx_medium, dx_large, g_reduce_a, g_spatial_a, g_expand_a,
+    g_shortcut_a, g_reduce_b, g_spatial_b, g_expand_b, gain_mid_grad, shift_mid_grad,
+    gain_out_grad, shift_out_grad, h1_kept, a1_kept,
+    edge_ref, mask_ref, big_b, big_a, h3, side, mb, h2, a2, h4, h5, a5, a4p, dhp, acc, wp, wq, w2,
     halo_up, halo_down, halo_in, keep, away, r0, r1, r2, r3, final, ready, pool_slots,
     thin, wide_h, wide_b, stat_mid, stat_out,
     w_sem, x_sem, u_send, u_recv, ready_sem, dx_sem, spill_sem, ar_send, ar_recv, halo_send, halo_recv, pool_sem,
@@ -154,6 +161,19 @@
         fetch(reduce_a.at[columns(k)], w2.at[k], w_sem.at[3])
     fetch_shortcut()
     fetch(spatial_a, wp, w_sem.at[0])
+
+    for g in groups:
+        live = row_counts[g, h]
+        for y in range(heights[g]):
+            row = (starts[g] + y * (widths[g] + 1)) * ROWS
+            shape = (widths[g] * ROWS, 128)
+            image = lax.rem(lax.broadcasted_iota(jnp.int32, shape, 0), ROWS)
+            inside = jnp.where(image < images, 1.0, 0.0)
+            alive = jnp.clip(live - y, 0, 1).astype(jnp.float32)
+            mask_ref[row : row + shape[0]] = low(inside * alive)
+            mask_ref[row + shape[0] : row + shape[0] + ROWS] = jnp.zeros((ROWS, 128), jnp.bfloat16)
+            is_last = jnp.maximum(1 - jnp.abs(live - 1 - y), 0).astype(jnp.float32)
+            edge_ref[g, y] = jnp.ones((8, 128), jnp.float32) * is_last
 
     halo_down[...] = jnp.zeros_like(halo_down)
     halo_up[...] = jnp.zeros_like(halo_up)
@@ -271,6 +291,8 @@
         kept[index, 2:3] = scale
         kept[index, 3:4] = shift - centre * scale
         kept[index, 4:5] = -centre * root
+        kept[index, 5:6] = 0.5 * scale
+        kept[index, 6:7] = 0.5 * (shift - centre * scale)
 
     def back_factors(kept, index, sums, number, gain):
         centre, root = kept[index, 0:1], kept[index, 1:2]
@@ -392,10 +414,10 @@
         others = r3.at[ring(r3, unit)]
         pltpu.make_async_copy(others, others, sems.at[3, lax.rem(unit, 16)]).wait()
 
-    def round_0(unit):
+    def round_0(unit, view):
         hop(0, unit).start()
 
-    def round_1(unit):
+    def round_1(unit, view):
         hop(0, unit).wait()
         kept, got = keep.at[ring(keep, unit)], r0.at[ring(r0, unit)]
 
@@ -407,7 +429,7 @@
 
         hop(1, unit).start()
 
-    def round_2(unit):
+    def round_2(unit, view):
         hop(1, unit).wait_recv()
         kept, got = keep.at[ring(keep, unit), first], r1.at[ring(r1, unit)]
 
@@ -418,7 +440,7 @@
 
         hop(2, unit).start()
 
-    def round_3(unit):
+    def round_3(unit, view):
         hop(2, unit).wait_recv()
         kept, got = keep.at[ring(keep, unit), first, second], r2.at[ring(r2, unit)]
 
@@ -436,7 +458,7 @@
                 (lax.rem(rest + k, n_rest) * 2 + low_bit, h),
             ).start()
 
-    def round_4(unit):
+    def round_4(unit, view):
         rest_wait(unit, u_recv)
         value = up32(keep[ring(keep, unit), first, second, rest])
         for k in range(n_rest - 1):
@@ -444,14 +466,14 @@
         final[ring(final, unit), core, high] = low(value)
         hop(4, unit).start()
 
-    def round_5(unit):
+    def round_5(unit, view):
         hop(4, unit).wait_recv()
         hop(5, unit).start()
         for level in (1, 2):
             hop(level, unit).wait_send()
         rest_wait(unit, u_send)
 
-    def round_6(unit):
+    def round_6(unit, view):
         hop(5, unit).wait_recv()
         for level in (4, 5):
             hop(level, unit).wait_send()
@@ -465,7 +487,7 @@
             for i in range(2):
                 lane = 128 * (2 * c + i)
                 ready[slot, :, lane : lane + 128] = up32(final[ring(final, unit), c, i])
-        fetch(ready.at[slot], g_units.at[unit], ready_sem.at[slot])
+        fetch(ready.at[slot], view(unit), ready_sem.at[slot])
 
     rounds = (
         (0, round_0), (2, round_1), (4, round_2), (6, round_3), (8, round_4), (10, round_5),
@@ -475,17 +497,17 @@
 
     def advance(index, base, count):
         for lag, act in rounds:
-            for start, size, unit in produced:
+            for start, size, unit, view in produced:
                 from_, to = max(base - lag, start), min(base - lag + count, start + size)
                 if from_ >= to:
                     continue
                 target = base - lag - start + unit + index
                 if to - from_ == count:
-                    act(target)
+                    act(target, view)
                 else:
                     shift = base - lag
                     inside = jnp.logical_and(index >= from_ - shift, index < to - shift)
-                    pl.when(inside)(functools.partial(act, target))
+                    pl.when(inside)(functools.partial(act, target, view))
 
     def idle(count):
         base = clock[0]
@@ -525,11 +547,32 @@
                         shard_rest,
                     ] = other[rows, lanes]
 
-    def run(count, body, make):
-        base, unit = clock[0], made[0]
+    views = {
+        "expand_b": lambda j: g_expand_b.at[:, lanes_at(j)],
+        "spatial_b": lambda j: g_spatial_b.at[j],
+        "reduce_b": lambda j: g_reduce_b.at[unit_rows_at(j)],
+        "expand_a": lambda j: g_expand_a.at[:, lanes_at(j)],
+        "shortcut_a": lambda j: g_shortcut_a.at[unit_rows_at(lax.rem(j, 2)), lanes_at(j // 2)],
+        "spatial_a": lambda j: g_spatial_a.at[j],
+        "reduce_a": lambda j: g_reduce_a.at[unit_rows_at(j)],
+    }
+    first_units = {}
+
+    def lanes_at(j):
+        return pl.ds(pl.multiple_of(j * WIDE, WIDE), WIDE)
+
+    def unit_rows_at(j):
+        return pl.ds(pl.multiple_of(j * unit_rows, unit_rows), unit_rows)
+
+    def view_of(name):
+        base = first_units.setdefault(name, made[0])
+        return lambda unit: views[name](unit - base)
+
+    def run(name, count, body, make):
+        base, unit, view = clock[0], made[0], view_of(name)
         clock[0] += count
         made[0] += count
-        produced.append((base, count, unit))
+        produced.append((base, count, unit, view))
 
         @pl.loop(0, count)
         def _(i):
@@ -537,9 +580,9 @@
             make(i, unit + i)
             advance(i, base, count)
 
-    def produce(count, units, make):
-        base, unit = clock[0], made[0]
-        produced.append((base, count * units, unit))
+    def produce(name, count, units, make):
+        base, unit, view = clock[0], made[0], view_of(name)
+        produced.append((base, count * units, unit, view))
         clock[0] += count * units
         made[0] += count * units
 
@@ -555,6 +598,10 @@
                     advance(t * units + q, base, count * units)
 
     zero8 = jnp.zeros((8, WIDE), jnp.float32)
+
+    def half_mask(rows):
+        return wide_mask(0.5 * up32(mask_ref[rows]))
+
 
     arrived(w2, w_sem.at[3])
     for k in range(2):
@@ -591,12 +638,12 @@
     sums = sums_end(state)
     keep_stats(stat_mid, 0, sums, total_in, gain_mid[0:1], shift_mid[0:1])
 
-    scale, offset = stat_mid[0, 2:3], stat_mid[0, 3:4]
+    scale, offset = stat_mid[0, 5:6], stat_mid[0, 6:7]
     for column in range(2):
         for g in groups:
             pre = last_row(h1.at[2 + column], g) * scale + offset
             mask = wide_mask(mask_ref[starts[g] * ROWS : (starts[g] + widths[g]) * ROWS])
-            halo_a[column, halo_rows(g)] = low(pre * sigmoid(pre) * mask)
+            halo_a[column, halo_rows(g)] = low(silu_of(pre) * mask)
 
     @pl.when(h < n_height - 1)
     def _():
@@ -619,7 +666,7 @@
             def _(i):
                 rows = pl.ds(pl.multiple_of(starts[g] * ROWS + i * STEP, ROWS), STEP)
                 pre = up32(h1[p, rows]) * scale + offset
-                value = pre * sigmoid(pre) * wide_mask(mask_ref[rows])
+                value = silu_of(pre) * wide_mask(mask_ref[rows])
                 big_a[p, pl.ds(pl.multiple_of(base + i * STEP, ROWS), STEP)] = low(value)
 
     fetch(h1, h1_kept, spill_sem.at[0])
@@ -648,7 +695,7 @@
                 acc[group_rows(g)] += product(window_of(g, t // 3, lax.rem(t, 3)), wp[t])
 
         if make is not None:
-            run(last - start, lambda i: tap(start + i), make)
+            run("spatial_b", last - start, lambda i: tap(start + i), make)
             return
         tick = ticks(last - start) if produced else None
 
@@ -682,13 +729,13 @@
     keep_stats(stat_mid, 1, sums, total_out, gain_mid[1:2], shift_mid[1:2])
 
     def activate(source, target, index):
-        scale, offset = stat_mid[index, 2:3], stat_mid[index, 3:4]
+        scale, offset = stat_mid[index, 5:6], stat_mid[index, 6:7]
 
         @pl.loop(0, total // part)
         def _(i):
             rows = steps(i)
             pre = up32(source[rows]) * scale + offset
-            target[rows] = low(pre * sigmoid(pre) * wide_mask(mask_ref[rows]))
+            target[rows] = low(silu_of(pre) * wide_mask(mask_ref[rows]))
 
     activate(h2, a2, 1)
     arrived(wq.at[0:4], w_sem.at[1])
@@ -713,8 +760,8 @@
             4 * index + n,
             [stat_out[row + n : row + n + 1], stat_out[row + 4 + n : row + 5 + n]],
             total_out,
-            gain_out[index, n : n + 1],
-            shift_out[index, n : n + 1],
+            gain_out[index : index + 1, n * WIDE : (n + 1) * WIDE],
+            shift_out[index : index + 1, n * WIDE : (n + 1) * WIDE],
         )
 
     mid_or_out = stat_mid.at[4:16]
@@ -725,11 +772,11 @@
     def out_stat(index, n, row):
         return stat_mid[4 + 4 * index + n, row : row + 1]
 
-    def joint(n, rows):
+    def half_joint(n, rows):
         return (
-            up32(h3[n, rows]) * out_stat(0, n, 2)
-            + up32(side[n, rows]) * out_stat(1, n, 2)
-            + (out_stat(0, n, 3) + out_stat(1, n, 3))
+            up32(h3[n, rows]) * out_stat(0, n, 5)
+            + up32(side[n, rows]) * out_stat(1, n, 5)
+            + (out_stat(0, n, 6) + out_stat(1, n, 6))
         )
 
     arrived(wq.at[4:8], w_sem.at[2])
@@ -740,8 +787,7 @@
         @pl.loop(0, 2)
         def _(i):
             rows = pl.ds(pl.multiple_of(i * half, ROWS), half)
-            value = joint(n, rows)
-            value = low(value * sigmoid(value) * wide_mask(mask_ref[rows]))
+            value = low(silu_of(half_joint(n, rows)) * wide_mask(mask_ref[rows]))
             mb[n, rows] = value
             acc[rows] += times(value, wq[4 + n])
 
@@ -761,16 +807,16 @@
     sums = sums_end(state)
     keep_stats(stat_mid, 2, sums, total_out, gain_mid[2:3], shift_mid[2:3])
 
-    scale, offset = stat_mid[2, 2:3], stat_mid[2, 3:4]
+    scale, offset = stat_mid[2, 5:6], stat_mid[2, 6:7]
     for g in groups:
         pre = last_row(h4, g) * scale + offset
         mask = wide_mask(mask_ref[starts[g] * ROWS : (starts[g] + widths[g]) * ROWS])
-        halo_down[halo_rows(g)] = low(pre * sigmoid(pre) * mask)
+        halo_down[halo_rows(g)] = low(silu_of(pre) * mask)
     send_down(halo_down, a4p, 1)
     for g in groups:
         pre = first_row(h4, g) * scale + offset
         mask = wide_mask(mask_ref[starts[g] * ROWS : (starts[g] + widths[g]) * ROWS])
-        halo_up[halo_rows(g)] = low(pre * sigmoid(pre) * mask)
+        halo_up[halo_rows(g)] = low(silu_of(pre) * mask)
     send_up(halo_up, 2)
 
     def both_base(g):
@@ -782,7 +828,7 @@
         def _(i):
             rows = pl.ds(pl.multiple_of(starts[g] * ROWS + i * STEP, ROWS), STEP)
             pre = up32(h4[rows]) * scale + offset
-            value = low(pre * sigmoid(pre) * wide_mask(mask_ref[rows]))
+            value = low(silu_of(pre) * wide_mask(mask_ref[rows]))
             a4p[pl.ds(pl.multiple_of(both_base(g) + i * STEP, ROWS), STEP)] = value
 
     def window_b(g, a, c):
@@ -827,17 +873,19 @@
         for g in groups:
             share = 1.0 / (widths[g] * widths[g])
 
-            up = jnp.concatenate([up32(up_ref[g, n]) * share] * (STEP // ROWS), axis=0)
+            up = jnp.concatenate([up32(up_ref[g, n]) * (0.5 * share)] * (STEP // ROWS), axis=0)
 
             def body(i, carry):
                 rows = pl.ds(pl.multiple_of(starts[g] * ROWS + i * STEP, ROWS), STEP)
                 value = up32(h6[n, rows])
                 mask = wide_mask(mask_ref[rows])
                 z = value * scale + offset + up32(mb[n, rows])
-                s = sigmoid(z)
-                grad = up * (s * (1.0 + z * (1.0 - s))) * mask
+                z = 0.5 * z
+                t = jnp.tanh(z)
+                last = z + z * t
+                grad = up * ((1.0 + t) + (z - z * t * t)) * mask
                 dz[n, rows] = low(grad)
-                last = (z * s * mask).reshape(STEP // ROWS, ROWS, WIDE)
+                last = (last * mask).reshape(STEP // ROWS, ROWS, WIDE)
                 return (
                     carry[0] + jnp.sum(last, axis=0),
                     carry[1] + fold(grad),
@@ -868,27 +916,26 @@
 
     def out_back(index, sum_row, dot_row, n):
         sums = [stat_out[pl.ds(sum_row + n, 1)], stat_out[pl.ds(dot_row + n, 1)]]
-        out_sums[index, 0, pl.ds(n, 1)] = sums[0]
-        out_sums[index, 1, pl.ds(n, 1)] = sums[1]
+        shift_out_grad[index : index + 1, lanes_at(n)] = sums[0]
+        gain_out_grad[index : index + 1, lanes_at(n)] = sums[1]
         return back_factors(
-            stat_mid, 4 + 4 * index + n, sums, total_out, gain_out[index, pl.ds(n, 1)]
+            stat_mid, 4 + 4 * index + n, sums, total_out, gain_out[index : index + 1, lanes_at(n)]
         )
 
     def mid_back(index, place, sums, number):
-        mid_sums[place, 0:1] = sums[0]
-        mid_sums[place, 1:2] = sums[1]
+        shift_mid_grad[place : place + 1] = sums[0]
+        gain_mid_grad[place : place + 1] = sums[1]
         return back_factors(stat_mid, index, sums, number, gain_mid[place : place + 1])
 
     def mid_gradient(source, index):
-        root, scale = stat_mid[index, 1:2], stat_mid[index, 2:3]
-        offset, back = stat_mid[index, 3:4], stat_mid[index, 4:5]
+        root, scale = stat_mid[index, 1:2], stat_mid[index, 5:6]
+        offset, back = stat_mid[index, 6:7], stat_mid[index, 4:5]
 
         def body(i, carry):
             rows = steps(i)
             value = up32(source[rows])
-            pre = value * scale + offset
-            s = sigmoid(pre)
-            grad = acc[rows] * (s * (1.0 + pre * (1.0 - s))) * wide_mask(mask_ref[rows])
+            slope = slope_of(value * scale + offset)
+            grad = acc[rows] * slope * half_mask(rows)
             acc[rows] = grad
             return carry[0] + fold(grad), carry[1] + fold(grad * (value * root + back))
 
@@ -911,7 +958,7 @@
     state = sums_start(sums)
     fetch_columns(expand_a, wq, 0, w_sem.at[1])
     sums_middle(state)
-    produce(4, 1, lambda t, unit: put(t_times(a5[...], h6[t, 0:total]), unit, 1, 0))
+    produce("expand_b", 4, 1, lambda t, unit: put(t_times(a5[...], h6[t, 0:total]), unit, 1, 0))
     fetch(a1_kept, big_a, spill_sem.at[1])
     sums = sums_end(state)
 
@@ -966,7 +1013,7 @@
     halo_wait(halo_up, halo_send, 2, h > 0)
     sums_middle(state)
 
-    produce(3, 1, make_b(6))
+    produce("spatial_b", 3, 1, make_b(6))
     sums = sums_end(state)
 
     mid_step(h4, mid_back(2, 2, sums, total_out), None)
@@ -980,9 +1027,7 @@
             tick(2 * n + i)
             rows = pl.ds(pl.multiple_of(i * half, ROWS), half)
             grad = times_t(h4[rows], wq[4 + n]) + up32(dz[n, rows])
-            z = joint(n, rows)
-            s = sigmoid(z)
-            grad = grad * (s * (1.0 + z * (1.0 - s))) * wide_mask(mask_ref[rows])
+            grad = grad * slope_of(half_joint(n, rows)) * half_mask(rows)
             dz[n, rows] = low(grad)
             main_hat = up32(h3[n, rows]) * out_stat(0, n, 1) + out_stat(0, n, 4)
             side_hat = up32(side[n, rows]) * out_stat(1, n, 1) + out_stat(1, n, 4)
@@ -1004,7 +1049,7 @@
         def _(t):
             put(t_times(mb[t], h4[...]), unit, 4, t * (n_batch // 4))
 
-    produce(1, 4, tile_reduce_b)
+    produce("reduce_b", 1, 4, tile_reduce_b)
     for p in range(4):
         fetch_plane(p, 0, mb.at[p], x_sem.at[0])
     clear_acc()
@@ -1027,7 +1072,7 @@
             other = main2 * grad_in + slope2 * up32(side[n, rows]) + constant2
             side[n, rows] = low(other * mask)
 
-    run(4, expansion_back, lambda n, unit: put(t_times(a2[...], h3[n]), unit, 1, 0))
+    run("expand_a", 4, expansion_back, lambda n, unit: put(t_times(a2[...], h3[n]), unit, 1, 0))
     fetch(h1_kept, h1, spill_sem.at[0])
     fetch_shortcut()
     sums = mid_gradient(h2, 1)
@@ -1041,7 +1086,7 @@
         put(t_times(mb[0], side[t]), unit, 2, 0)
         put(t_times(a4p[0:total], side[t]), unit, 2, n_batch // 2)
 
-    produce(1, 2, lambda step, unit: tile_shortcut(0, unit))
+    produce("shortcut_a", 1, 2, lambda step, unit: tile_shortcut(0, unit))
     sums = sums_end(state)
 
     mid_step(h2, mid_back(1, 1, sums, total_out), dhp)
@@ -1050,8 +1095,8 @@
     send_up(halo_up, 2)
     arrived(wp, w_sem.at[0])
     arrived(h1, spill_sem.at[0])
-    root, scale = stat_mid[0, 1:2], stat_mid[0, 2:3]
-    offset, back = stat_mid[0, 3:4], stat_mid[0, 4:5]
+    root, scale = stat_mid[0, 1:2], stat_mid[0, 5:6]
+    offset, back = stat_mid[0, 6:7], stat_mid[0, 4:5]
     carry = (zero8, zero8)
     for p in range(4):
         py, px = p // 2, p % 2
@@ -1071,21 +1116,19 @@
         def body(i, carry):
             rows = steps(i)
             value = up32(h1[p, rows])
-            pre = value * scale + offset
-            s = sigmoid(pre)
-            grad = acc[rows] * (s * (1.0 + pre * (1.0 - s))) * wide_mask(mask_ref[rows])
+            grad = acc[rows] * slope_of(value * scale + offset) * half_mask(rows)
             h3[p, rows] = low(grad)
             return carry[0] + fold(grad), carry[1] + fold(grad * (value * root + back))
 
         carry = lax.fori_loop(0, total // part, body, carry)
         if p > 0:
-            produce(1, 2, lambda step, unit: tile_shortcut(p, unit))
+            produce("shortcut_a", 1, 2, lambda step, unit: tile_shortcut(p, unit))
     state = sums_start([one_row(v) for v in carry])
     halo_wait(halo_up, halo_send, 2, h > 0)
     sums_middle(state)
     arrived(big_a, spill_sem.at[1])
     make_a = spatial_maker(window_a, h2)
-    produce(3, 1, make_a(0))
+    produce("spatial_a", 3, 1, make_a(0))
     sums = sums_end(state)
 
     main, slope, constant = mid_back(0, 0, sums, total_in)
@@ -1099,8 +1142,8 @@
 
         fetch_plane(p, 1, h3.at[p], x_sem.at[1])
 
-    run(4, first_back, make_a(3))
-    produce(2, 1, make_a(7))
+    run("spatial_a", 4, first_back, make_a(3))
+    produce("spatial_a", 2, 1, make_a(7))
     for p in range(4):
         plane_arrived(h3.at[p], x_sem.at[1])
 
@@ -1114,7 +1157,7 @@
         put(last_tile(lambda p: mb[p]), unit, 2, 0)
         put(last_tile(lambda p: h3[p]), unit, 2, n_batch // 2)
 
-    produce(1, 2, tile_reduce_a)
+    produce("reduce_a", 1, 2, tile_reduce_a)
     arrived(wq, w_sem.at[1])
     for k in range(2):
         tick_13 = ticks(2)
@@ -1185,31 +1228,16 @@
     heights = [value.shape[1] // 2 for value in images]
     widths = [value.shape[2] // 2 for value in images]
     count = images[0].shape[0]
-    live = row_counts[:, lax.axis_index("height")]
     pixels = sum(o * o for o in widths) * count * n_batch
     counts, starts, top_total, _, both_total, _, _ = grids(heights, widths)
     total = sum(counts) * ROWS
     planes = [to_planes(image) for image in images]
-    masks = []
-    for g in range(3):
-        row_ok = (jnp.arange(heights[g], dtype=jnp.int32) < live[g])[:, None, None]
-        column_ok = (jnp.arange(widths[g] + 1) < widths[g])[None, :, None]
-        image_ok = (jnp.arange(ROWS) < count)[None, None, :]
-        masks.append(jnp.logical_and(jnp.logical_and(row_ok, column_ok), image_ok).reshape(-1))
-    mask = jnp.concatenate(masks).astype(jnp.bfloat16)
-    mask = jnp.broadcast_to(mask[:, None], (total, 128))
-    edges = (jnp.arange(max(heights))[None, :] == live[:, None] - 1).astype(jnp.float32)
-    edges = jnp.broadcast_to(edges[:, :, None, None], edges.shape + (8, 128))
-    up = jnp.stack([jnp.pad(value, ((0, ROWS - count), (0, 0))) for value in upstreams])
+    up = jnp.pad(jnp.stack(upstreams), ((0, 0), (0, ROWS - count), (0, 0)))
     up = jnp.transpose(up.reshape(3, ROWS, 4, WIDE), (0, 2, 1, 3))
     halo = sum(widths) * ROWS
     bf, f32 = jnp.bfloat16, jnp.float32
     unit_rows, n_rest = WIDE // n_batch, n_batch // 2
     n_thin = n_batch * n_height if n_batch * n_height <= 64 else n_batch + n_height
-    n_units = sum(
-        w.size for w in (reduce_a, first_spatial_weight, expand_a, shortcut_a, reduce_b,
-                         second_spatial_weight, expand_b)
-    ) // (WIDE * WIDE)
     dma = pltpu.SemaphoreType.DMA
     vmem = pl.BlockSpec(memory_space=pltpu.VMEM)
     anywhere = pl.BlockSpec(memory_space=pl.ANY)
@@ -1219,20 +1247,25 @@
     thin = pltpu.VMEM((total, WIDE), bf)
     results = pl.pallas_call(
         functools.partial(
-            main_kernel, n_batch, n_height, heights, widths, float(4 * pixels), float(pixels)
+            main_kernel, n_batch, n_height, heights, widths, count, float(4 * pixels),
+            float(pixels)
         ),
         out_shape=[
             jax.ShapeDtypeStruct((3, 4, ROWS, WIDE), f32),
             *[jax.ShapeDtypeStruct(value.shape, bf) for value in planes],
-            jax.ShapeDtypeStruct((n_units, unit_rows, WIDE), f32),
-            jax.ShapeDtypeStruct((4, 2, WIDE), f32),
-            jax.ShapeDtypeStruct((3, 2, 4, WIDE), f32),
+            *[
+                jax.ShapeDtypeStruct(w.shape[:-2] + (w.shape[-2] // n_batch, w.shape[-1]), f32)
+                for w in (reduce_a, flat_a, expand_a, shortcut_a, reduce_b, flat_b, expand_b)
+            ],
+            *[jax.ShapeDtypeStruct(w.shape, f32) for w in (gain_mid, shift_mid, gain_out, shift_out)],
             jax.ShapeDtypeStruct((4, total, WIDE), bf),
             jax.ShapeDtypeStruct((4, top_total * ROWS, WIDE), bf),
         ],
-        in_specs=[anywhere] * 10 + [vmem] * 7,
-        out_specs=[vmem] + [anywhere] * 4 + [vmem] * 2 + [anywhere] * 2,
+        in_specs=[anywhere] * 10 + [pl.BlockSpec(memory_space=pltpu.SMEM)] + [vmem] * 5,
+        out_specs=[vmem] + [anywhere] * 10 + [vmem] * 4 + [anywhere] * 2,
         scratch_shapes=[
+            pltpu.VMEM((3, max(heights), 8, 128), f32),
+            pltpu.VMEM((total, 128), bf),
             big,
             pltpu.VMEM((4, top_total * ROWS, WIDE), bf),
             big, big, big,
@@ -1269,41 +1302,14 @@
         name="both_blocks",
     )(
         *planes, reduce_a, flat_a, expand_a, shortcut_a, reduce_b, flat_b, expand_b,
-        edges, mask, gain_mid, shift_mid,
-        gain_out.reshape(3, 4, WIDE), shift_out.reshape(3, 4, WIDE), up,
+        row_counts, gain_mid, shift_mid, gain_out, shift_out, up,
     )
     pooled = jnp.transpose(results[0], (0, 2, 1, 3)).reshape(3, ROWS, -1)[:, :count]
     backs = [from_planes(results[1 + g], images[g].shape) for g in range(3)]
-    units, place, shards = results[4], 0, {}
-    for name, shape in (
-        ("expand_b", expand_b.shape),
-        ("spatial_b", second_spatial_weight.shape),
-        ("reduce_b", reduce_b.shape),
-        ("expand_a", expand_a.shape),
-        ("shortcut_a", shortcut_a.shape),
-        ("spatial_a", first_spatial_weight.shape),
-        ("reduce_a", reduce_a.shape),
-    ):
-        lead = shape[:-2]
-        count_units = shape[-2] * shape[-1] // (WIDE * WIDE)
-        for size in lead:
-            count_units *= size
-        value = units[place : place + count_units]
-        place += count_units
-        rows = shape[-2] // n_batch
-        if lead:
-            shards[name] = value.reshape(lead + (rows, WIDE))
-        else:
-            value = value.reshape(shape[1] // WIDE, rows, WIDE)
-            shards[name] = jnp.transpose(value, (1, 0, 2)).reshape(rows, shape[1])
-    order = (
-        "reduce_a", "spatial_a", "expand_a", "shortcut_a", "reduce_b", "spatial_b", "expand_b"
-    )
-    mid, out = results[5], results[6].reshape(3, 2, -1)
-    return (
-        pooled[0], pooled[1], pooled[2], backs[0], backs[1], backs[2], *[shards[name] for name in order],
-        mid[:, 1], mid[:, 0], out[:, 1], out[:, 0],
-    )
+    shards = list(results[4:11])
+    for place in (1, 5):
+        shards[place] = shards[place].reshape((3, 3) + shards[place].shape[1:])
+    return (pooled[0], pooled[1], pooled[2], *backs, *shards, *results[11:15])
 
 
 def solution(mesh):

time: 343 us -> 325 us (0.948)
  local copies, waits for them, and re-layouts: 44.9 us -> 33.6 us
    slice x6 -> x0, local copies, waits for them, and re-layouts: 7.01 us -> none  [the longest x3 6.44 us: per_device(): value = units[place:place + count_units]]
    unnamed x19 -> x44, local copies, waits for them, and re-layouts: 12.4 us -> 18.3 us
    reshape x6 -> x1, local copies, waits for them, and re-layouts: 5.58 us -> 0.7 us  [per_device(): up = jnp.transpose(up.reshape(3, ROWS, 4, WIDE), (0, 2, 1, 3))]
where the time goes in v7:
time: 325 us; the launch traced here: 319 us
  Pallas kernels  284 us (87%)
  local copies, waits for them, and re-layouts  33.6 us (10%)
    pallas_call x1, Pallas kernels, per_device(): pl.pallas_call(functools.partial(main_kernel, n_batch, n_height, heights,...  284 us
    unnamed x44, local copies, waits for them, and re-layouts  18.3 us
    transpose x6, local copies, waits for them, and re-layouts, to_planes(): value = jnp.transpose(value, (1, 2, 0, 3))  12.7 us

profile of v7, /device:TPU:0, one launch (start us, length us, event | category | flops | bytes accessed | tf_op | source)
XLA Modules:
  0.0 319.2 jit_solution(6093285930281773964)
XLA Ops:
  0.7 0.9 fusion.4
  1.6 0.7 copy.61
  2.3 1.9 pad_bitcast_fusion.2
  4.2 1.8 copy.41
  6.0 0.6 pad_bitcast_fusion.1
  6.6 3.1 copy.42
  10.2 4.8 %copy.43 = bf16[8,18,16,1024]{3,2,1,0:T(8,128)(2,1)} copy(bf16[8,18,16,1024]{3,0,1,2:T(8,128)(2,1)S(1)} %pad_bitcast_fusion) | data formatting | bytes 9437184 | tf_op jit(solution)/shard_map/transpose | solution.py:1210
  15.0 283.8 %both_blocks.1 = (f32[3,4,16,512]{3,2,1,0:T(8,128)}, bf16[2,2,5,2,16,1024]{5,4,3,2,1,0:T(8,128)(2,1)}, bf16[3,2,7,2,16,1024]{5,4,3,2,1,0:T(8,128)(2,1)}, bf16[4,...) custom-call(bf16[2,2,5,2,16,1024]{5,4,3,2,1,0:T(8,128)(2,1)} %bitcas, ...), custom_call_target="tpu_custom_call" | custom-call | tf_op jit(solution)/shard_map/both_blocks/pallas_call | solution.py:1248
  298.8 1.2 copy.53
  300.0 3.0 copy.60
  303.0 0.8 slice_bitcast_fusion
  303.7 2.5 copy.59
  306.7 3.7 %copy.58 = bf16[8,18,12,1024]{3,0,1,2:T(8,128)(2,1)} copy(bf16[8,18,12,1024]{3,2,1,0:T(8,128)(2,1)S(1)} %bitcast.52) | data formatting | bytes 7077888
  310.5 0.7 copy.73
  311.2 1.0 copy.74
  312.2 0.8 copy.75
  313.0 1.0 copy.76
  314.0 0.8 copy.77
  314.8 1.0 copy.78
  315.8 0.8 copy.79
  316.6 0.6 copy.80
  317.2 0.6 copy.81
  317.8 0.6 copy.82
  318.4 0.6 copy.83
  (31 shorter events, 1.0 us)
Async XLA Ops:
  1.6 4.4 %copy-start.3 = (bf16[12,6,14,1024]{3,2,1,0:T(8,128)(2,1)S(1)}, bf16[12,6,14,1024]{3,2,1,0:T(8,128)(2,1)}, u32[]{:S(2)}) copy-start(bf16[12,6,14,1024]{3,2,1,0:T(8,128)(2,1)} %param.19) | copy-start | bytes 6193156
  6.6 3.2 copy-start.1
  298.8 5.0 %copy-start.2 = (bf16[3,2,7,2,16,1024]{5,4,3,2,1,0:T(8,128)(2,1)S(1)}, bf16[3,2,7,2,16,1024]{5,4,3,2,1,0:T(8,128)(2,1)}, u32[]{:S(2)}) copy-start(bf16[3,2,7,2,16,1024]{5,4,3,2,1,0:T(8,128)(2,1)} %get-tuple-element.34) | copy-start | bytes 8257540
  303.7 3.0 copy-start
  306.7 3.8 %copy-start.10 = (f32[128,512]{1,0:T(8,128)S(1)}, f32[128,512]{1,0:T(8,128)}, u32[]{:S(2)}) copy-start(f32[128,512]{1,0:T(8,128)} %get-tuple-element.73) | copy-start | bytes 786436
  306.7 4.5 %copy-start.5 = (f32[9,64,512]{2,1,0:T(8,128)S(1)}, f32[9,64,512]{2,1,0:T(8,128)}, u32[]{:S(2)}) copy-start(f32[9,64,512]{2,1,0:T(8,128)} %get-tuple-element.37) | copy-start | bytes 3538948
  310.5 1.7 copy-start.9
  310.5 2.5 copy-start.6
  311.2 2.8 copy-start.8
  311.2 3.6 %copy-start.4 = (f32[9,64,512]{2,1,0:T(8,128)S(1)}, f32[9,64,512]{2,1,0:T(8,128)}, u32[]{:S(2)}) copy-start(f32[9,64,512]{2,1,0:T(8,128)} %get-tuple-element.41) | copy-start | bytes 3538948
  313.0 2.8 copy-start.7
  314.0 2.6 copy-start.14
  314.0 3.2 %copy-start.13 = (f32[4,512]{1,0:T(4,128)S(1)}, f32[4,512]{1,0:T(4,128)}, u32[]{:S(2)}) copy-start(f32[4,512]{1,0:T(4,128)} %get-tuple-element.81) | copy-start | bytes 24580
  314.0 3.8 %copy-start.12 = (f32[3,2048]{1,0:T(4,128)S(1)}, f32[3,2048]{1,0:T(4,128)}, u32[]{:S(2)}) copy-start(f32[3,2048]{1,0:T(4,128)} %get-tuple-element.82) | copy-start | bytes 73732
  314.0 4.4 %copy-start.11 = (f32[3,2048]{1,0:T(4,128)S(1)}, f32[3,2048]{1,0:T(4,128)}, u32[]{:S(2)}) copy-start(f32[3,2048]{1,0:T(4,128)} %get-tuple-element.83) | copy-start | bytes 73732

commit v8 on v7

--- a/solution.py
+++ b/solution.py
@@ -247,16 +247,16 @@
             for j in range(4):
                 slots[me, 4 * v + j : 4 * v + j + 1, :] = vector[:, 128 * j : 128 * (j + 1)]
 
-    def wide_start(part):
+    def wide_start(part, at=0):
         count = 16 if part is None else 8
         rows = pl.ds(8 * (part or 0), count)
         first, second = wide_h.at[:, rows], wide_b.at[:, rows]
-        first[h] = stat_out[0:count]
+        first[h] = stat_out[at : at + count]
         ar_spread(first, h, n_height, lambda p: (b, p), (1, 0, part or 0))
-        return first, second, 1, part or 0
+        return first, second, 1, part or 0, at
 
     def sums_middle(state):
-        first, second, kind, slot = state
+        first, second, kind, slot = state[:4]
         if kind == 0:
             return
         ar_wait(first, n_height, (kind % 2, 0, slot), ar_recv)
@@ -264,7 +264,7 @@
         ar_spread(second, b, n_batch, lambda p: (p, h), (kind % 2, 1, slot))
 
     def sums_end(state):
-        first, second, kind, slot = state
+        first, second, kind, slot = state[:4]
         if kind == 0:
             ar_wait(first, n_batch * n_height, (0, 0, slot), ar_recv)
             summed = jnp.sum(first[...], axis=0)
@@ -275,7 +275,7 @@
             ar_wait(first, n_height, (kind % 2, 0, slot), ar_send)
             ar_wait(second, n_batch, (kind % 2, 1, slot), ar_send)
         if kind == 1:
-            stat_out[0 : summed.shape[0]] = summed
+            stat_out[state[4] : state[4] + summed.shape[0]] = summed
             return None
         return [
             jnp.concatenate([summed[4 * v + j : 4 * v + j + 1] for j in range(4)], axis=1)
@@ -632,6 +632,7 @@
     lax.fori_loop(0, 2, shortcut_product, 0)
     sums_middle(state)
     lax.fori_loop(2, 4, shortcut_product, 0)
+    side_state = wide_start(1, 8)
     fetch_columns(expand_a, wq, 0, w_sem.at[1])
     for k in range(4):
         fetch(reduce_b.at[columns(k)], wq.at[4 + k], w_sem.at[2])
@@ -717,6 +718,7 @@
     clear_acc()
     arrived(wp, w_sem.at[0])
     conv_taps(3, 9, window_a, times)
+    sums_middle(side_state)
     halo_wait(halo_a, halo_recv, 0, h > 0)
     conv_taps(0, 3, window_a, times)
     sums = masked_sums(h2)
@@ -749,7 +751,7 @@
             stat_out[pl.ds(4 + n, 1)] = one_row(fold(value * value))
 
     expansion(a2, h3)
-    state = wide_start(None)
+    state = wide_start(0)
     fetch_columns(expand_b, wq, 0, w_sem.at[1])
     sums_middle(state)
     sums_end(state)
@@ -764,6 +766,7 @@
             shift_out[index : index + 1, n * WIDE : (n + 1) * WIDE],
         )
 
+    sums_end(side_state)
     mid_or_out = stat_mid.at[4:16]
     for n in range(4):
         out_stats(0, n, 0)

time: 325 us -> 323 us (level)
  no operation moved by 1% of the time
where the time goes in v8:
time: 323 us; the launch traced here: 317 us
  Pallas kernels  282 us (87%)
  local copies, waits for them, and re-layouts  33.6 us (10%)
    pallas_call x1, Pallas kernels, per_device(): pl.pallas_call(functools.partial(main_kernel, n_batch, n_height, heights,...  282 us
    unnamed x44, local copies, waits for them, and re-layouts  18.3 us
    transpose x6, local copies, waits for them, and re-layouts, to_planes(): value = jnp.transpose(value, (1, 2, 0, 3))  12.7 us

profile of v8, /device:TPU:0, one launch (start us, length us, event | category | flops | bytes accessed | tf_op | source)
XLA Modules:
  0.0 317.1 jit_solution(1855749516382501911)
XLA Ops:
  0.7 0.9 fusion.4
  1.6 0.7 copy.61
  2.3 1.9 pad_bitcast_fusion.2
  4.2 1.8 copy.41
  6.0 0.6 pad_bitcast_fusion.1
  6.6 3.1 copy.42
  10.2 4.8 %copy.43 = bf16[8,18,16,1024]{3,2,1,0:T(8,128)(2,1)} copy(bf16[8,18,16,1024]{3,0,1,2:T(8,128)(2,1)S(1)} %pad_bitcast_fusion) | data formatting | bytes 9437184 | tf_op jit(solution)/shard_map/transpose | solution.py:1213
  15.0 281.7 %both_blocks.1 = (f32[3,4,16,512]{3,2,1,0:T(8,128)}, bf16[2,2,5,2,16,1024]{5,4,3,2,1,0:T(8,128)(2,1)}, bf16[3,2,7,2,16,1024]{5,4,3,2,1,0:T(8,128)(2,1)}, bf16[4,...) custom-call(bf16[2,2,5,2,16,1024]{5,4,3,2,1,0:T(8,128)(2,1)} %bitcas, ...), custom_call_target="tpu_custom_call" | custom-call | tf_op jit(solution)/shard_map/both_blocks/pallas_call | solution.py:1251
  296.7 1.2 copy.53
  297.9 3.0 copy.60
  300.9 0.8 slice_bitcast_fusion
  301.6 2.5 copy.59
  304.6 3.7 %copy.58 = bf16[8,18,12,1024]{3,0,1,2:T(8,128)(2,1)} copy(bf16[8,18,12,1024]{3,2,1,0:T(8,128)(2,1)S(1)} %bitcast.52) | data formatting | bytes 7077888
  308.4 0.7 copy.73
  309.1 1.0 copy.74
  310.1 0.8 copy.75
  310.9 1.0 copy.76
  311.9 0.8 copy.77
  312.7 1.0 copy.78
  313.7 0.8 copy.79
  314.5 0.6 copy.80
  315.1 0.6 copy.81
  315.7 0.6 copy.82
  316.3 0.6 copy.83
  (31 shorter events, 1.0 us)
Async XLA Ops:
  1.6 4.4 %copy-start.3 = (bf16[12,6,14,1024]{3,2,1,0:T(8,128)(2,1)S(1)}, bf16[12,6,14,1024]{3,2,1,0:T(8,128)(2,1)}, u32[]{:S(2)}) copy-start(bf16[12,6,14,1024]{3,2,1,0:T(8,128)(2,1)} %param.19) | copy-start | bytes 6193156
  6.6 3.2 copy-start.1
  296.7 5.0 %copy-start.2 = (bf16[3,2,7,2,16,1024]{5,4,3,2,1,0:T(8,128)(2,1)S(1)}, bf16[3,2,7,2,16,1024]{5,4,3,2,1,0:T(8,128)(2,1)}, u32[]{:S(2)}) copy-start(bf16[3,2,7,2,16,1024]{5,4,3,2,1,0:T(8,128)(2,1)} %get-tuple-element.34) | copy-start | bytes 8257540
  301.6 3.0 copy-start
  304.6 3.8 %copy-start.10 = (f32[128,512]{1,0:T(8,128)S(1)}, f32[128,512]{1,0:T(8,128)}, u32[]{:S(2)}) copy-start(f32[128,512]{1,0:T(8,128)} %get-tuple-element.73) | copy-start | bytes 786436
  304.6 4.5 %copy-start.5 = (f32[9,64,512]{2,1,0:T(8,128)S(1)}, f32[9,64,512]{2,1,0:T(8,128)}, u32[]{:S(2)}) copy-start(f32[9,64,512]{2,1,0:T(8,128)} %get-tuple-element.37) | copy-start | bytes 3538948
  308.4 1.7 copy-start.9
  308.4 2.5 copy-start.6
  309.1 2.8 copy-start.8
  309.1 3.6 %copy-start.4 = (f32[9,64,512]{2,1,0:T(8,128)S(1)}, f32[9,64,512]{2,1,0:T(8,128)}, u32[]{:S(2)}) copy-start(f32[9,64,512]{2,1,0:T(8,128)} %get-tuple-element.41) | copy-start | bytes 3538948
  310.9 2.8 copy-start.7
  311.9 2.6 copy-start.14
  311.9 3.2 %copy-start.13 = (f32[4,512]{1,0:T(4,128)S(1)}, f32[4,512]{1,0:T(4,128)}, u32[]{:S(2)}) copy-start(f32[4,512]{1,0:T(4,128)} %get-tuple-element.81) | copy-start | bytes 24580
  311.9 3.8 %copy-start.12 = (f32[3,2048]{1,0:T(4,128)S(1)}, f32[3,2048]{1,0:T(4,128)}, u32[]{:S(2)}) copy-start(f32[3,2048]{1,0:T(4,128)} %get-tuple-element.82) | copy-start | bytes 73732
  311.9 4.4 %copy-start.11 = (f32[3,2048]{1,0:T(4,128)S(1)}, f32[3,2048]{1,0:T(4,128)}, u32[]{:S(2)}) copy-start(f32[3,2048]{1,0:T(4,128)} %get-tuple-element.83) | copy-start | bytes 73732

commit v9 on v8

--- a/solution.py
+++ b/solution.py
@@ -90,6 +90,7 @@
     total = sum(counts) * ROWS
     half = total // 2
     part = total // 4
+    step_of = [ROWS * max(d for d in range(1, 21) if n % d == 0) for n in counts]
     groups = range(3)
     h1, dz, h6 = big_b, big_b, big_a
     halo_a = mb.at[0:2, 0 : sum(widths) * ROWS]
@@ -658,17 +659,18 @@
                 ).start()
 
     for g in groups:
-        per = counts[g] * ROWS // STEP
+        step = step_of[g]
+        per = counts[g] * ROWS // step
         base = (top_starts[g] + 1 + widths[g] + 1) * ROWS
 
         @pl.loop(0, 4)
         def _(p):
             @pl.loop(0, per)
             def _(i):
-                rows = pl.ds(pl.multiple_of(starts[g] * ROWS + i * STEP, ROWS), STEP)
+                rows = pl.ds(pl.multiple_of(starts[g] * ROWS + i * step, ROWS), step)
                 pre = up32(h1[p, rows]) * scale + offset
                 value = silu_of(pre) * wide_mask(mask_ref[rows])
-                big_a[p, pl.ds(pl.multiple_of(base + i * STEP, ROWS), STEP)] = low(value)
+                big_a[p, pl.ds(pl.multiple_of(base + i * step, ROWS), step)] = low(value)
 
     fetch(h1, h1_kept, spill_sem.at[0])
 
@@ -681,7 +683,7 @@
 
     def window_a(g, a, c):
         py, dy = lax.rem(a + 1, 2), (a + 1) // 2 - 1
-        px, dx_ = lax.rem(c + 1, 2), (c + 1) // 2 - 1
+        px, dx_ = (c + 1) % 2, (c + 1) // 2 - 1
         first = top_starts[g] + 1 + (1 + dy) * (widths[g] + 1) + dx_
         return big_a[2 * py + px, rows_at(first, counts[g])]
 
@@ -698,13 +700,21 @@
         if make is not None:
             run("spatial_b", last - start, lambda i: tap(start + i), make)
             return
-        tick = ticks(last - start) if produced else None
+        if not produced:
+
+            @pl.loop(start // 3, last // 3)
+            def _(a):
+                for g in groups:
+                    parts = [product(window_of(g, a, c), wp[3 * a + c]) for c in range(3)]
+                    acc[group_rows(g)] += parts[0] + parts[1] + parts[2]
+
+            return
+        tick = ticks(last - start)
 
         @pl.loop(start, last)
         def _(t):
             tap(t)
-            if tick is not None:
-                tick(t - start)
+            tick(t - start)
 
     def masked_sums(target):
         def body(i, carry):
@@ -827,12 +837,14 @@
 
     for g in groups:
 
-        @pl.loop(0, counts[g] * ROWS // STEP)
+        step = step_of[g]
+
+        @pl.loop(0, counts[g] * ROWS // step)
         def _(i):
-            rows = pl.ds(pl.multiple_of(starts[g] * ROWS + i * STEP, ROWS), STEP)
+            rows = pl.ds(pl.multiple_of(starts[g] * ROWS + i * step, ROWS), step)
             pre = up32(h4[rows]) * scale + offset
             value = low(silu_of(pre) * wide_mask(mask_ref[rows]))
-            a4p[pl.ds(pl.multiple_of(both_base(g) + i * STEP, ROWS), STEP)] = value
+            a4p[pl.ds(pl.multiple_of(both_base(g) + i * step, ROWS), step)] = value
 
     def window_b(g, a, c):
         return window(a4p, both_starts[g], g, a - 1, c - 1)
@@ -974,13 +986,15 @@
 
         for g in groups:
 
-            @pl.loop(0, counts[g] * ROWS // STEP)
+            step = step_of[g]
+
+            @pl.loop(0, counts[g] * ROWS // step)
             def _(i):
-                rows = pl.ds(pl.multiple_of(starts[g] * ROWS + i * STEP, ROWS), STEP)
+                rows = pl.ds(pl.multiple_of(starts[g] * ROWS + i * step, ROWS), step)
                 grad = tile(rows)
                 target[rows] = grad
                 if padded is not None:
-                    padded[pl.ds(pl.multiple_of(both_base(g) + i * STEP, ROWS), STEP)] = grad
+                    padded[pl.ds(pl.multiple_of(both_base(g) + i * step, ROWS), step)] = grad
 
     mid_step(h5, mid_back(3, 3, sums, total_out), dhp)
     for g in groups:

time: 323 us -> 322 us (level)
  no operation moved by 1% of the time
where the time goes in v9:
time: 322 us; the launch traced here: 316 us
  Pallas kernels  280 us (87%)
  local copies, waits for them, and re-layouts  33.6 us (10%)
    pallas_call x1, Pallas kernels, per_device(): pl.pallas_call(functools.partial(main_kernel, n_batch, n_height, heights,...  280 us
    unnamed x44, local copies, waits for them, and re-layouts  18.3 us
    transpose x6, local copies, waits for them, and re-layouts, to_planes(): value = jnp.transpose(value, (1, 2, 0, 3))  12.7 us

profile of v9, /device:TPU:0, one launch (start us, length us, event | category | flops | bytes accessed | tf_op | source)
XLA Modules:
  0.0 315.9 jit_solution(6243050703840634917)
XLA Ops:
  0.7 0.9 fusion.4
  1.6 0.7 copy.61
  2.3 1.9 pad_bitcast_fusion.2
  4.2 1.8 copy.41
  6.0 0.6 pad_bitcast_fusion.1
  6.6 3.1 copy.42
  10.2 4.8 %copy.43 = bf16[8,18,16,1024]{3,2,1,0:T(8,128)(2,1)} copy(bf16[8,18,16,1024]{3,0,1,2:T(8,128)(2,1)S(1)} %pad_bitcast_fusion) | data formatting | bytes 9437184 | tf_op jit(solution)/shard_map/transpose | solution.py:1227
  15.0 280.2 %both_blocks.1 = (f32[3,4,16,512]{3,2,1,0:T(8,128)}, bf16[2,2,5,2,16,1024]{5,4,3,2,1,0:T(8,128)(2,1)}, bf16[3,2,7,2,16,1024]{5,4,3,2,1,0:T(8,128)(2,1)}, bf16[4,...) custom-call(bf16[2,2,5,2,16,1024]{5,4,3,2,1,0:T(8,128)(2,1)} %bitcas, ...), custom_call_target="tpu_custom_call" | custom-call | tf_op jit(solution)/shard_map/both_blocks/pallas_call | solution.py:1265
  295.2 1.2 copy.53
  296.4 3.0 copy.60
  299.4 0.8 slice_bitcast_fusion
  300.2 2.5 copy.59
  303.2 3.7 %copy.58 = bf16[8,18,12,1024]{3,0,1,2:T(8,128)(2,1)} copy(bf16[8,18,12,1024]{3,2,1,0:T(8,128)(2,1)S(1)} %bitcast.52) | data formatting | bytes 7077888
  306.9 0.7 copy.73
  307.6 1.0 copy.74
  308.6 0.8 copy.75
  309.4 1.0 copy.76
  310.4 0.8 copy.77
  311.2 1.0 copy.78
  312.2 0.8 copy.79
  313.0 0.6 copy.80
  313.6 0.6 copy.81
  314.2 0.6 copy.82
  314.9 0.6 copy.83
  (31 shorter events, 1.0 us)
Async XLA Ops:
  1.6 4.4 %copy-start.3 = (bf16[12,6,14,1024]{3,2,1,0:T(8,128)(2,1)S(1)}, bf16[12,6,14,1024]{3,2,1,0:T(8,128)(2,1)}, u32[]{:S(2)}) copy-start(bf16[12,6,14,1024]{3,2,1,0:T(8,128)(2,1)} %param.19) | copy-start | bytes 6193156
  6.6 3.2 %copy-start.1 = (bf16[12,8,18,1024]{3,1,2,0:T(8,128)(2,1)S(1)}, bf16[12,8,18,1024]{3,1,2,0:T(8,128)(2,1)}, u32[]{:S(2)}) copy-start(bf16[12,8,18,1024]{3,1,2,0:T(8,128)(2,1)} %param.20) | copy-start | bytes 10616836
  295.2 5.0 %copy-start.2 = (bf16[3,2,7,2,16,1024]{5,4,3,2,1,0:T(8,128)(2,1)S(1)}, bf16[3,2,7,2,16,1024]{5,4,3,2,1,0:T(8,128)(2,1)}, u32[]{:S(2)}) copy-start(bf16[3,2,7,2,16,1024]{5,4,3,2,1,0:T(8,128)(2,1)} %get-tuple-element.34) | copy-start | bytes 8257540
  300.2 3.0 copy-start
  303.1 3.8 %copy-start.10 = (f32[128,512]{1,0:T(8,128)S(1)}, f32[128,512]{1,0:T(8,128)}, u32[]{:S(2)}) copy-start(f32[128,512]{1,0:T(8,128)} %get-tuple-element.73) | copy-start | bytes 786436
  303.2 4.5 %copy-start.5 = (f32[9,64,512]{2,1,0:T(8,128)S(1)}, f32[9,64,512]{2,1,0:T(8,128)}, u32[]{:S(2)}) copy-start(f32[9,64,512]{2,1,0:T(8,128)} %get-tuple-element.37) | copy-start | bytes 3538948
  306.9 1.7 copy-start.9
  306.9 2.5 copy-start.6
  307.6 2.8 copy-start.8
  307.6 3.6 %copy-start.4 = (f32[9,64,512]{2,1,0:T(8,128)S(1)}, f32[9,64,512]{2,1,0:T(8,128)}, u32[]{:S(2)}) copy-start(f32[9,64,512]{2,1,0:T(8,128)} %get-tuple-element.41) | copy-start | bytes 3538948
  309.4 2.8 copy-start.7
  310.4 2.6 copy-start.14
  310.4 3.2 %copy-start.13 = (f32[4,512]{1,0:T(4,128)S(1)}, f32[4,512]{1,0:T(4,128)}, u32[]{:S(2)}) copy-start(f32[4,512]{1,0:T(4,128)} %get-tuple-element.81) | copy-start | bytes 24580
  310.4 3.8 %copy-start.12 = (f32[3,2048]{1,0:T(4,128)S(1)}, f32[3,2048]{1,0:T(4,128)}, u32[]{:S(2)}) copy-start(f32[3,2048]{1,0:T(4,128)} %get-tuple-element.82) | copy-start | bytes 73732
  310.4 4.4 %copy-start.11 = (f32[3,2048]{1,0:T(4,128)S(1)}, f32[3,2048]{1,0:T(4,128)}, u32[]{:S(2)}) copy-start(f32[3,2048]{1,0:T(4,128)} %get-tuple-element.83) | copy-start | bytes 73732
